TPU v7x, 256 devices: a whole 4x4x8 slice. The times are simulated.
256 devices in a mesh: space: 16 (over y, z_lo), mode: 16 (over x, z_hi, core).
Axes of the slice: x: 4, y: 4, z: 8 (z_hi: 2, z_lo: 4; z = z_hi * 4 + z_lo), core: 2. Of those that a mesh axis runs over, the one named last changes fastest.
Arguments:
- fields: bfloat16 [64, 8192, 512], P('mode', 'space'), may hold values from -6 to 6
- pre_act: bfloat16 [64, 8192, 512], P('mode', 'space'), may hold values from -6 to 6
- cotangent: bfloat16 [64, 8192, 512], P('mode', 'space'), may hold values from -3 to 3
- weights: bfloat16 [64, 2, 512, 512], P('mode'), may hold values from -0.1875 to 0.1875
Outputs:
- field_grad: bfloat16 [64, 8192, 512], P('mode', 'space')
- weight_grad: float32 [64, 2, 512, 512], P('mode', None, None, 'space')
All inputs are finite; a program needn't handle non-finite values.
Results may differ from a plain program's by a relative error of at most 0.0072.
Values may be sent and summed in bfloat16 or wider, within the bound.
No kernel may reach another device: no remote copies, remote signals or barrier semaphores. Data moves between devices by JAX's collectives and lax.ppermute only.
A program may use at most 64 MiB of HBM per device.

v0:
```python
import math

import jax
import jax.numpy as jnp
from jax import lax
from jax.sharding import PartitionSpec as P


def make_table(n_modes, points, offset, total):
    wave_nums = jnp.arange(n_modes, dtype=jnp.int32)
    position = jnp.arange(points, dtype=jnp.int32) + offset
    phases = wave_nums[:, None] * position[None, :] % total
    angles = phases.astype(jnp.float32) * (2.0 * math.pi / total)
    return jnp.stack([jnp.cos(angles), -jnp.sin(angles)], axis=1).astype(jnp.bfloat16)


def gelu_slope(values):
    normal_cdf = 0.5 * (1.0 + jax.scipy.special.erf(values / math.sqrt(2.0)))
    density = jnp.exp(-0.5 * values * values) / math.sqrt(2.0 * math.pi)
    return normal_cdf + values * density


def weight_terms(input_low, grad_low):
    u_real, u_imag = (input_low[:, 0], input_low[:, 1])
    g_real, g_imag = (grad_low[:, 0], grad_low[:, 1])
    left_one = jnp.concatenate([u_real, u_imag], axis=1)
    right_one = jnp.concatenate([g_real, g_imag], axis=1)
    left_two = jnp.concatenate([u_real, -u_imag], axis=1)
    right_two = jnp.concatenate([g_imag, g_real], axis=1)
    grad_real = jnp.einsum("mbc,mbd->mcd", left_one, right_one, preferred_element_type=jnp.float32)
    grad_imag = jnp.einsum("mbc,mbd->mcd", left_two, right_two, preferred_element_type=jnp.float32)
    return jnp.stack([grad_real, grad_imag], axis=1)


def mode_terms(grad_low, weight_part):
    g_real, g_imag = (grad_low[:, 0], grad_low[:, 1])
    w_real, w_imag = (weight_part[:, 0], weight_part[:, 1])
    mode_real = jnp.einsum(
        "mbd,mcd->mbc",
        jnp.concatenate([g_real, g_imag], axis=2),
        jnp.concatenate([w_real, w_imag], axis=2),
        preferred_element_type=jnp.float32,
    )
    mode_imag = jnp.einsum(
        "mbd,mcd->mbc",
        jnp.concatenate([-g_real, g_imag], axis=2),
        jnp.concatenate([w_imag, w_real], axis=2),
        preferred_element_type=jnp.float32,
    )
    return jnp.stack([mode_real, mode_imag], axis=1)


def shards(fields, pre_act, cotangent, weights):
    n_space = lax.axis_size("space")
    n_mode = lax.axis_size("mode")
    mode_dev = weights.shape[0]
    n_modes = mode_dev * n_mode
    points = fields.shape[1]
    total = points * n_space
    width = weights.shape[2]
    columns = width // n_space
    factor = float(total) ** (-0.5)
    offset = lax.axis_index("space") * points
    table = make_table(n_modes, points, offset, total)
    slopes = (cotangent.astype(jnp.float32) * gelu_slope(pre_act.astype(jnp.float32))).astype(
        jnp.bfloat16
    )
    part_u = jnp.einsum("kpx,bxc->kpbc", table, fields, preferred_element_type=jnp.float32)
    part_g = jnp.einsum("kpx,bxc->kpbc", table, slopes, preferred_element_type=jnp.float32)
    part_u, part_g = (
        lax.all_to_all(part_u, "mode", split_axis=0, concat_axis=2, tiled=True),
        lax.all_to_all(part_g, "mode", split_axis=0, concat_axis=2, tiled=True),
    )
    k_local = lax.axis_index("mode") * mode_dev + jnp.arange(mode_dev, dtype=jnp.int32)
    weight_k = jnp.where(k_local == 0, 1.0, 2.0).astype(jnp.float32) * factor
    col_start = lax.axis_index("space") * columns
    spec_u = lax.psum(part_u, "space") * factor
    spec_g = (
        lax.psum_scatter(part_g, "space", scatter_dimension=3, tiled=True)
        * weight_k[:, None, None, None]
    )
    input_low = spec_u.astype(jnp.bfloat16)
    grad_low = spec_g.astype(jnp.bfloat16)
    weight_grad = weight_terms(input_low, grad_low)
    weight_cols = lax.dynamic_slice_in_dim(weights, col_start, columns, 3)
    partial_terms = mode_terms(grad_low, weight_cols)
    mode_grad = lax.psum(partial_terms, "space").astype(jnp.bfloat16)
    returned = lax.all_to_all(mode_grad, "mode", split_axis=2, concat_axis=0, tiled=True)
    field_grad = jnp.einsum("kpbc,kpx->bxc", returned, table, preferred_element_type=jnp.float32)
    return ((field_grad * factor).astype(jnp.bfloat16), weight_grad)


def solution(mesh):
    in_specs = (
        P("mode", "space", None),
        P("mode", "space", None),
        P("mode", "space", None),
        P("mode", None, None, None),
    )
    out_specs = (P("mode", "space", None), P("mode", None, None, "space"))
    return jax.shard_map(shards, mesh=mesh, in_specs=in_specs, out_specs=out_specs, check_vma=False)
```

profile of v0, /device:TPU:1, one launch (start us, length us, event | category | flops | bytes accessed | tf_op | source)
XLA Modules:
  0.0 406.3 jit_solution(9781130711301878386)
XLA Ops:
  7.2 0.5 cosine_convert_fusion
  7.7 4.0 fusion.11
  11.8 1.6 copy.26
  13.4 12.4 %all-to-all-start = ((f32[64,2,4,512]{3,2,1,0:T(4,128)}), f32[64,2,4,512]{3,2,1,0:T(4,128)S(1)}, u32[]{:S(2)}, u32[]{:S(2)}) async-start(f32[64,2,4,512]{3,2,1,0:T(4,128)} %copy.26), calls=%async_computation | async-start | bytes 2097152 | tf_op jit(solution)/shard_map/all_to_all | solution.py:72
  25.8 0.4 fusion.9
  26.3 1.7 copy.33
  28.0 19.8 %all-to-all-done = f32[64,2,4,512]{3,2,1,0:T(4,128)S(1)} async-done(((f32[64,2,4,512]{3,2,1,0:T(4,128)}), f32[64,2,4,512]{3,2,1,0:T(4,128)S(1)}, u32[]{:S(2)}, u32[]{:S(2)}) %all-to-all-start) | async-done | bytes 1048608 | tf_op jit(solution)/shard_map/all_to_all | solution.py:72
  47.8 9.0 %all-to-all-start.2 = ((f32[64,2,4,512]{3,2,1,0:T(4,128)}), f32[64,2,4,512]{3,2,1,0:T(4,128)}, u32[]{:S(2)}, u32[]{:S(2)}) async-start(f32[64,2,4,512]{3,2,1,0:T(4,128)} %copy.33), calls=%async_computation.2 | async-start | bytes 2097152 | tf_op jit(solution)/shard_map/all_to_all | solution.py:71
  56.9 1.8 copy.27
  58.6 2.5 copy.28
  61.1 15.5 %all-to-all-done.2 = f32[64,2,4,512]{3,2,1,0:T(4,128)} async-done(((f32[64,2,4,512]{3,2,1,0:T(4,128)}), f32[64,2,4,512]{3,2,1,0:T(4,128)}, u32[]{:S(2)}, u32[]{:S(2)}) %all-to-all-start.2) | async-done | bytes 1048608 | tf_op jit(solution)/shard_map/all_to_all | solution.py:71
  76.7 1.3 copy.47
  78.0 1.4 all_to_all.50
  79.4 1.6 constant_dynamic-slice_fusion.2
  81.0 0.2 copy.43
  81.2 0.2 copy.44
  81.4 0.6 dynamic-slice
  82.7 182.8 %all-reduce.5.cloned.1.call-done = (f32[4,2,64,512]{2,0,1,3:T(4,128)}, f32[4,2,64,512]{3,2,0,1:T(8,128)}) async-done(((f32[4,2,64,512]{2,0,1,3:T(4,128)}, f32[4,2,64,512]{3,2,0,1:T(8,128)}), (f32[4,2,64,512]{2,0,1,3:T(4,128)}, f32[4,2,64,512]{3,2,0,1:T(8,128)})) %all-reduce.5.cloned.1.call-update) | async-done | bytes 2097168
  265.5 0.9 constant_dynamic-slice_fusion
  266.4 0.1 copy.29
  266.7 0.3 convolution_bitcast_fusion.1
  266.9 0.3 convolution_bitcast_fusion
  267.3 85.9 %all-reduce.6 = bf16[4,2,64,512]{3,2,0,1:T(8,128)(2,1)} all-reduce(f32[4,2,64,512]{3,2,0,1:T(8,128)S(1)} %pad_maximum_fusion), channel_id=1, replica_groups=mesh['space'=16,'mode'=16] {'space'}, use_global_device_ids=true, to_apply=%region_1.2 | all-reduce | flops 262144 | bytes 1572864 | tf_op jit(solution)/shard_map/psum | solution.py:87
  353.3 2.2 copy.31
  355.5 27.7 %all-to-all-start.1 = ((bf16[4,2,64,512]{3,0,1,2:T(4,128)(2,1)}), bf16[4,2,64,512]{3,0,1,2:T(4,128)(2,1)S(1)}, u32[]{:S(2)}, u32[]{:S(2)}) async-start(bf16[4,2,64,512]{3,0,1,2:T(4,128)(2,1)} %copy.31), calls=%async_computation.1 | async-start | bytes 1048576 | tf_op jit(solution)/shard_map/all_to_all | solution.py:88
  383.3 1.4 multiply_convert_fusion
  384.7 0.3 convolution_bitcast_fusion.3
  385.0 0.3 convolution_bitcast_fusion.2
  385.4 0.8 copy.39
  386.2 10.9 %all-to-all-done.1 = bf16[4,2,64,512]{3,0,1,2:T(4,128)(2,1)S(1)} async-done(((bf16[4,2,64,512]{3,0,1,2:T(4,128)(2,1)}), bf16[4,2,64,512]{3,0,1,2:T(4,128)(2,1)S(1)}, u32[]{:S(2)}, u32[]{:S(2)}) %all-to-all-start.1) | async-done | bytes 524320 | tf_op jit(solution)/shard_map/all_to_all | solution.py:88
  397.1 0.2 copy.48
  397.4 2.1 fusion.14
  (20 shorter events, 0.7 us)
Async XLA Ops:
  7.2 18.7 %copy-start = (bf16[4,512,512]{2,1,0:T(8,128)(2,1)S(1)}, bf16[4,512,512]{2,1,0:T(8,128)(2,1)}, u32[]{:S(2)}) copy-start(bf16[4,512,512]{2,1,0:T(8,128)(2,1)} %param.4) | copy-start | bytes 6291460
  13.4 34.4 %all-to-all-start = ((f32[64,2,4,512]{3,2,1,0:T(4,128)}), f32[64,2,4,512]{3,2,1,0:T(4,128)S(1)}, u32[]{:S(2)}, u32[]{:S(2)}) async-start(f32[64,2,4,512]{3,2,1,0:T(4,128)} %copy.26), calls=%async_computation | async-start | bytes 2097152 | tf_op jit(solution)/shard_map/all_to_all | solution.py:72
  47.8 9.1 %copy-start.1 = (f32[64,2,4,512]{3,2,1,0:T(4,128)}, f32[64,2,4,512]{3,2,1,0:T(4,128)S(1)}, u32[]{:S(2)}) copy-start(f32[64,2,4,512]{3,2,1,0:T(4,128)S(1)} %all-to-all-done) | copy-start | bytes 3145732
  47.8 28.9 %all-to-all-start.2 = ((f32[64,2,4,512]{3,2,1,0:T(4,128)}), f32[64,2,4,512]{3,2,1,0:T(4,128)}, u32[]{:S(2)}, u32[]{:S(2)}) async-start(f32[64,2,4,512]{3,2,1,0:T(4,128)} %copy.33), calls=%async_computation.2 | async-start | bytes 2097152 | tf_op jit(solution)/shard_map/all_to_all | solution.py:71
  56.8 208.7 %all-reduce.5.cloned.1.call-start = ((), (), s32[]{:S(2)}) async-start(), calls=%async_computation.3 | async-start | bytes 6291456
  78.0 3.4 copy-start.2
  355.5 41.6 %all-to-all-start.1 = ((bf16[4,2,64,512]{3,0,1,2:T(4,128)(2,1)}), bf16[4,2,64,512]{3,0,1,2:T(4,128)(2,1)S(1)}, u32[]{:S(2)}, u32[]{:S(2)}) async-start(bf16[4,2,64,512]{3,0,1,2:T(4,128)(2,1)} %copy.31), calls=%async_computation.1 | async-start | bytes 1048576 | tf_op jit(solution)/shard_map/all_to_all | solution.py:88
Sparse Core Ops, SparseCore 0:
  79.5 185.9 all-reduce.4
where the time goes:
time: 407 us; the launch traced here: 406 us
  waiting for transfers between devices  229 us (56%)
  blocking collectives  85.9 us (21%)
  starting transfers between devices  49.1 us (12%)
  local copies, waits for them, and re-layouts  17.5 us (4%)
  between operations  14.9 us (4%)
  matrix products  7.56 us (2%)
    unnamed x2, waiting for transfers between devices  183 us
    psum x1, blocking collectives, shards(): mode_grad = lax.psum(partial_terms, 'space').astype(jnp.bfloat16)  85.9 us
    all_to_all x1, starting transfers between devices, shards(): lax.all_to_all(mode_grad, 'mode', split_axis=2, concat_axis=0, tiled=True)  27.7 us
    all_to_all x1, waiting for transfers between devices, shards(): lax.all_to_all(part_g, 'mode', split_axis=0, concat_axis=2, tiled=True)  19.8 us
    all_to_all x1, waiting for transfers between devices, shards(): lax.all_to_all(part_u, 'mode', split_axis=0, concat_axis=2, tiled=True)  15.5 us
    all_to_all x1, starting transfers between devices, shards(): lax.all_to_all(part_g, 'mode', split_axis=0, concat_axis=2, tiled=True)  12.4 us
    all_to_all x1, waiting for transfers between devices, shards(): lax.all_to_all(mode_grad, 'mode', split_axis=2, concat_axis=0, tiled=True)  10.9 us
    all_to_all x1, starting transfers between devices, shards(): lax.all_to_all(part_u, 'mode', split_axis=0, concat_axis=2, tiled=True)  9.01 us
  transfers between devices with their start and end apart: 4, of which 4 were waited for; matrix products, arithmetic and copies ran while one was open for 3% of the time, Pallas kernels for 0%

commit v1 on v0

v1 whole, which is shorter than its diff:
```python
import functools
import math

import jax
import jax.numpy as jnp
from jax import lax
from jax.experimental import pallas as pl
from jax.experimental.pallas import tpu as pltpu
from jax.sharding import Mesh
from jax.sharding import PartitionSpec as P

F32, BF16 = jnp.float32, jnp.bfloat16
FIRST = ("y", "x")
SECOND = ("zl", "w")
NT = (((1,), (1,)), ((), ()))
TN = (((0,), (0,)), ((), ()))


def make_table(n_modes, points, offset, total):
    wave_nums = jnp.arange(n_modes, dtype=jnp.int32)
    position = jnp.arange(points, dtype=jnp.int32) + offset
    phases = wave_nums[:, None] * position[None, :] % total
    angles = phases.astype(F32) * (2.0 * math.pi / total)
    return jnp.concatenate([jnp.cos(angles), -jnp.sin(angles)], axis=0).astype(BF16)


def gelu_slope(values):
    normal_cdf = 0.5 * (1.0 + lax.erf(values * (1.0 / math.sqrt(2.0))))
    density = jnp.exp(-0.5 * values * values) * (1.0 / math.sqrt(2.0 * math.pi))
    return normal_cdf + values * density


def dot(a, b, dims=None):
    if dims is None:
        return jnp.dot(a, b, preferred_element_type=F32)
    return lax.dot_general(a, b, dims, preferred_element_type=F32)


def row_moves(n, digits):
    row = lax.broadcasted_iota(jnp.int32, (n, n), 0)
    col = lax.broadcasted_iota(jnp.int32, (n, n), 1)
    source = jnp.zeros((n, n), jnp.int32)
    for out_stride, size, in_stride in digits:
        digit = (row >> (out_stride.bit_length() - 1)) & (size - 1)
        source = source + (digit << (in_stride.bit_length() - 1))
    return jnp.where(source == col, 1.0, 0.0).astype(BF16)


def turned(n):
    row = lax.broadcasted_iota(jnp.int32, (n, n), 0)
    col = lax.broadcasted_iota(jnp.int32, (n, n), 1)
    sign = jnp.where((row & 4) == 0, 1.0, -1.0)
    return jnp.where((row ^ 4) == col, sign, 0.0).astype(BF16)


def gather_lanes(values, quarter):
    lane = lax.broadcasted_iota(jnp.int32, (values.shape[0], 128), 1) >> 5
    out = None
    for j in range(4):
        block = values[:, 128 * j : 128 * j + 128]
        shift = (32 * (j - quarter)) % 128
        if shift:
            block = pltpu.roll(block, shift, 1)
        out = block if out is None else jnp.where(lane == j, block, out)
    return out


def spectra_kernel(table_ref, fields_ref, pre_ref, cot_ref, out_ref, table_u):
    @pl.when((pl.program_id(0) == 0) & (pl.program_id(1) == 0))
    def _():
        moves = row_moves(128, [(64, 2, 64), (16, 4, 1), (4, 4, 16), (1, 4, 4)])
        table_u[...] = dot(moves, table_ref[...]).astype(BF16)

    spec_u = dot(table_u[...], fields_ref[0]).astype(BF16)
    slopes = cot_ref[0].astype(F32) * gelu_slope(pre_ref[0].astype(F32))
    spec_g = dot(table_ref[...], slopes.astype(BF16)).astype(BF16)
    for j in range(4):
        for p in range(2):
            rows = slice(64 * p + 16 * j, 64 * p + 16 * j + 16)
            out_ref[j, 16 * p : 16 * p + 16, :] = spec_g[rows]
            out_ref[j, 32 + 16 * p : 48 + 16 * p, :] = spec_u[rows]


def sum_y_kernel(in_ref, out_ref):
    total = in_ref[0:4].astype(F32)
    for y in range(1, 4):
        total = total + in_ref[4 * y : 4 * y + 4].astype(F32)
    low = total.astype(BF16)
    g = low[:, :32].reshape(128, 512)
    u = low[:, 32:].reshape(128, 512)
    g = dot(row_moves(128, [(32, 4, 1), (8, 4, 4), (4, 2, 16), (1, 4, 32)]), g)
    u = dot(row_moves(128, [(32, 4, 32), (8, 4, 4), (4, 2, 16), (1, 4, 1)]), u)
    for i in range(16):
        both = jnp.concatenate([g[8 * i : 8 * i + 8], u[8 * i : 8 * i + 8]], axis=0)
        out_ref[i] = both.astype(BF16)


def modes_kernel(factor, where_ref, in_ref, w_ref, out_ref):
    total = in_ref[0:4].astype(F32)
    for zl in range(1, 4):
        total = total + in_ref[4 * zl : 4 * zl + 4].astype(F32)
    first_mode = (where_ref[0] == 0) & (where_ref[1] == 0) & (where_ref[2] == 0)
    g = total[:, :8].reshape(32, 512) * jnp.where(first_mode, factor, 2.0 * factor)
    u = total[:, 8:].reshape(32, 512) * factor
    g_low = g.astype(BF16)
    u = dot(row_moves(32, [(8, 4, 1), (4, 2, 4), (1, 4, 8)]), u.astype(BF16))
    g_turned = dot(turned(32), g_low).astype(BF16)
    grad = dot(g_low, w_ref[0], NT) + dot(g_turned, w_ref[1], NT)
    for zl in range(4):
        lanes = gather_lanes(g, zl)
        chunk = jnp.concatenate([lanes[8 * w : 8 * w + 8] for w in range(4)], axis=1)
        for w in range(4):
            rows = slice(8 * w, 8 * w + 8)
            out_ref[4 * zl + w] = jnp.concatenate([grad[rows], u[rows], chunk], axis=0).astype(BF16)


def turn_kernel(where_ref, in_ref, out_ref):
    grad = in_ref[:, 0:8].astype(F32).reshape(128, 512).astype(BF16)
    u = in_ref[:, 8:16].astype(F32).reshape(128, 512).astype(BF16)
    grad = dot(row_moves(128, [(32, 4, 1), (16, 2, 4), (4, 4, 8), (1, 4, 32)]), grad)
    u = dot(row_moves(128, [(32, 4, 8), (8, 4, 1), (4, 2, 4), (1, 4, 32)]), u)
    mine = [in_ref[4 * ki + where_ref[1], 16:24, :].astype(F32) for ki in range(4)]
    for y in range(4):
        chunk = jnp.concatenate([gather_lanes(m, y) for m in mine], axis=1)
        for x in range(4):
            rows = slice(32 * x, 32 * x + 32)
            out_ref[4 * y + x] = jnp.concatenate([grad[rows], u[rows], chunk], axis=0).astype(BF16)


def last_kernel(factor, where_ref, in_ref, table_ref, field_ref, weight_ref):
    sub = pl.program_id(0)

    @pl.when(sub == 0)
    def _():
        g = jnp.concatenate(
            [in_ref[4 * s + where_ref[0], 64:72, :].astype(F32) for s in range(4)], axis=0
        )
        g_turned = dot(turned(32), g.astype(BF16))
        lane = lax.broadcasted_iota(jnp.int32, (32, 128), 1)
        for ki in range(4):
            one, two = (v[:, 128 * ki : 128 * ki + 128] for v in (g, g_turned))
            left, right = [], []
            for w in range(4):
                a = pltpu.roll(one, (128 - 32 * w) % 128, 1) if w else one
                b = pltpu.roll(two, (160 - 32 * w) % 128, 1) if w != 1 else two
                left.append(jnp.where(lane < 32, a, b))
                for s in range(4):
                    right.append(in_ref[4 * s + ki, 32 + 8 * w : 40 + 8 * w, :].astype(F32))
            left = jnp.concatenate(left, axis=0).astype(BF16)
            right = jnp.concatenate(right, axis=0).astype(BF16)
            grad = dot(left, right, TN)
            weight_ref[ki, 0] = grad[0:32]
            weight_ref[ki, 1] = grad[32:64]

    modes = jnp.concatenate(
        [in_ref[4 * sub + j, 16 * p : 16 * p + 16, :] for p in range(2) for j in range(4)], axis=0
    )
    field_ref[0] = (dot(table_ref[...], modes) * factor).astype(BF16)


def shards(fields, pre_act, cotangent, weights):
    points = fields.shape[1]
    total = points * lax.axis_size("y") * lax.axis_size("zl")
    factor = float(total) ** (-0.5)
    x, w, zl = lax.axis_index("x"), lax.axis_index("w"), lax.axis_index("zl")
    table = make_table(64, points, (lax.axis_index("y") * 4 + zl) * points, total)
    where = jnp.stack([x, w, zl]).astype(jnp.int32)
    smem = pl.BlockSpec(memory_space=pltpu.SMEM)
    vmem = pl.BlockSpec(memory_space=pltpu.VMEM)
    params = pltpu.CompilerParams(vmem_limit_bytes=40 * 2**20)

    half = pl.BlockSpec((1, 512, 256), lambda b, h: (b, 0, h))
    send = pl.pallas_call(
        spectra_kernel,
        grid=(4, 2),
        in_specs=[pl.BlockSpec((128, 512), lambda b, h: (0, 0)), half, half, half],
        out_specs=pl.BlockSpec((4, 64, 256), lambda b, h: (b, 0, h)),
        out_shape=jax.ShapeDtypeStruct((16, 64, 512), BF16),
        scratch_shapes=[pltpu.VMEM((128, 512), BF16)],
        compiler_params=params,
        name="spectra",
    )(table, fields, pre_act, cotangent)
    got = lax.all_to_all(send, FIRST, 0, 0, tiled=True)
    send = pl.pallas_call(
        sum_y_kernel,
        in_specs=[vmem],
        out_specs=vmem,
        out_shape=jax.ShapeDtypeStruct((16, 16, 512), BF16),
        compiler_params=params,
        name="sum_y",
    )(got)
    got = lax.all_to_all(send, SECOND, 0, 0, tiled=True)
    mine = lax.dynamic_index_in_dim(weights, zl, 0, keepdims=False)
    send = pl.pallas_call(
        functools.partial(modes_kernel, factor),
        in_specs=[smem, vmem, vmem],
        out_specs=vmem,
        out_shape=jax.ShapeDtypeStruct((16, 24, 512), BF16),
        compiler_params=params,
        name="modes",
    )(where, got, mine)
    got = lax.all_to_all(send, SECOND, 0, 0, tiled=True)
    send = pl.pallas_call(
        turn_kernel,
        in_specs=[smem, vmem],
        out_specs=vmem,
        out_shape=jax.ShapeDtypeStruct((16, 72, 512), BF16),
        compiler_params=params,
        name="turn",
    )(where, got)
    got = lax.all_to_all(send, FIRST, 0, 0, tiled=True)
    field_grad, weight_grad = pl.pallas_call(
        functools.partial(last_kernel, factor),
        grid=(4,),
        in_specs=[
            smem,
            pl.BlockSpec((16, 72, 512), lambda b: (0, 0, 0)),
            pl.BlockSpec((512, 128), lambda b: (0, 0)),
        ],
        out_specs=[
            pl.BlockSpec((1, 512, 512), lambda b: (b, 0, 0)),
            pl.BlockSpec((4, 2, 32, 512), lambda b: (0, 0, 0, 0)),
        ],
        out_shape=[
            jax.ShapeDtypeStruct((4, 512, 512), BF16),
            jax.ShapeDtypeStruct((4, 2, 32, 512), F32),
        ],
        compiler_params=params,
        name="last",
    )(where, got, table.T)
    return field_grad, jnp.swapaxes(weight_grad, 2, 3)


def solution(mesh):
    grid = Mesh(mesh.devices.reshape(4, 4, 4, 4), ("y", "zl", "x", "w"))
    space, mode = ("y", "zl"), ("x", "w")
    whole = P(mode, space, None)
    return jax.shard_map(
        shards,
        mesh=grid,
        in_specs=(whole, whole, whole, P(mode, None, None, None)),
        out_specs=(whole, P(mode, None, None, space)),
        check_vma=False,
    )
```

time: 407 us -> 107 us (0.26)
  waiting for transfers between devices: 229 us -> 31.5 us
  blocking collectives: 85.9 us -> 40.5 us
  starting transfers between devices: 49.1 us -> 14.2 us
  between operations: 14.9 us -> 0.72 us
  Pallas kernels: 0 us -> 11.5 us
  local copies, waits for them, and re-layouts: 17.5 us -> 6.3 us
  matrix products: 7.56 us -> 0 us
    unnamed x2 -> x0, waiting for transfers between devices: 183 us -> none
    psum x1 -> x0, blocking collectives: 85.9 us -> none  [shards(): mode_grad = lax.psum(partial_terms, 'space').astype(jnp.bfloat16)]
    all_to_all x0 -> x2, blocking collectives: none -> 40.5 us  [the longest x1 23.5 us: shards(): got = lax.all_to_all(send, FIRST, 0, 0, tiled=True)]
    all_to_all x3 -> x2, starting transfers between devices: 49.1 us -> 14.2 us  [the longest x1 10.5 us: shards(): got = lax.all_to_all(send, SECOND, 0, 0, tiled=True)]
    all_to_all x3 -> x2, waiting for transfers between devices: 46.2 us -> 31.5 us  [the longest x1 21.2 us: shards(): got = lax.all_to_all(send, FIRST, 0, 0, tiled=True)]
    pallas_call x0 -> x5, Pallas kernels: none -> 11.5 us  [the longest x1 4.11 us: shards(): pl.pallas_call(spectra_kernel, grid=(4, 2), in_specs=[pl.BlockSpec((128,...]
    dot_general x7 -> x0, matrix products: 7.56 us -> none  [the longest x1 4.01 us: shards(): jnp.einsum('kpx,bxc->kpbc', table, slopes, preferred_element_type=jnp.flo...]
    all_to_all x6 -> x0, local copies, waits for them, and re-layouts: 7.26 us -> none  [the longest x2 4.28 us: shards(): lax.all_to_all(part_g, 'mode', split_axis=0, concat_axis=2, tiled=True)]
  transfers between devices with their start and end apart: 4 -> 2, of which waited for: 4 -> 2; matrix products, arithmetic and copies ran while one was open for 3% -> 1% of each run, Pallas kernels for 0% -> 0%
where the time goes in v1:
time: 107 us; the launch traced here: 106 us
  blocking collectives  40.5 us (38%)
  waiting for transfers between devices  31.5 us (29%)
  starting transfers between devices  14.2 us (13%)
  Pallas kernels  11.5 us (11%)
  local copies, waits for them, and re-layouts  6.3 us (6%)
  other arithmetic  1.37 us (1%)
    all_to_all x1, blocking collectives, shards(): got = lax.all_to_all(send, FIRST, 0, 0, tiled=True)  23.5 us
    all_to_all x1, waiting for transfers between devices, shards(): got = lax.all_to_all(send, FIRST, 0, 0, tiled=True)  21.2 us
    all_to_all x1, blocking collectives, shards(): got = lax.all_to_all(send, SECOND, 0, 0, tiled=True)  17 us
    all_to_all x1, starting transfers between devices, shards(): got = lax.all_to_all(send, SECOND, 0, 0, tiled=True)  10.5 us
    all_to_all x1, waiting for transfers between devices, shards(): got = lax.all_to_all(send, SECOND, 0, 0, tiled=True)  10.3 us
    unnamed x6, local copies, waits for them, and re-layouts  4.77 us
    pallas_call x1, Pallas kernels, shards(): pl.pallas_call(spectra_kernel, grid=(4, 2), in_specs=[pl.BlockSpec((128,...  4.11 us
    all_to_all x1, starting transfers between devices, shards(): got = lax.all_to_all(send, FIRST, 0, 0, tiled=True)  3.7 us
  transfers between devices with their start and end apart: 2, of which 2 were waited for; matrix products, arithmetic and copies ran while one was open for 1% of the time, Pallas kernels for 0%

profile of v1, /device:TPU:1, one launch (start us, length us, event | category | flops | bytes accessed | tf_op | source)
XLA Modules:
  0.0 106.1 jit_solution(13669570215692566830)
XLA Ops:
  0.6 0.1 fusion.1
  0.7 0.1 copy.7
  0.8 1.0 cosine_convert_fusion
  1.9 0.1 pad_maximum_fusion
  2.0 0.1 copy.8.table_ref
  2.1 0.0 copy-start
  2.1 1.6 %copy-done = bf16[4,512,512]{2,1,0:T(8,128)(2,1)S(1)} copy-done((bf16[4,512,512]{2,1,0:T(8,128)(2,1)S(1)}, bf16[4,512,512]{2,1,0:T(8,128)(2,1)}, u32[]{:S(2)}) %copy-start) | copy-done | bytes 2097176
  3.7 0.0 copy-start.1
  3.7 1.6 %copy-done.1 = bf16[4,512,512]{2,1,0:T(8,128)(2,1)S(1)} copy-done((bf16[4,512,512]{2,1,0:T(8,128)(2,1)S(1)}, bf16[4,512,512]{2,1,0:T(8,128)(2,1)}, u32[]{:S(2)}) %copy-start.1) | copy-done | bytes 2097176
  5.3 0.0 copy-start.2
  5.3 1.6 %copy-done.2 = bf16[4,512,512]{2,1,0:T(8,128)(2,1)S(1)} copy-done((bf16[4,512,512]{2,1,0:T(8,128)(2,1)S(1)}, bf16[4,512,512]{2,1,0:T(8,128)(2,1)}, u32[]{:S(2)}) %copy-start.2) | copy-done | bytes 2097176
  6.9 4.1 %spectra.1 = bf16[16,64,512]{2,1,0:T(8,128)(2,1)S(1)} custom-call(bf16[128,512]{1,0:T(8,128)(2,1)S(1)} %copy.8.table_ref, bf16[4,512,512]{2,1,0:T(8,128)(2,1)S(1)} %copy-done, bf16[4,512,512]{2,1,0:T(8,128)(2,1)S(1)} %copy-done.1, bf16[4,512,512]{2,1,0:T(8,128)(2,1)S(1)} %copy-done.2), custom_call_target="tpu_custom_call" | custom-call | tf_op jit(solution)/shard_map/spectra/pallas_call | solution.py:173
  11.0 23.5 %all_to_all.20.in_ref = bf16[16,64,512]{2,1,0:T(8,128)(2,1)S(1)} all-to-all(bf16[16,64,512]{2,1,0:T(8,128)(2,1)S(1)} %spectra.1), channel_id=1, replica_groups=mesh['y'=4,'zl'=4,'x'=4,'w'=4] {'y','x'}, dimensions={0} | all-to-all | bytes 2097152 | tf_op jit(solution)/shard_map/all_to_all | solution.py:183
  34.5 1.0 sum_y.1
  35.5 10.5 %all-to-all-start.1 = ((bf16[16,16,512]{2,1,0:T(8,128)(2,1)}), bf16[16,16,512]{2,1,0:T(8,128)(2,1)S(1)}, u32[]{:S(2)}, u32[]{:S(2)}) async-start(bf16[16,16,512]{2,1,0:T(8,128)(2,1)} %sum_y.1), calls=%async_computation.1 | async-start | bytes 524288 | tf_op jit(solution)/shard_map/all_to_all | solution.py:192
  46.0 0.1 pad_add_fusion.where_ref
  46.1 1.3 %dynamic-slice_bitcast_fusion.w_ref = bf16[2,512,512]{2,1,0:T(8,128)(2,1)S(1)} fusion(bf16[4,2,512,512]{3,2,1,0:T(8,128)(2,1)} %param.7, s32[]{:T(128)S(6)} %select_n.12), kind=kLoop, calls=%fused_computation | loop fusion | bytes 2097156 | tf_op jit(solution)/shard_map/jit(dynamic_index_in_dim)/squeeze | solution.py:193
  47.4 10.3 %all-to-all-done.1.in_ref = bf16[16,16,512]{2,1,0:T(8,128)(2,1)S(1)} async-done(((bf16[16,16,512]{2,1,0:T(8,128)(2,1)}), bf16[16,16,512]{2,1,0:T(8,128)(2,1)S(1)}, u32[]{:S(2)}, u32[]{:S(2)}) %all-to-all-start.1) | async-done | bytes 262176 | tf_op jit(solution)/shard_map/all_to_all | solution.py:192
  57.7 1.0 modes.1
  58.7 17.0 %all_to_all.21.in_ref = bf16[16,24,512]{2,1,0:T(8,128)(2,1)S(1)} all-to-all(bf16[16,24,512]{2,1,0:T(8,128)(2,1)S(1)} %modes.1), channel_id=1, replica_groups=mesh['y'=4,'zl'=4,'x'=4,'w'=4] {'zl','w'}, dimensions={0} | all-to-all | bytes 786432 | tf_op jit(solution)/shard_map/all_to_all | solution.py:202
  75.8 1.8 %turn.1 = bf16[16,72,512]{2,1,0:T(8,128)(2,1)} custom-call(s32[3]{0:T(128)S(1)} %pad_add_fusion.where_ref, bf16[16,24,512]{2,1,0:T(8,128)(2,1)S(1)} %all_to_all.21.in_ref), custom_call_target="tpu_custom_call" | custom-call | tf_op jit(solution)/shard_map/turn/pallas_call | solution.py:203
  77.6 3.7 %all-to-all-start.3 = ((bf16[16,72,512]{2,1,0:T(8,128)(2,1)}), bf16[16,72,512]{2,1,0:T(8,128)(2,1)S(1)}, u32[]{:S(2)}, u32[]{:S(2)}) async-start(bf16[16,72,512]{2,1,0:T(8,128)(2,1)} %turn.1), calls=%async_computation.3 | async-start | bytes 2359296 | tf_op jit(solution)/shard_map/all_to_all | solution.py:211
  81.3 0.1 fusion.5.table_ref
  81.4 21.2 %all-to-all-done.3.in_ref = bf16[16,72,512]{2,1,0:T(8,128)(2,1)S(1)} async-done(((bf16[16,72,512]{2,1,0:T(8,128)(2,1)}), bf16[16,72,512]{2,1,0:T(8,128)(2,1)S(1)}, u32[]{:S(2)}, u32[]{:S(2)}) %all-to-all-start.3) | async-done | bytes 1179680 | tf_op jit(solution)/shard_map/all_to_all | solution.py:211
  102.5 3.6 %last.1 = (bf16[4,512,512]{2,1,0:T(8,128)(2,1)}, f32[4,2,32,512]{3,2,1,0:T(8,128)}) custom-call(s32[3]{0:T(128)S(1)} %pad_add_fusion.where_ref, bf16[16,72,512]{2,1,0:T(8,128)(2,1)S(1)} %all-to-all-done.3.in_ref, bf16[512,128]{1,0:T(8,128)(2,1)S(1)} %fusion.5.table_ref), custom_call_target="tpu_custom_call" | custom-call | tf_op jit(solution)/shard_map/last/pallas_call | solution.py:212
  (1 shorter events, 0.0 us)
Async XLA Ops:
  2.1 1.6 %copy-start = (bf16[4,512,512]{2,1,0:T(8,128)(2,1)S(1)}, bf16[4,512,512]{2,1,0:T(8,128)(2,1)}, u32[]{:S(2)}) copy-start(bf16[4,512,512]{2,1,0:T(8,128)(2,1)} %fields_ref.1) | copy-start | bytes 6291460
  3.7 1.6 %copy-start.1 = (bf16[4,512,512]{2,1,0:T(8,128)(2,1)S(1)}, bf16[4,512,512]{2,1,0:T(8,128)(2,1)}, u32[]{:S(2)}) copy-start(bf16[4,512,512]{2,1,0:T(8,128)(2,1)} %pre_ref.1) | copy-start | bytes 6291460
  5.3 1.6 %copy-start.2 = (bf16[4,512,512]{2,1,0:T(8,128)(2,1)S(1)}, bf16[4,512,512]{2,1,0:T(8,128)(2,1)}, u32[]{:S(2)}) copy-start(bf16[4,512,512]{2,1,0:T(8,128)(2,1)} %cot_ref.1) | copy-start | bytes 6291460
  35.5 22.2 %all-to-all-start.1 = ((bf16[16,16,512]{2,1,0:T(8,128)(2,1)}), bf16[16,16,512]{2,1,0:T(8,128)(2,1)S(1)}, u32[]{:S(2)}, u32[]{:S(2)}) async-start(bf16[16,16,512]{2,1,0:T(8,128)(2,1)} %sum_y.1), calls=%async_computation.1 | async-start | bytes 524288 | tf_op jit(solution)/shard_map/all_to_all | solution.py:192
  77.6 25.0 %all-to-all-start.3 = ((bf16[16,72,512]{2,1,0:T(8,128)(2,1)}), bf16[16,72,512]{2,1,0:T(8,128)(2,1)S(1)}, u32[]{:S(2)}, u32[]{:S(2)}) async-start(bf16[16,72,512]{2,1,0:T(8,128)(2,1)} %turn.1), calls=%async_computation.3 | async-start | bytes 2359296 | tf_op jit(solution)/shard_map/all_to_all | solution.py:211

commit v2 on v1

v2 whole, which is shorter than its diff:
```python
import functools
import math

import jax
import jax.numpy as jnp
from jax import lax
from jax.experimental import pallas as pl
from jax.experimental.pallas import tpu as pltpu
from jax.sharding import Mesh
from jax.sharding import PartitionSpec as P

F32, BF16 = jnp.float32, jnp.bfloat16
FIRST = ("y", "x")
SECOND = ("zl", "w")
SPECTRA_VMEM = 61 * 2**20
NT = (((1,), (1,)), ((), ()))
TN = (((0,), (0,)), ((), ()))


def make_table(n_modes, points, offset, total):
    wave_nums = jnp.arange(n_modes, dtype=jnp.int32)
    position = jnp.arange(points, dtype=jnp.int32) + offset
    phases = wave_nums[:, None] * position[None, :] % total
    angles = phases.astype(F32) * (2.0 * math.pi / total)
    return jnp.concatenate([jnp.cos(angles), -jnp.sin(angles)], axis=0).astype(BF16)


def gelu_slope(values):
    normal_cdf = 0.5 * (1.0 + lax.erf(values * (1.0 / math.sqrt(2.0))))
    density = jnp.exp(-0.5 * values * values) * (1.0 / math.sqrt(2.0 * math.pi))
    return normal_cdf + values * density


def dot(a, b, dims=None):
    if dims is None:
        return jnp.dot(a, b, preferred_element_type=F32)
    return lax.dot_general(a, b, dims, preferred_element_type=F32)


def row_moves(n, digits):
    row = lax.broadcasted_iota(jnp.int32, (n, n), 0)
    col = lax.broadcasted_iota(jnp.int32, (n, n), 1)
    source = jnp.zeros((n, n), jnp.int32)
    for out_stride, size, in_stride in digits:
        digit = (row >> (out_stride.bit_length() - 1)) & (size - 1)
        source = source + (digit << (in_stride.bit_length() - 1))
    return jnp.where(source == col, 1.0, 0.0).astype(BF16)


def turned(n):
    row = lax.broadcasted_iota(jnp.int32, (n, n), 0)
    col = lax.broadcasted_iota(jnp.int32, (n, n), 1)
    sign = jnp.where((row & 4) == 0, 1.0, -1.0)
    return jnp.where((row ^ 4) == col, sign, 0.0).astype(BF16)


def gather_lanes(values, quarter):
    lane = lax.broadcasted_iota(jnp.int32, (values.shape[0], 128), 1) >> 5
    out = None
    for j in range(4):
        block = values[:, 128 * j : 128 * j + 128]
        shift = (32 * (j - quarter)) % 128
        if shift:
            block = pltpu.roll(block, shift, 1)
        out = block if out is None else jnp.where(lane == j, block, out)
    return out


def spectra_kernel(table_ref, fields_ref, pre_ref, cot_ref, out_ref):
    spec_u = dot(table_ref[...], fields_ref[0]).astype(BF16)
    slopes = cot_ref[0].astype(F32) * gelu_slope(pre_ref[0].astype(F32))
    spec_g = dot(table_ref[...], slopes.astype(BF16)).astype(BF16)
    for j in range(4):
        for p in range(2):
            rows = slice(64 * p + 16 * j, 64 * p + 16 * j + 16)
            out_ref[j, 16 * p : 16 * p + 16, :] = spec_g[rows]
            out_ref[j, 32 + 16 * p : 48 + 16 * p, :] = spec_u[rows]


def sum_y_kernel(in_ref, out_ref):
    total = in_ref[0:4].astype(F32)
    for y in range(1, 4):
        total = total + in_ref[4 * y : 4 * y + 4].astype(F32)
    low = total.astype(BF16)
    moves = row_moves(128, [(32, 4, 1), (8, 4, 4), (4, 2, 16), (1, 4, 32)])
    g = dot(moves, low[:, :32].reshape(128, 512))
    u = dot(moves, low[:, 32:].reshape(128, 512))
    for i in range(16):
        both = jnp.concatenate([g[8 * i : 8 * i + 8], u[8 * i : 8 * i + 8]], axis=0)
        out_ref[i] = both.astype(BF16)


def modes_kernel(factor, where_ref, in_ref, w_ref, out_ref, *rest):
    side_refs, chunks = rest[:4], rest[4]
    x, w_mine, zl_mine = where_ref[0], where_ref[1], where_ref[2]
    total = in_ref[0:4].astype(F32)
    for zl in range(1, 4):
        total = total + in_ref[4 * zl : 4 * zl + 4].astype(F32)
    first_mode = (x == 0) & (w_mine == 0) & (zl_mine == 0)
    g = total[:, :8].reshape(32, 512) * jnp.where(first_mode, factor, 2.0 * factor)
    u = total[:, 8:].reshape(32, 512) * factor
    g_low = g.astype(BF16)
    g_turned = dot(turned(32), g_low).astype(BF16)
    grad = dot(g_low, w_ref[0], NT) + dot(g_turned, w_ref[1], NT)
    for w in range(4):
        part = grad[8 * w : 8 * w + 8].astype(BF16)
        for zl in range(4):
            out_ref[4 * zl + w] = part
    for zl in range(4):
        lanes = gather_lanes(g, zl)
        chunks[zl] = jnp.concatenate([lanes[8 * w : 8 * w + 8] for w in range(4)], axis=1)
    for t in range(4):
        chunk = chunks[(zl_mine + t) & 3]
        side_refs[t][...] = jnp.concatenate([u, chunk], axis=0).astype(BF16)


def turn_kernel(where_ref, in_ref, *rest):
    side_refs, out_ref, send_refs, chunks = rest[:4], rest[4], rest[5:9], rest[9]
    y_mine = where_ref[3]
    grad = in_ref[...].astype(F32).reshape(128, 512).astype(BF16)
    grad = dot(row_moves(128, [(32, 4, 1), (16, 2, 4), (4, 4, 8), (1, 4, 32)]), grad)
    for x in range(4):
        part = grad[32 * x : 32 * x + 32].astype(BF16)
        for y in range(4):
            out_ref[4 * y + x] = part
    mine = [ref[32:40, :].astype(F32) for ref in side_refs]
    for y in range(4):
        chunks[y] = jnp.concatenate([gather_lanes(m, y) for m in mine], axis=1)
    for t in range(4):
        for q in range(4):
            send_refs[t][32 * q : 32 * q + 32, :] = side_refs[q][0:32, :]
        send_refs[t][128:136, :] = chunks[(y_mine + t) & 3].astype(BF16)


def weight_kernel(where_ref, *refs):
    in_refs, weight_ref = refs[:4], refs[4]
    zl_mine = where_ref[2]
    g = jnp.concatenate([ref[128:136, :].astype(F32) for ref in in_refs], axis=0)
    g_turned = dot(turned(32), g.astype(BF16))
    lane = lax.broadcasted_iota(jnp.int32, (32, 128), 1)
    for q in range(4):
        one, two = (v[:, 128 * q : 128 * q + 128] for v in (g, g_turned))
        left, right = [], []
        for w in range(4):
            a = pltpu.roll(one, (128 - 32 * w) % 128, 1) if w else one
            b = pltpu.roll(two, (160 - 32 * w) % 128, 1) if w != 1 else two
            left.append(jnp.where(lane < 32, a, b))
            rows = slice(32 * q + 8 * w, 32 * q + 8 * w + 8)
            right += [ref[rows, :].astype(F32) for ref in in_refs]
        left = jnp.concatenate(left, axis=0).astype(BF16)
        right = jnp.concatenate(right, axis=0).astype(BF16)
        grad = dot(left, right, TN)
        ki = (zl_mine - q) & 3
        weight_ref[ki, 0] = grad[0:32]
        weight_ref[ki, 1] = grad[32:64]


def field_kernel(factor, in_ref, table_ref, field_ref):
    modes = jnp.concatenate(
        [in_ref[j, 16 * p : 16 * p + 16, :] for p in range(2) for j in range(4)], axis=0
    )
    field_ref[0] = (dot(table_ref[...], modes) * factor).astype(BF16)


def shifted(value, axis, distance):
    return lax.ppermute(value, axis, [(i, (i + distance) % 4) for i in range(4)])


def shards(fields, pre_act, cotangent, weights):
    points = fields.shape[1]
    total = points * lax.axis_size("y") * lax.axis_size("zl")
    factor = float(total) ** (-0.5)
    x, w, zl, y = (lax.axis_index(name) for name in ("x", "w", "zl", "y"))
    table = make_table(64, points, (y * 4 + zl) * points, total)
    where = jnp.stack([x, w, zl, y]).astype(jnp.int32)
    smem = pl.BlockSpec(memory_space=pltpu.SMEM)
    vmem = pl.BlockSpec(memory_space=pltpu.VMEM)
    params = pltpu.CompilerParams(vmem_limit_bytes=40 * 2**20)

    def block(*shape):
        return jax.ShapeDtypeStruct(shape, BF16)

    half = pl.BlockSpec((1, 512, 256), lambda b, h: (b, 0, h))
    send = pl.pallas_call(
        spectra_kernel,
        grid=(4, 2),
        in_specs=[pl.BlockSpec((128, 512), lambda b, h: (0, 0)), half, half, half],
        out_specs=pl.BlockSpec((4, 64, 256), lambda b, h: (b, 0, h)),
        out_shape=block(16, 64, 512),
        compiler_params=pltpu.CompilerParams(vmem_limit_bytes=SPECTRA_VMEM),
        name="spectra",
    )(table, fields, pre_act, cotangent)
    got = lax.all_to_all(send, FIRST, 0, 0, tiled=True)
    send = pl.pallas_call(
        sum_y_kernel,
        in_specs=[vmem],
        out_specs=vmem,
        out_shape=block(16, 16, 512),
        compiler_params=params,
        name="sum_y",
    )(got)
    got = lax.all_to_all(send, SECOND, 0, 0, tiled=True)
    mine = lax.dynamic_index_in_dim(weights, zl, 0, keepdims=False)
    send, *sides = pl.pallas_call(
        functools.partial(modes_kernel, factor),
        in_specs=[smem, vmem, vmem],
        out_specs=[vmem] * 5,
        out_shape=[block(16, 8, 512)] + [block(40, 512)] * 4,
        scratch_shapes=[pltpu.VMEM((4, 8, 512), F32)],
        compiler_params=params,
        name="modes",
    )(where, got, mine)
    sides = [sides[0]] + [shifted(sides[t], "zl", t) for t in range(1, 4)]
    got = lax.all_to_all(send, SECOND, 0, 0, tiled=True)
    send, *sides = pl.pallas_call(
        turn_kernel,
        in_specs=[smem] + [vmem] * 5,
        out_specs=[vmem] * 5,
        out_shape=[block(16, 32, 512)] + [block(136, 512)] * 4,
        scratch_shapes=[pltpu.VMEM((4, 8, 512), F32)],
        compiler_params=params,
        name="turn",
    )(where, got, *sides)
    sides = [sides[0]] + [shifted(sides[t], "y", t) for t in range(1, 4)]
    got = lax.all_to_all(send, FIRST, 0, 0, tiled=True)
    weight_grad = pl.pallas_call(
        weight_kernel,
        in_specs=[smem] + [vmem] * 4,
        out_specs=vmem,
        out_shape=jax.ShapeDtypeStruct((4, 2, 32, 512), F32),
        compiler_params=params,
        cost_estimate=pl.CostEstimate(
            flops=2**26, bytes_accessed=2**20, transcendentals=0
        ),
        name="weight",
    )(where, *sides)
    field_grad = pl.pallas_call(
        functools.partial(field_kernel, factor),
        grid=(4,),
        in_specs=[
            pl.BlockSpec((4, 32, 512), lambda b: (b, 0, 0)),
            pl.BlockSpec((512, 128), lambda b: (0, 0)),
        ],
        out_specs=pl.BlockSpec((1, 512, 512), lambda b: (b, 0, 0)),
        out_shape=block(4, 512, 512),
        compiler_params=params,
        name="field",
    )(got, lax.optimization_barrier(table).T)
    return field_grad, jnp.swapaxes(weight_grad, 2, 3)


def solution(mesh):
    grid = Mesh(mesh.devices.reshape(4, 4, 4, 4), ("y", "zl", "x", "w"))
    space, mode = ("y", "zl"), ("x", "w")
    whole = P(mode, space, None)
    return jax.shard_map(
        shards,
        mesh=grid,
        in_specs=(whole, whole, whole, P(mode, None, None, None)),
        out_specs=(whole, P(mode, None, None, space)),
        check_vma=False,
    )
```

time: 107 us -> 97.9 us (0.915)
  blocking collectives: 40.5 us -> 23.7 us
  starting transfers between devices: 14.2 us -> 27.1 us
  waiting for transfers between devices: 31.5 us -> 26 us
  Pallas kernels: 11.5 us -> 16.3 us
  local copies, waits for them, and re-layouts: 6.3 us -> 2.19 us
    all_to_all x1, waiting for transfers between devices: 21.2 us -> 0.01 us  [shards(): got = lax.all_to_all(send, FIRST, 0, 0, tiled=True)]
    all_to_all x1 -> x0, blocking collectives: 17 us -> none  [shards(): got = lax.all_to_all(send, SECOND, 0, 0, tiled=True)]
    ppermute x0 -> x6, waiting for transfers between devices: none -> 14.6 us  [shifted(): lax.ppermute(value, axis, [(i, (i + distance) % 4) for i in range(4)])]
    ppermute x0 -> x6, starting transfers between devices: none -> 9.57 us  [shifted(): lax.ppermute(value, axis, [(i, (i + distance) % 4) for i in range(4)])]
    unnamed x6 -> x0, local copies, waits for them, and re-layouts: 4.77 us -> none
    pallas_call x1, Pallas kernels: 4.11 us -> 7.84 us  [shards(): pl.pallas_call(spectra_kernel, grid=(4, 2), in_specs=[pl.BlockSpec((128,...]
    all_to_all x1 -> x2, starting transfers between devices: 10.5 us -> 13.9 us  [shards(): got = lax.all_to_all(send, SECOND, 0, 0, tiled=True)]
    all_to_all x1 -> x2, waiting for transfers between devices: 10.3 us -> 11.3 us  [shards(): got = lax.all_to_all(send, SECOND, 0, 0, tiled=True)]
  transfers between devices with their start and end apart: 2 -> 9, of which waited for: 2 -> 6; matrix products, arithmetic and copies ran while one was open for 1% -> 1% of each run, Pallas kernels for 0% -> 2%
where the time goes in v2:
time: 97.9 us; the launch traced here: 97.3 us
  starting transfers between devices  27.1 us (28%)
  waiting for transfers between devices  26 us (27%)
  blocking collectives  23.7 us (24%)
  Pallas kernels  16.3 us (17%)
  local copies, waits for them, and re-layouts  2.19 us (2%)
  other arithmetic  1.26 us (1%)
    all_to_all x1, blocking collectives, shards(): got = lax.all_to_all(send, FIRST, 0, 0, tiled=True)  23.7 us
    ppermute x6, waiting for transfers between devices, shifted(): lax.ppermute(value, axis, [(i, (i + distance) % 4) for i in range(4)])  14.6 us
    all_to_all x2, starting transfers between devices, shards(): got = lax.all_to_all(send, SECOND, 0, 0, tiled=True)  13.9 us
    all_to_all x2, waiting for transfers between devices, shards(): got = lax.all_to_all(send, SECOND, 0, 0, tiled=True)  11.3 us
    ppermute x6, starting transfers between devices, shifted(): lax.ppermute(value, axis, [(i, (i + distance) % 4) for i in range(4)])  9.57 us
    pallas_call x1, Pallas kernels, shards(): pl.pallas_call(spectra_kernel, grid=(4, 2), in_specs=[pl.BlockSpec((128,...  7.84 us
    all_to_all x1, starting transfers between devices, shards(): got = lax.all_to_all(send, FIRST, 0, 0, tiled=True)  3.57 us
    pallas_call x1, Pallas kernels, shards(): pl.pallas_call(functools.partial(field_kernel, factor), grid=(4,), in_spe...  2.43 us
  transfers between devices with their start and end apart: 9, of which 6 were waited for; matrix products, arithmetic and copies ran while one was open for 1% of the time, Pallas kernels for 2%

profile of v2, /device:TPU:1, one launch (start us, length us, event | category | flops | bytes accessed | tf_op | source)
XLA Modules:
  0.0 97.3 jit_solution(8934464602767361016)
XLA Ops:
  0.6 0.1 fusion.1
  0.7 0.1 copy.7
  0.8 1.0 %cosine_convert_fusion = (bf16[64,512]{0,1:T(8,128)(2,1)S(1)}, bf16[64,512]{0,1:T(8,128)(2,1)S(1)}) fusion(f32[64,512]{0,1:T(8,128)S(1)} %copy.7), kind=kLoop, calls=%fused_computation.2 | loop fusion | flops 131072 | bytes 262144 | tf_op jit(solution)/shard_map/convert
  1.9 0.1 pad_maximum_fusion
  2.0 0.8 copy.8.table_ref
  2.7 7.8 %spectra.1 = bf16[16,64,512]{2,1,0:T(8,128)(2,1)} custom-call(bf16[128,512]{1,0:T(8,128)(2,1)} %copy.8.table_ref, bf16[4,512,512]{2,1,0:T(8,128)(2,1)} %fields_ref.1, bf16[4,512,512]{2,1,0:T(8,128)(2,1)} %pre_ref.1, bf16[4,512,512]{2,1,0:T(8,128)(2,1)} %cot_ref.1), custom_call_target="tpu_custom_call" | custom-call | tf_op jit(solution)/shard_map/spectra/pallas_call | solution.py:184
  10.6 23.7 %all_to_all.20.in_ref = bf16[16,64,512]{2,1,0:T(8,128)(2,1)S(1)} all-to-all(bf16[16,64,512]{2,1,0:T(8,128)(2,1)} %spectra.1), channel_id=1, replica_groups=mesh['y'=4,'zl'=4,'x'=4,'w'=4] {'y','x'}, dimensions={0} | all-to-all | bytes 2097152 | tf_op jit(solution)/shard_map/all_to_all | solution.py:193
  34.3 1.0 %sum_y.1 = bf16[16,16,512]{2,1,0:T(8,128)(2,1)} custom-call(bf16[16,64,512]{2,1,0:T(8,128)(2,1)S(1)} %all_to_all.20.in_ref), custom_call_target="tpu_custom_call" | custom-call | tf_op jit(solution)/shard_map/sum_y/pallas_call | solution.py:194
  35.3 10.5 %all-to-all-start.1 = ((bf16[16,16,512]{2,1,0:T(8,128)(2,1)}), bf16[16,16,512]{2,1,0:T(8,128)(2,1)S(1)}, u32[]{:S(2)}, u32[]{:S(2)}) async-start(bf16[16,16,512]{2,1,0:T(8,128)(2,1)} %sum_y.1), calls=%async_computation.1 | async-start | bytes 524288 | tf_op jit(solution)/shard_map/all_to_all | solution.py:202
  45.8 0.1 pad_add_fusion.where_ref
  45.9 1.3 %dynamic-slice_bitcast_fusion.w_ref = bf16[2,512,512]{2,1,0:T(8,128)(2,1)S(1)} fusion(bf16[4,2,512,512]{3,2,1,0:T(8,128)(2,1)} %param.7, s32[]{:T(128)S(6)} %select_n.12), kind=kLoop, calls=%fused_computation | loop fusion | bytes 2097156 | tf_op jit(solution)/shard_map/jit(dynamic_index_in_dim)/squeeze | solution.py:203
  47.1 10.3 %all-to-all-done.1.in_ref = bf16[16,16,512]{2,1,0:T(8,128)(2,1)S(1)} async-done(((bf16[16,16,512]{2,1,0:T(8,128)(2,1)}), bf16[16,16,512]{2,1,0:T(8,128)(2,1)S(1)}, u32[]{:S(2)}, u32[]{:S(2)}) %all-to-all-start.1) | async-done | bytes 262176 | tf_op jit(solution)/shard_map/all_to_all | solution.py:202
  57.5 1.7 %modes.1 = (bf16[16,8,512]{2,1,0:T(8,128)(2,1)}, bf16[40,512]{1,0:T(8,128)(2,1)S(1)}, bf16[40,512]{1,0:T(8,128)(2,1)S(1)}, bf16[40,512]{1,0:T(8,128)(2,1)S(1)}, bf16[40,512]{1,0:T(8,128)(2,1)S(1)}) custom-call(s32[4]{0:T(128)S(1)} %pad_add_fusion.where_ref, bf16[16,16,512]{2,1,0:T(8,128)(2,1)S(1)} %all-to-all-done.1.in_ref, ...), custom_call_target="tpu_custom_call" | custom-call | tf_op jit(solution)/shard_map/modes/pallas_call | solution.py:204
  59.2 3.5 %all-to-all-start.2 = ((bf16[16,8,512]{2,1,0:T(8,128)(2,1)}), bf16[16,8,512]{2,1,0:T(8,128)(2,1)S(1)}, u32[]{:S(2)}, u32[]{:S(2)}) async-start(bf16[16,8,512]{2,1,0:T(8,128)(2,1)} %get-tuple-element.12), calls=%async_computation.2 | async-start | bytes 262144 | tf_op jit(solution)/shard_map/all_to_all | solution.py:214
  62.7 1.4 %collective-permute-start = (bf16[40,512]{1,0:T(8,128)(2,1)S(1)}, bf16[40,512]{1,0:T(8,128)(2,1)S(1)}, u32[]{:S(2)}, u32[]{:S(2)}) collective-permute-start(bf16[40,512]{1,0:T(8,128)(2,1)S(1)} %get-tuple-element.14), channel_id=1, source_target_pairs={{0,16},{16,32},{32,48},{48,0},{1,17},{17,33},{33,49},{49,1},{2,18}... | collective-permute-start | bytes 122888 | tf_op jit(solution)/shard_map/ppermute | solution.py:166
  64.1 2.1 %collective-permute-start.1 = (bf16[40,512]{1,0:T(8,128)(2,1)S(1)}, bf16[40,512]{1,0:T(8,128)(2,1)S(1)}, u32[]{:S(2)}, u32[]{:S(2)}) collective-permute-start(bf16[40,512]{1,0:T(8,128)(2,1)S(1)} %get-tuple-element.15), channel_id=1, source_target_pairs={{0,32},{16,48},{32,0},{48,16},{1,33},{17,49},{33,1},{49,17},{2,34}... | collective-permute-start | bytes 122888 | tf_op jit(solution)/shard_map/ppermute | solution.py:166
  66.2 1.2 %collective-permute-start.2 = (bf16[40,512]{1,0:T(8,128)(2,1)S(1)}, bf16[40,512]{1,0:T(8,128)(2,1)S(1)}, u32[]{:S(2)}, u32[]{:S(2)}) collective-permute-start(bf16[40,512]{1,0:T(8,128)(2,1)S(1)} %get-tuple-element.16), channel_id=1, source_target_pairs={{0,48},{16,0},{32,16},{48,32},{1,49},{17,1},{33,17},{49,33},{2,50}... | collective-permute-start | bytes 122888 | tf_op jit(solution)/shard_map/ppermute | solution.py:166
  67.4 1.8 %collective-permute-done.rest_1_ = bf16[40,512]{1,0:T(8,128)(2,1)S(1)} collective-permute-done((bf16[40,512]{1,0:T(8,128)(2,1)S(1)}, bf16[40,512]{1,0:T(8,128)(2,1)S(1)}, u32[]{:S(2)}, u32[]{:S(2)}) %collective-permute-start) | collective-permute-done | bytes 40992 | tf_op jit(solution)/shard_map/ppermute | solution.py:166
  69.2 2.1 %collective-permute-done.1.rest_2_ = bf16[40,512]{1,0:T(8,128)(2,1)S(1)} collective-permute-done((bf16[40,512]{1,0:T(8,128)(2,1)S(1)}, bf16[40,512]{1,0:T(8,128)(2,1)S(1)}, u32[]{:S(2)}, u32[]{:S(2)}) %collective-permute-start.1) | collective-permute-done | bytes 40992 | tf_op jit(solution)/shard_map/ppermute | solution.py:166
  71.2 0.0 collective-permute-done.2.rest_3_
  71.2 1.0 %all-to-all-done.2.in_ref = bf16[16,8,512]{2,1,0:T(8,128)(2,1)S(1)} async-done(((bf16[16,8,512]{2,1,0:T(8,128)(2,1)}), bf16[16,8,512]{2,1,0:T(8,128)(2,1)S(1)}, u32[]{:S(2)}, u32[]{:S(2)}) %all-to-all-start.2) | async-done | bytes 131104 | tf_op jit(solution)/shard_map/all_to_all | solution.py:214
  72.2 1.5 %turn.1 = (bf16[16,32,512]{2,1,0:T(8,128)(2,1)}, bf16[136,512]{1,0:T(8,128)(2,1)S(1)}, bf16[136,512]{1,0:T(8,128)(2,1)S(1)}, bf16[136,512]{1,0:T(8,128)(2,1)S(1)}, bf16[136,512]{1,0:T(8,128)(2,1)S(1)}) custom-call(s32[4]{0:T(128)S(1)} %pad_add_fusion.where_ref, bf16[16,8,512]{2,1,0:T(8,128)(2,1)S(1)} %all-to-all-done.2.in_ref, ...), custom_call_target="tpu_custom_call" | custom-call | tf_op jit(solution)/shard_map/turn/pallas_call | solution.py:215
  73.8 3.6 %all-to-all-start.3 = ((bf16[16,32,512]{2,1,0:T(8,128)(2,1)}), bf16[16,32,512]{2,1,0:T(8,128)(2,1)S(1)}, u32[]{:S(2)}, u32[]{:S(2)}) async-start(bf16[16,32,512]{2,1,0:T(8,128)(2,1)} %get-tuple-element.17), calls=%async_computation.3 | async-start | bytes 1048576 | tf_op jit(solution)/shard_map/all_to_all | solution.py:225
  77.3 1.3 %collective-permute-start.3 = (bf16[136,512]{1,0:T(8,128)(2,1)S(1)}, bf16[136,512]{1,0:T(8,128)(2,1)S(1)}, u32[]{:S(2)}, u32[]{:S(2)}) collective-permute-start(bf16[136,512]{1,0:T(8,128)(2,1)S(1)} %get-tuple-element.19), channel_id=1, source_target_pairs={{0,64},{64,128},{128,192},{192,0},{1,65},{65,129},{129,193},{193,1... | collective-permute-start | bytes 417800 | tf_op jit(solution)/shard_map/ppermute | solution.py:166
  78.6 2.4 %collective-permute-start.4 = (bf16[136,512]{1,0:T(8,128)(2,1)S(1)}, bf16[136,512]{1,0:T(8,128)(2,1)S(1)}, u32[]{:S(2)}, u32[]{:S(2)}) collective-permute-start(bf16[136,512]{1,0:T(8,128)(2,1)S(1)} %get-tuple-element.20), channel_id=1, source_target_pairs={{0,128},{64,192},{128,0},{192,64},{1,129},{65,193},{129,1},{193,65... | collective-permute-start | bytes 417800 | tf_op jit(solution)/shard_map/ppermute | solution.py:166
  81.0 1.2 %collective-permute-start.5 = (bf16[136,512]{1,0:T(8,128)(2,1)S(1)}, bf16[136,512]{1,0:T(8,128)(2,1)S(1)}, u32[]{:S(2)}, u32[]{:S(2)}) collective-permute-start(bf16[136,512]{1,0:T(8,128)(2,1)S(1)} %get-tuple-element.21), channel_id=1, source_target_pairs={{0,192},{64,0},{128,64},{192,128},{1,193},{65,1},{129,65},{193,129... | collective-permute-start | bytes 417800 | tf_op jit(solution)/shard_map/ppermute | solution.py:166
  82.2 7.5 %collective-permute-done.3.refs_1_ = bf16[136,512]{1,0:T(8,128)(2,1)S(1)} collective-permute-done((bf16[136,512]{1,0:T(8,128)(2,1)S(1)}, bf16[136,512]{1,0:T(8,128)(2,1)S(1)}, u32[]{:S(2)}, u32[]{:S(2)}) %collective-permute-start.3) | collective-permute-done | bytes 139296 | tf_op jit(solution)/shard_map/ppermute | solution.py:166
  89.7 3.2 %collective-permute-done.4.refs_2_ = bf16[136,512]{1,0:T(8,128)(2,1)S(1)} collective-permute-done((bf16[136,512]{1,0:T(8,128)(2,1)S(1)}, bf16[136,512]{1,0:T(8,128)(2,1)S(1)}, u32[]{:S(2)}, u32[]{:S(2)}) %collective-permute-start.4) | collective-permute-done | bytes 139296 | tf_op jit(solution)/shard_map/ppermute | solution.py:166
  93.0 0.0 collective-permute-done.5.refs_3_
  93.0 1.8 %weight.1 = f32[4,2,32,512]{3,2,1,0:T(8,128)} custom-call(s32[4]{0:T(128)S(1)} %pad_add_fusion.where_ref, bf16[136,512]{1,0:T(8,128)(2,1)S(1)} %get-tuple-element.18.refs_0_, bf16[136,512]{1,0:T(8,128)(2,1)S(1)} %collective-permute-done.3.refs_1_, bf16[136,512]{1,0:T(8,128)(2,1)S(1)} %collective-permute-done.4.refs_2_, ...), custom_call_target="tpu_custom_call" | custom-call | flops 67108864 | bytes 1048576 | tf_op jit(solution)/shard_map/weight/pallas_call | solution.py:226
  94.8 0.0 all-to-all-done.3.in_ref
  94.8 2.4 %field.1 = bf16[4,512,512]{2,1,0:T(8,128)(2,1)} custom-call(bf16[16,32,512]{2,1,0:T(8,128)(2,1)S(1)} %all-to-all-done.3.in_ref, bf16[512,128]{1,0:T(8,128)(2,1)S(1)} %bitcast.8), custom_call_target="tpu_custom_call" | custom-call | tf_op jit(solution)/shard_map/field/pallas_call | solution.py:237
  (1 shorter events, 0.0 us)
Async XLA Ops:
  35.3 22.2 %all-to-all-start.1 = ((bf16[16,16,512]{2,1,0:T(8,128)(2,1)}), bf16[16,16,512]{2,1,0:T(8,128)(2,1)S(1)}, u32[]{:S(2)}, u32[]{:S(2)}) async-start(bf16[16,16,512]{2,1,0:T(8,128)(2,1)} %sum_y.1), calls=%async_computation.1 | async-start | bytes 524288 | tf_op jit(solution)/shard_map/all_to_all | solution.py:202
  59.2 13.1 %all-to-all-start.2 = ((bf16[16,8,512]{2,1,0:T(8,128)(2,1)}), bf16[16,8,512]{2,1,0:T(8,128)(2,1)S(1)}, u32[]{:S(2)}, u32[]{:S(2)}) async-start(bf16[16,8,512]{2,1,0:T(8,128)(2,1)} %get-tuple-element.12), calls=%async_computation.2 | async-start | bytes 262144 | tf_op jit(solution)/shard_map/all_to_all | solution.py:214
  62.7 6.5 %collective-permute-start = (bf16[40,512]{1,0:T(8,128)(2,1)S(1)}, bf16[40,512]{1,0:T(8,128)(2,1)S(1)}, u32[]{:S(2)}, u32[]{:S(2)}) collective-permute-start(bf16[40,512]{1,0:T(8,128)(2,1)S(1)} %get-tuple-element.14), channel_id=1, source_target_pairs={{0,16},{16,32},{32,48},{48,0},{1,17},{17,33},{33,49},{49,1},{2,18}... | collective-permute-start | bytes 122888 | tf_op jit(solution)/shard_map/ppermute | solution.py:166
  64.1 7.2 %collective-permute-start.1 = (bf16[40,512]{1,0:T(8,128)(2,1)S(1)}, bf16[40,512]{1,0:T(8,128)(2,1)S(1)}, u32[]{:S(2)}, u32[]{:S(2)}) collective-permute-start(bf16[40,512]{1,0:T(8,128)(2,1)S(1)} %get-tuple-element.15), channel_id=1, source_target_pairs={{0,32},{16,48},{32,0},{48,16},{1,33},{17,49},{33,1},{49,17},{2,34}... | collective-permute-start | bytes 122888 | tf_op jit(solution)/shard_map/ppermute | solution.py:166
  66.2 5.0 %collective-permute-start.2 = (bf16[40,512]{1,0:T(8,128)(2,1)S(1)}, bf16[40,512]{1,0:T(8,128)(2,1)S(1)}, u32[]{:S(2)}, u32[]{:S(2)}) collective-permute-start(bf16[40,512]{1,0:T(8,128)(2,1)S(1)} %get-tuple-element.16), channel_id=1, source_target_pairs={{0,48},{16,0},{32,16},{48,32},{1,49},{17,1},{33,17},{49,33},{2,50}... | collective-permute-start | bytes 122888 | tf_op jit(solution)/shard_map/ppermute | solution.py:166
  73.8 21.1 %all-to-all-start.3 = ((bf16[16,32,512]{2,1,0:T(8,128)(2,1)}), bf16[16,32,512]{2,1,0:T(8,128)(2,1)S(1)}, u32[]{:S(2)}, u32[]{:S(2)}) async-start(bf16[16,32,512]{2,1,0:T(8,128)(2,1)} %get-tuple-element.17), calls=%async_computation.3 | async-start | bytes 1048576 | tf_op jit(solution)/shard_map/all_to_all | solution.py:225
  77.3 12.4 %collective-permute-start.3 = (bf16[136,512]{1,0:T(8,128)(2,1)S(1)}, bf16[136,512]{1,0:T(8,128)(2,1)S(1)}, u32[]{:S(2)}, u32[]{:S(2)}) collective-permute-start(bf16[136,512]{1,0:T(8,128)(2,1)S(1)} %get-tuple-element.19), channel_id=1, source_target_pairs={{0,64},{64,128},{128,192},{192,0},{1,65},{65,129},{129,193},{193,1... | collective-permute-start | bytes 417800 | tf_op jit(solution)/shard_map/ppermute | solution.py:166
  78.6 14.4 %collective-permute-start.4 = (bf16[136,512]{1,0:T(8,128)(2,1)S(1)}, bf16[136,512]{1,0:T(8,128)(2,1)S(1)}, u32[]{:S(2)}, u32[]{:S(2)}) collective-permute-start(bf16[136,512]{1,0:T(8,128)(2,1)S(1)} %get-tuple-element.20), channel_id=1, source_target_pairs={{0,128},{64,192},{128,0},{192,64},{1,129},{65,193},{129,1},{193,65... | collective-permute-start | bytes 417800 | tf_op jit(solution)/shard_map/ppermute | solution.py:166
  81.0 11.9 %collective-permute-start.5 = (bf16[136,512]{1,0:T(8,128)(2,1)S(1)}, bf16[136,512]{1,0:T(8,128)(2,1)S(1)}, u32[]{:S(2)}, u32[]{:S(2)}) collective-permute-start(bf16[136,512]{1,0:T(8,128)(2,1)S(1)} %get-tuple-element.21), channel_id=1, source_target_pairs={{0,192},{64,0},{128,64},{192,128},{1,193},{65,1},{129,65},{193,129... | collective-permute-start | bytes 417800 | tf_op jit(solution)/shard_map/ppermute | solution.py:166

commit v3 on v2

v3 whole, which is shorter than its diff:
```python
import functools
import math

import jax
import jax.numpy as jnp
from jax import lax
from jax.experimental import pallas as pl
from jax.experimental.pallas import tpu as pltpu
from jax.sharding import Mesh
from jax.sharding import PartitionSpec as P

F32, BF16 = jnp.float32, jnp.bfloat16
FIRST = ("y", "x")
SECOND = ("zl", "w")
SPECTRA_VMEM = 60 * 2**20
NT = (((1,), (1,)), ((), ()))
TN = (((0,), (0,)), ((), ()))


def table_of(points, rows_are_points, offset):
    shape = (points, 128) if rows_are_points else (128, points)
    point = lax.broadcasted_iota(jnp.int32, shape, 0 if rows_are_points else 1) + offset
    row = lax.broadcasted_iota(jnp.int32, shape, 1 if rows_are_points else 0)
    phase = ((row & 63) * point + ((row >> 6) << 11)) & 8191
    quadrant = (phase + 1024) >> 11
    angle = (phase - (quadrant << 11)).astype(F32) * (2.0 * math.pi / 8192.0)
    square = angle * angle
    sine = 1.0 / 362880.0
    for c in (-1.0 / 5040.0, 1.0 / 120.0, -1.0 / 6.0, 1.0):
        sine = sine * square + c
    sine = sine * angle
    cosine = -1.0 / 3628800.0
    for c in (1.0 / 40320.0, -1.0 / 720.0, 1.0 / 24.0, -0.5, 1.0):
        cosine = cosine * square + c
    value = jnp.where((quadrant & 1) == 0, cosine, sine)
    negative = ((quadrant + 1) & 2) != 0
    return jnp.where(negative, -value, value).astype(BF16)


def gelu_slope(values):
    normal_cdf = 0.5 * (1.0 + lax.erf(values * (1.0 / math.sqrt(2.0))))
    density = jnp.exp(-0.5 * values * values) * (1.0 / math.sqrt(2.0 * math.pi))
    return normal_cdf + values * density


def dot(a, b, dims=None):
    if dims is None:
        return jnp.dot(a, b, preferred_element_type=F32)
    return lax.dot_general(a, b, dims, preferred_element_type=F32)


def row_moves(n, digits):
    row = lax.broadcasted_iota(jnp.int32, (n, n), 0)
    col = lax.broadcasted_iota(jnp.int32, (n, n), 1)
    source = jnp.zeros((n, n), jnp.int32)
    for out_stride, size, in_stride in digits:
        digit = (row >> (out_stride.bit_length() - 1)) & (size - 1)
        source = source + (digit << (in_stride.bit_length() - 1))
    return jnp.where(source == col, 1.0, 0.0).astype(BF16)


def turned(n):
    row = lax.broadcasted_iota(jnp.int32, (n, n), 0)
    col = lax.broadcasted_iota(jnp.int32, (n, n), 1)
    sign = jnp.where((row & 4) == 0, 1.0, -1.0)
    return jnp.where((row ^ 4) == col, sign, 0.0).astype(BF16)


def gather_lanes(values, quarter):
    lane = lax.broadcasted_iota(jnp.int32, (values.shape[0], 128), 1) >> 5
    out = None
    for j in range(4):
        block = values[:, 128 * j : 128 * j + 128]
        shift = (32 * (j - quarter)) % 128
        if shift:
            block = pltpu.roll(block, shift, 1)
        out = block if out is None else jnp.where(lane == j, block, out)
    return out


def spectra_kernel(fields_hbm, pre_hbm, cot_hbm, out_hbm, fields, pre, cot, out_ref, table, sems, out_sems):
    def copies(b):
        return [
            pltpu.make_async_copy(hbm.at[b], vmem.at[b], sems.at[i, b])
            for i, (hbm, vmem) in enumerate(((pre_hbm, pre), (cot_hbm, cot), (fields_hbm, fields)))
        ]

    def copy_out(b):
        rows = pl.ds(4 * b, 4)
        return pltpu.make_async_copy(out_ref.at[rows], out_hbm.at[rows], out_sems.at[b])

    for b in range(4):
        for copy in copies(b):
            copy.start()
    points = table.shape[1]
    table[...] = table_of(points, False, (lax.axis_index("y") * 4 + lax.axis_index("zl")) * points)

    def one(b, _):
        for copy in copies(b):
            copy.wait()
        for h in range(2):
            lanes = slice(256 * h, 256 * h + 256)
            slopes = cot[b, :, lanes].astype(F32) * gelu_slope(pre[b, :, lanes].astype(F32))
            spec_g = dot(table[...], slopes.astype(BF16)).astype(BF16)
            spec_u = dot(table[...], fields[b, :, lanes]).astype(BF16)
            for j in range(4):
                for p in range(2):
                    rows = slice(64 * p + 16 * j, 64 * p + 16 * j + 16)
                    out_ref[4 * b + j, 16 * p : 16 * p + 16, lanes] = spec_g[rows]
                    out_ref[4 * b + j, 32 + 16 * p : 48 + 16 * p, lanes] = spec_u[rows]
        copy_out(b).start()
        return 0

    lax.fori_loop(0, 4, one, 0)
    for b in range(4):
        copy_out(b).wait()


def sum_y_kernel(in_ref, out_ref):
    total = in_ref[0:4].astype(F32)
    for y in range(1, 4):
        total = total + in_ref[4 * y : 4 * y + 4].astype(F32)
    low = total.astype(BF16)
    moves = row_moves(128, [(32, 4, 1), (8, 4, 4), (4, 2, 16), (1, 4, 32)])
    g = dot(moves, low[:, :32].reshape(128, 512))
    u = dot(moves, low[:, 32:].reshape(128, 512))
    for i in range(16):
        both = jnp.concatenate([g[8 * i : 8 * i + 8], u[8 * i : 8 * i + 8]], axis=0)
        out_ref[i] = both.astype(BF16)


def modes_kernel(factor, in_ref, w_ref, out_ref, *rest):
    side_refs, chunks = rest[:4], rest[4]
    x, w_mine, zl_mine, y_mine = (lax.axis_index(name) for name in ("x", "w", "zl", "y"))
    total = in_ref[0:4].astype(F32)
    for zl in range(1, 4):
        total = total + in_ref[4 * zl : 4 * zl + 4].astype(F32)
    first_mode = (x == 0) & (w_mine == 0) & (zl_mine == 0)
    g = total[:, :8].reshape(32, 512) * jnp.where(first_mode, factor, 2.0 * factor)
    u = total[:, 8:].reshape(32, 512) * factor
    g_low = g.astype(BF16)
    g_turned = dot(turned(32), g_low).astype(BF16)
    grad = dot(g_low, w_ref[0], NT) + dot(g_turned, w_ref[1], NT)
    for w in range(4):
        part = grad[8 * w : 8 * w + 8].astype(BF16)
        for zl in range(4):
            out_ref[4 * zl + w] = part
    for y in range(4):
        lanes = slice(128 * y, 128 * y + 128)
        chunks[y] = jnp.concatenate([g[8 * w : 8 * w + 8, lanes] for w in range(4)], axis=1)
    for t in range(4):
        chunk = chunks[(y_mine + t) & 3]
        side_refs[t][...] = jnp.concatenate([u, chunk], axis=0).astype(BF16)


def turn_kernel(in_ref, *rest):
    side_refs, out_ref, send_refs, chunks = rest[:4], rest[4], rest[5:9], rest[9]
    grad = in_ref[...].astype(F32).reshape(128, 512).astype(BF16)
    grad = dot(row_moves(128, [(32, 4, 1), (16, 2, 4), (4, 4, 8), (1, 4, 32)]), grad)
    for x in range(4):
        part = grad[32 * x : 32 * x + 32].astype(BF16)
        for y in range(4):
            out_ref[4 * y + x] = part
    mine = [ref[32:40, :].astype(F32) for ref in side_refs]
    for zl in range(4):
        chunks[zl] = jnp.concatenate([gather_lanes(m, zl) for m in mine], axis=1)
    for t in range(4):
        for q in range(4):
            send_refs[t][32 * q : 32 * q + 32, :] = side_refs[q][0:32, :]
        send_refs[t][128:136, :] = chunks[(lax.axis_index("zl") + t) & 3].astype(BF16)


def weight_kernel(done_ref, *refs):
    in_refs, weight_ref = refs[:4], refs[4]
    g = jnp.concatenate([ref[128:136, :].astype(F32) for ref in in_refs], axis=0)
    g_turned = dot(turned(32), g.astype(BF16))
    lane = lax.broadcasted_iota(jnp.int32, (32, 128), 1)
    left = []
    for q in range(4):
        one, two = (v[:, 128 * q : 128 * q + 128] for v in (g, g_turned))
        for w in range(4):
            a = pltpu.roll(one, (128 - 32 * w) % 128, 1) if w else one
            b = pltpu.roll(two, (160 - 32 * w) % 128, 1) if w != 1 else two
            left.append(jnp.where(lane < 32, a, b))
    for t in range(4):
        mine = jnp.concatenate([rows[8 * t : 8 * t + 8] for rows in left], axis=0)
        grad = dot(mine.astype(BF16), in_refs[t][0:128, :], TN)
        ki = (lax.axis_index("zl") - t) & 3
        weight_ref[ki, 0] = grad[0:32]
        weight_ref[ki, 1] = grad[32:64]


def field_kernel(factor, in_ref, field_ref, done_ref, table):
    @pl.when(pl.program_id(0) == 0)
    def _():
        done_ref[...] = jnp.zeros_like(done_ref)
        points = table.shape[0]
        offset = (lax.axis_index("y") * 4 + lax.axis_index("zl")) * points
        table[...] = table_of(points, True, offset)

    modes = jnp.concatenate(
        [in_ref[j, 16 * p : 16 * p + 16, :] for p in range(2) for j in range(4)], axis=0
    )
    field_ref[0] = (dot(table[...], modes) * factor).astype(BF16)


def shifted(value, axis, distance):
    return lax.ppermute(value, axis, [(i, (i + distance) % 4) for i in range(4)])


def shards(fields, pre_act, cotangent, weights):
    total = fields.shape[1] * lax.axis_size("y") * lax.axis_size("zl")
    factor = float(total) ** (-0.5)
    vmem = pl.BlockSpec(memory_space=pltpu.VMEM)
    hbm = pl.BlockSpec(memory_space=pltpu.HBM)
    params = pltpu.CompilerParams(vmem_limit_bytes=40 * 2**20)

    def block(*shape):
        return jax.ShapeDtypeStruct(shape, BF16)

    send = pl.pallas_call(
        spectra_kernel,
        in_specs=[hbm] * 3,
        out_specs=hbm,
        out_shape=block(16, 64, 512),
        scratch_shapes=[pltpu.VMEM((4, 512, 512), BF16)] * 3
        + [pltpu.VMEM((16, 64, 512), BF16), pltpu.VMEM((128, 512), BF16)]
        + [pltpu.SemaphoreType.DMA((3, 4)), pltpu.SemaphoreType.DMA((4,))],
        compiler_params=pltpu.CompilerParams(vmem_limit_bytes=SPECTRA_VMEM),
        name="spectra",
    )(fields, pre_act, cotangent)
    got = lax.all_to_all(send, FIRST, 0, 0, tiled=True)
    send = pl.pallas_call(
        sum_y_kernel,
        in_specs=[vmem],
        out_specs=vmem,
        out_shape=block(16, 16, 512),
        compiler_params=params,
        name="sum_y",
    )(got)
    got = lax.all_to_all(send, SECOND, 0, 0, tiled=True)
    mine = lax.dynamic_index_in_dim(weights, lax.axis_index("zl"), 0, keepdims=False)
    send, *sides = pl.pallas_call(
        functools.partial(modes_kernel, factor),
        in_specs=[vmem, vmem],
        out_specs=[vmem] * 5,
        out_shape=[block(16, 8, 512)] + [block(40, 512)] * 4,
        scratch_shapes=[pltpu.VMEM((4, 8, 512), F32)],
        compiler_params=params,
        name="modes",
    )(got, mine)
    sides = [sides[0]] + [shifted(sides[t], "y", t) for t in range(1, 4)]
    got = lax.all_to_all(send, SECOND, 0, 0, tiled=True)
    send, *sides = pl.pallas_call(
        turn_kernel,
        in_specs=[vmem] * 5,
        out_specs=[vmem] * 5,
        out_shape=[block(16, 32, 512)] + [block(136, 512)] * 4,
        scratch_shapes=[pltpu.VMEM((4, 8, 512), F32)],
        compiler_params=params,
        name="turn",
    )(got, *sides)
    sides = [sides[0]] + [shifted(sides[t], "zl", t) for t in range(1, 4)]
    got = lax.all_to_all(send, FIRST, 0, 0, tiled=True)
    field_grad, done = pl.pallas_call(
        functools.partial(field_kernel, factor),
        grid=(4,),
        in_specs=[pl.BlockSpec((4, 32, 512), lambda b: (b, 0, 0))],
        out_specs=[
            pl.BlockSpec((1, 512, 512), lambda b: (b, 0, 0)),
            pl.BlockSpec((8, 128), lambda b: (0, 0)),
        ],
        out_shape=[block(4, 512, 512), jax.ShapeDtypeStruct((8, 128), F32)],
        scratch_shapes=[pltpu.VMEM((512, 128), BF16)],
        compiler_params=params,
        name="field",
    )(got)
    weight_grad = pl.pallas_call(
        weight_kernel,
        in_specs=[vmem] * 5,
        out_specs=vmem,
        out_shape=jax.ShapeDtypeStruct((4, 2, 32, 512), F32),
        compiler_params=params,
        name="weight",
    )(done, *sides)
    return field_grad, jnp.swapaxes(weight_grad, 2, 3)


def solution(mesh):
    grid = Mesh(mesh.devices.reshape(4, 4, 4, 4), ("y", "zl", "x", "w"))
    space, mode = ("y", "zl"), ("x", "w")
    whole = P(mode, space, None)
    return jax.shard_map(
        shards,
        mesh=grid,
        in_specs=(whole, whole, whole, P(mode, None, None, None)),
        out_specs=(whole, P(mode, None, None, space)),
        check_vma=False,
    )
```

time: 97.9 us -> 87 us (0.89)
  Pallas kernels: 16.3 us -> 12.1 us
  starting transfers between devices: 27.1 us -> 23.6 us
  other arithmetic: 1.26 us -> 0 us
    ppermute x6, waiting for transfers between devices: 14.6 us -> 2.7 us  [shifted(): lax.ppermute(value, axis, [(i, (i + distance) % 4) for i in range(4)])]
    all_to_all x1, waiting for transfers between devices: 0.01 us -> 8.41 us  [shards(): got = lax.all_to_all(send, FIRST, 0, 0, tiled=True)]
    pallas_call x4, Pallas kernels: 12.9 us -> 8.3 us  [the longest x1 4.9 us: shards(): pl.pallas_call(spectra_kernel, in_specs=[hbm] * 3, out_specs=hbm, out_sha...]
    ppermute x6, starting transfers between devices: 9.57 us -> 6.07 us  [shifted(): lax.ppermute(value, axis, [(i, (i + distance) % 4) for i in range(4)])]
    all_to_all x2, waiting for transfers between devices: 11.3 us -> 14 us  [shards(): got = lax.all_to_all(send, SECOND, 0, 0, tiled=True)]
    another operation x2 -> x0, other arithmetic: 1.08 us -> none
  transfers between devices with their start and end apart: 9 -> 9, of which waited for: 6 -> 6; matrix products, arithmetic and copies ran while one was open for 1% -> 1% of each run, Pallas kernels for 2% -> 3%
where the time goes in v3:
time: 87 us; the launch traced here: 86.5 us
  waiting for transfers between devices  25.1 us (29%)
  blocking collectives  23.7 us (27%)
  starting transfers between devices  23.6 us (27%)
  Pallas kernels  12.1 us (14%)
  local copies, waits for them, and re-layouts  1.29 us (1%)
    all_to_all x1, blocking collectives, shards(): got = lax.all_to_all(send, FIRST, 0, 0, tiled=True)  23.7 us
    all_to_all x2, waiting for transfers between devices, shards(): got = lax.all_to_all(send, SECOND, 0, 0, tiled=True)  14 us
    all_to_all x2, starting transfers between devices, shards(): got = lax.all_to_all(send, SECOND, 0, 0, tiled=True)  14 us
    all_to_all x1, waiting for transfers between devices, shards(): got = lax.all_to_all(send, FIRST, 0, 0, tiled=True)  8.41 us
    ppermute x6, starting transfers between devices, shifted(): lax.ppermute(value, axis, [(i, (i + distance) % 4) for i in range(4)])  6.07 us
    pallas_call x1, Pallas kernels, shards(): pl.pallas_call(spectra_kernel, in_specs=[hbm] * 3, out_specs=hbm, out_sha...  4.9 us
    all_to_all x1, starting transfers between devices, shards(): got = lax.all_to_all(send, FIRST, 0, 0, tiled=True)  3.57 us
    pallas_call x1, Pallas kernels, shards(): pl.pallas_call(functools.partial(field_kernel, factor), grid=(4,), in_spe...  2.79 us
  transfers between devices with their start and end apart: 9, of which 6 were waited for; matrix products, arithmetic and copies ran while one was open for 1% of the time, Pallas kernels for 3%

profile of v3, /device:TPU:1, one launch (start us, length us, event | category | flops | bytes accessed | tf_op | source)
XLA Modules:
  0.0 86.5 jit_solution(7278715199615571412)
XLA Ops:
  0.6 4.9 %spectra.1 = bf16[16,64,512]{2,1,0:T(8,128)(2,1)} custom-call(bf16[4,512,512]{2,1,0:T(8,128)(2,1)} %fields_hbm.1, bf16[4,512,512]{2,1,0:T(8,128)(2,1)} %pre_hbm.1, bf16[4,512,512]{2,1,0:T(8,128)(2,1)} %cot_hbm.1), custom_call_target="tpu_custom_call" | custom-call | tf_op jit(solution)/shard_map/spectra/pallas_call | solution.py:221
  5.5 23.7 %all_to_all.20.in_ref = bf16[16,64,512]{2,1,0:T(8,128)(2,1)S(1)} all-to-all(bf16[16,64,512]{2,1,0:T(8,128)(2,1)} %spectra.1), channel_id=1, replica_groups=mesh['y'=4,'zl'=4,'x'=4,'w'=4] {'y','x'}, dimensions={0} | all-to-all | bytes 2097152 | tf_op jit(solution)/shard_map/all_to_all | solution.py:232
  29.3 1.0 %sum_y.1 = bf16[16,16,512]{2,1,0:T(8,128)(2,1)} custom-call(bf16[16,64,512]{2,1,0:T(8,128)(2,1)S(1)} %all_to_all.20.in_ref), custom_call_target="tpu_custom_call" | custom-call | tf_op jit(solution)/shard_map/sum_y/pallas_call | solution.py:233
  30.3 10.5 %all-to-all-start.1 = ((bf16[16,16,512]{2,1,0:T(8,128)(2,1)}), bf16[16,16,512]{2,1,0:T(8,128)(2,1)S(1)}, u32[]{:S(2)}, u32[]{:S(2)}) async-start(bf16[16,16,512]{2,1,0:T(8,128)(2,1)} %sum_y.1), calls=%async_computation.1 | async-start | bytes 524288 | tf_op jit(solution)/shard_map/all_to_all | solution.py:241
  40.7 1.3 %dynamic-slice_bitcast_fusion.w_ref = bf16[2,512,512]{2,1,0:T(8,128)(2,1)S(1)} fusion(bf16[4,2,512,512]{3,2,1,0:T(8,128)(2,1)} %param.7, s32[]{:T(128)S(6)} %select_n.4), kind=kLoop, calls=%fused_computation | loop fusion | bytes 2097156 | tf_op jit(solution)/shard_map/jit(dynamic_index_in_dim)/squeeze | solution.py:242
  42.0 10.4 %all-to-all-done.1.in_ref = bf16[16,16,512]{2,1,0:T(8,128)(2,1)S(1)} async-done(((bf16[16,16,512]{2,1,0:T(8,128)(2,1)}), bf16[16,16,512]{2,1,0:T(8,128)(2,1)S(1)}, u32[]{:S(2)}, u32[]{:S(2)}) %all-to-all-start.1) | async-done | bytes 262176 | tf_op jit(solution)/shard_map/all_to_all | solution.py:241
  52.4 1.1 %modes.1 = (bf16[16,8,512]{2,1,0:T(8,128)(2,1)}, bf16[40,512]{1,0:T(8,128)(2,1)S(1)}, bf16[40,512]{1,0:T(8,128)(2,1)S(1)}, bf16[40,512]{1,0:T(8,128)(2,1)S(1)}, bf16[40,512]{1,0:T(8,128)(2,1)S(1)}) custom-call(bf16[16,16,512]{2,1,0:T(8,128)(2,1)S(1)} %all-to-all-done.1.in_ref, bf16[2,512,512]{2,1,0:T(8,128)(2,1)S(1)} %dynamic-slice_bitcast_fusion.w_ref), custom_call_target="tpu_custom_call" | custom-call | tf_op jit(solution)/shard_map/modes/pallas_call | solution.py:243
  53.6 3.5 %all-to-all-start.2 = ((bf16[16,8,512]{2,1,0:T(8,128)(2,1)}), bf16[16,8,512]{2,1,0:T(8,128)(2,1)S(1)}, u32[]{:S(2)}, u32[]{:S(2)}) async-start(bf16[16,8,512]{2,1,0:T(8,128)(2,1)} %get-tuple-element.14), calls=%async_computation.2 | async-start | bytes 262144 | tf_op jit(solution)/shard_map/all_to_all | solution.py:253
  57.1 0.1 collective-permute-start
  57.1 1.7 %collective-permute-start.1 = (bf16[40,512]{1,0:T(8,128)(2,1)S(1)}, bf16[40,512]{1,0:T(8,128)(2,1)S(1)}, u32[]{:S(2)}, u32[]{:S(2)}) collective-permute-start(bf16[40,512]{1,0:T(8,128)(2,1)S(1)} %get-tuple-element.17), channel_id=1, source_target_pairs={{0,128},{64,192},{128,0},{192,64},{1,129},{65,193},{129,1},{193,65... | collective-permute-start | bytes 122888 | tf_op jit(solution)/shard_map/ppermute | solution.py:208
  58.9 0.9 %collective-permute-start.2 = (bf16[40,512]{1,0:T(8,128)(2,1)S(1)}, bf16[40,512]{1,0:T(8,128)(2,1)S(1)}, u32[]{:S(2)}, u32[]{:S(2)}) collective-permute-start(bf16[40,512]{1,0:T(8,128)(2,1)S(1)} %get-tuple-element.18), channel_id=1, source_target_pairs={{0,192},{64,0},{128,64},{192,128},{1,193},{65,1},{129,65},{193,129... | collective-permute-start | bytes 122888 | tf_op jit(solution)/shard_map/ppermute | solution.py:208
  59.8 1.7 %collective-permute-done.rest_1_ = bf16[40,512]{1,0:T(8,128)(2,1)S(1)} collective-permute-done((bf16[40,512]{1,0:T(8,128)(2,1)S(1)}, bf16[40,512]{1,0:T(8,128)(2,1)S(1)}, u32[]{:S(2)}, u32[]{:S(2)}) %collective-permute-start) | collective-permute-done | bytes 40992 | tf_op jit(solution)/shard_map/ppermute | solution.py:208
  61.5 0.2 collective-permute-done.1.rest_2_
  61.6 0.9 collective-permute-done.2.rest_3_
  62.5 3.6 %all-to-all-done.2.in_ref = bf16[16,8,512]{2,1,0:T(8,128)(2,1)S(1)} async-done(((bf16[16,8,512]{2,1,0:T(8,128)(2,1)}), bf16[16,8,512]{2,1,0:T(8,128)(2,1)S(1)}, u32[]{:S(2)}, u32[]{:S(2)}) %all-to-all-start.2) | async-done | bytes 131104 | tf_op jit(solution)/shard_map/all_to_all | solution.py:253
  66.1 1.0 %turn.1 = (bf16[16,32,512]{2,1,0:T(8,128)(2,1)}, bf16[136,512]{1,0:T(8,128)(2,1)S(1)}, bf16[136,512]{1,0:T(8,128)(2,1)S(1)}, bf16[136,512]{1,0:T(8,128)(2,1)S(1)}, bf16[136,512]{1,0:T(8,128)(2,1)S(1)}) custom-call(bf16[16,8,512]{2,1,0:T(8,128)(2,1)S(1)} %all-to-all-done.2.in_ref, bf16[40,512]{1,0:T(8,128)(2,1)S(1)} %get-tuple-element.15.rest_0_, ...), custom_call_target="tpu_custom_call" | custom-call | tf_op jit(solution)/shard_map/turn/pallas_call | solution.py:254
  67.1 3.6 %all-to-all-start.3 = ((bf16[16,32,512]{2,1,0:T(8,128)(2,1)}), bf16[16,32,512]{2,1,0:T(8,128)(2,1)S(1)}, u32[]{:S(2)}, u32[]{:S(2)}) async-start(bf16[16,32,512]{2,1,0:T(8,128)(2,1)} %get-tuple-element.19), calls=%async_computation.3 | async-start | bytes 1048576 | tf_op jit(solution)/shard_map/all_to_all | solution.py:264
  70.6 0.6 collective-permute-start.3
  71.2 0.2 collective-permute-start.4
  71.4 2.5 %collective-permute-start.5 = (bf16[136,512]{1,0:T(8,128)(2,1)S(1)}, bf16[136,512]{1,0:T(8,128)(2,1)S(1)}, u32[]{:S(2)}, u32[]{:S(2)}) collective-permute-start(bf16[136,512]{1,0:T(8,128)(2,1)S(1)} %get-tuple-element.25), channel_id=1, source_target_pairs={{0,48},{16,0},{32,16},{48,32},{1,49},{17,1},{33,17},{49,33},{2,50}... | collective-permute-start | bytes 417800 | tf_op jit(solution)/shard_map/ppermute | solution.py:208
  74.0 8.4 %all-to-all-done.3.in_ref = bf16[16,32,512]{2,1,0:T(8,128)(2,1)S(1)} async-done(((bf16[16,32,512]{2,1,0:T(8,128)(2,1)}), bf16[16,32,512]{2,1,0:T(8,128)(2,1)S(1)}, u32[]{:S(2)}, u32[]{:S(2)}) %all-to-all-start.3) | async-done | bytes 524320 | tf_op jit(solution)/shard_map/all_to_all | solution.py:264
  82.4 2.8 %field.1 = (bf16[4,512,512]{2,1,0:T(8,128)(2,1)}, f32[8,128]{1,0:T(8,128)S(1)}) custom-call(bf16[16,32,512]{2,1,0:T(8,128)(2,1)S(1)} %all-to-all-done.3.in_ref), custom_call_target="tpu_custom_call" | custom-call | tf_op jit(solution)/shard_map/field/pallas_call | solution.py:265
  85.2 0.0 collective-permute-done.3.refs_1_
  85.2 0.0 collective-permute-done.4.refs_2_
  85.2 0.0 collective-permute-done.5.refs_3_
  85.2 1.3 %weight.1 = f32[4,2,32,512]{3,2,1,0:T(8,128)} custom-call(f32[8,128]{1,0:T(8,128)S(1)} %get-tuple-element.21.done_ref, bf16[136,512]{1,0:T(8,128)(2,1)S(1)} %get-tuple-element.22.refs_0_, bf16[136,512]{1,0:T(8,128)(2,1)S(1)} %collective-permute-done.3.refs_1_, bf16[136,512]{1,0:T(8,128)(2,1)S(1)} %collective-permute-done.4.refs_2_, ...), custom_call_target="tpu_custom_call" | custom-call | tf_op jit(solution)/shard_map/weight/pallas_call | solution.py:278
Async XLA Ops:
  30.3 22.2 %all-to-all-start.1 = ((bf16[16,16,512]{2,1,0:T(8,128)(2,1)}), bf16[16,16,512]{2,1,0:T(8,128)(2,1)S(1)}, u32[]{:S(2)}, u32[]{:S(2)}) async-start(bf16[16,16,512]{2,1,0:T(8,128)(2,1)} %sum_y.1), calls=%async_computation.1 | async-start | bytes 524288 | tf_op jit(solution)/shard_map/all_to_all | solution.py:241
  53.6 12.5 %all-to-all-start.2 = ((bf16[16,8,512]{2,1,0:T(8,128)(2,1)}), bf16[16,8,512]{2,1,0:T(8,128)(2,1)S(1)}, u32[]{:S(2)}, u32[]{:S(2)}) async-start(bf16[16,8,512]{2,1,0:T(8,128)(2,1)} %get-tuple-element.14), calls=%async_computation.2 | async-start | bytes 262144 | tf_op jit(solution)/shard_map/all_to_all | solution.py:253
  57.1 4.4 %collective-permute-start = (bf16[40,512]{1,0:T(8,128)(2,1)S(1)}, bf16[40,512]{1,0:T(8,128)(2,1)S(1)}, u32[]{:S(2)}, u32[]{:S(2)}) collective-permute-start(bf16[40,512]{1,0:T(8,128)(2,1)S(1)} %get-tuple-element.16), channel_id=1, source_target_pairs={{0,64},{64,128},{128,192},{192,0},{1,65},{65,129},{129,193},{193,1... | collective-permute-start | bytes 122888 | tf_op jit(solution)/shard_map/ppermute | solution.py:208
  57.1 4.5 %collective-permute-start.1 = (bf16[40,512]{1,0:T(8,128)(2,1)S(1)}, bf16[40,512]{1,0:T(8,128)(2,1)S(1)}, u32[]{:S(2)}, u32[]{:S(2)}) collective-permute-start(bf16[40,512]{1,0:T(8,128)(2,1)S(1)} %get-tuple-element.17), channel_id=1, source_target_pairs={{0,128},{64,192},{128,0},{192,64},{1,129},{65,193},{129,1},{193,65... | collective-permute-start | bytes 122888 | tf_op jit(solution)/shard_map/ppermute | solution.py:208
  58.9 3.6 %collective-permute-start.2 = (bf16[40,512]{1,0:T(8,128)(2,1)S(1)}, bf16[40,512]{1,0:T(8,128)(2,1)S(1)}, u32[]{:S(2)}, u32[]{:S(2)}) collective-permute-start(bf16[40,512]{1,0:T(8,128)(2,1)S(1)} %get-tuple-element.18), channel_id=1, source_target_pairs={{0,192},{64,0},{128,64},{192,128},{1,193},{65,1},{129,65},{193,129... | collective-permute-start | bytes 122888 | tf_op jit(solution)/shard_map/ppermute | solution.py:208
  67.1 15.3 %all-to-all-start.3 = ((bf16[16,32,512]{2,1,0:T(8,128)(2,1)}), bf16[16,32,512]{2,1,0:T(8,128)(2,1)S(1)}, u32[]{:S(2)}, u32[]{:S(2)}) async-start(bf16[16,32,512]{2,1,0:T(8,128)(2,1)} %get-tuple-element.19), calls=%async_computation.3 | async-start | bytes 1048576 | tf_op jit(solution)/shard_map/all_to_all | solution.py:264
  70.6 14.6 %collective-permute-start.3 = (bf16[136,512]{1,0:T(8,128)(2,1)S(1)}, bf16[136,512]{1,0:T(8,128)(2,1)S(1)}, u32[]{:S(2)}, u32[]{:S(2)}) collective-permute-start(bf16[136,512]{1,0:T(8,128)(2,1)S(1)} %get-tuple-element.23), channel_id=1, source_target_pairs={{0,16},{16,32},{32,48},{48,0},{1,17},{17,33},{33,49},{49,1},{2,18}... | collective-permute-start | bytes 417800 | tf_op jit(solution)/shard_map/ppermute | solution.py:208
  71.2 14.0 %collective-permute-start.4 = (bf16[136,512]{1,0:T(8,128)(2,1)S(1)}, bf16[136,512]{1,0:T(8,128)(2,1)S(1)}, u32[]{:S(2)}, u32[]{:S(2)}) collective-permute-start(bf16[136,512]{1,0:T(8,128)(2,1)S(1)} %get-tuple-element.24), channel_id=1, source_target_pairs={{0,32},{16,48},{32,0},{48,16},{1,33},{17,49},{33,1},{49,17},{2,34}... | collective-permute-start | bytes 417800 | tf_op jit(solution)/shard_map/ppermute | solution.py:208
  71.4 13.8 %collective-permute-start.5 = (bf16[136,512]{1,0:T(8,128)(2,1)S(1)}, bf16[136,512]{1,0:T(8,128)(2,1)S(1)}, u32[]{:S(2)}, u32[]{:S(2)}) collective-permute-start(bf16[136,512]{1,0:T(8,128)(2,1)S(1)} %get-tuple-element.25), channel_id=1, source_target_pairs={{0,48},{16,0},{32,16},{48,32},{1,49},{17,1},{33,17},{49,33},{2,50}... | collective-permute-start | bytes 417800 | tf_op jit(solution)/shard_map/ppermute | solution.py:208

commit v4 on v3

v4 whole, which is shorter than its diff:
```python
import functools
import math

import jax
import jax.numpy as jnp
from jax import lax
from jax.experimental import pallas as pl
from jax.experimental.pallas import tpu as pltpu
from jax.sharding import Mesh
from jax.sharding import PartitionSpec as P

F32, BF16 = jnp.float32, jnp.bfloat16
OTHERS = ("x", "w", "zl")
SPECTRA_VMEM = 60 * 2**20
NT = (((1,), (1,)), ((), ()))
TN = (((0,), (0,)), ((), ()))


def table_of(points, rows_are_points, offset):
    shape = (points, 128) if rows_are_points else (128, points)
    point = lax.broadcasted_iota(jnp.int32, shape, 0 if rows_are_points else 1) + offset
    row = lax.broadcasted_iota(jnp.int32, shape, 1 if rows_are_points else 0)
    phase = ((row & 63) * point + ((row >> 6) << 11)) & 8191
    quadrant = (phase + 1024) >> 11
    angle = (phase - (quadrant << 11)).astype(F32) * (2.0 * math.pi / 8192.0)
    square = angle * angle
    sine = 1.0 / 362880.0
    for c in (-1.0 / 5040.0, 1.0 / 120.0, -1.0 / 6.0, 1.0):
        sine = sine * square + c
    sine = sine * angle
    cosine = -1.0 / 3628800.0
    for c in (1.0 / 40320.0, -1.0 / 720.0, 1.0 / 24.0, -0.5, 1.0):
        cosine = cosine * square + c
    value = jnp.where((quadrant & 1) == 0, cosine, sine)
    negative = ((quadrant + 1) & 2) != 0
    return jnp.where(negative, -value, value).astype(BF16)


def gelu_slope(values):
    normal_cdf = 0.5 * (1.0 + lax.erf(values * (1.0 / math.sqrt(2.0))))
    density = jnp.exp(-0.5 * values * values) * (1.0 / math.sqrt(2.0 * math.pi))
    return normal_cdf + values * density


def dot(a, b, dims=None):
    if dims is None:
        return jnp.dot(a, b, preferred_element_type=F32)
    return lax.dot_general(a, b, dims, preferred_element_type=F32)


def row_moves(shape, digits, only=(), base=0):
    row = lax.broadcasted_iota(jnp.int32, shape, 0)
    col = lax.broadcasted_iota(jnp.int32, shape, 1)
    source = jnp.full(shape, base, jnp.int32)
    for out_stride, size, in_stride in digits:
        digit = (row >> (out_stride.bit_length() - 1)) & (size - 1)
        source = source + (digit << (in_stride.bit_length() - 1))
    for out_stride, size, wanted in only:
        digit = (row >> (out_stride.bit_length() - 1)) & (size - 1)
        source = jnp.where(digit == wanted, source, -1)
    return jnp.where(source == col, 1.0, 0.0).astype(BF16)


def turned(n):
    row = lax.broadcasted_iota(jnp.int32, (n, n), 0)
    col = lax.broadcasted_iota(jnp.int32, (n, n), 1)
    sign = jnp.where((row & 4) == 0, 1.0, -1.0)
    return jnp.where((row ^ 4) == col, sign, 0.0).astype(BF16)


def gather_lanes(values, quarter):
    lane = lax.broadcasted_iota(jnp.int32, (values.shape[0], 128), 1) >> 5
    out = None
    for j in range(4):
        block = values[:, 128 * j : 128 * j + 128]
        shift = (32 * (j - quarter)) % 128
        if shift:
            block = pltpu.roll(block, shift, 1)
        out = block if out is None else jnp.where(lane == j, block, out)
    return out


def spectra_kernel(steps, fields_hbm, pre_hbm, cot_hbm, _, *rest):
    out_refs, (fields, pre, cot, table, sems) = rest[: len(steps)], rest[len(steps) :]
    y = lax.axis_index("y")

    def copies(i):
        b = (y + steps[i]) & 3
        return [
            pltpu.make_async_copy(hbm.at[b], vmem.at[i], sems.at[n, i])
            for n, (hbm, vmem) in enumerate(((pre_hbm, pre), (cot_hbm, cot), (fields_hbm, fields)))
        ]

    for i in range(len(steps)):
        for copy in copies(i):
            copy.start()
    points = table.shape[1]
    table[...] = table_of(points, False, (y * 4 + lax.axis_index("zl")) * points)
    for i in range(len(steps)):
        for copy in copies(i):
            copy.wait()
        for h in range(2):
            lanes = slice(256 * h, 256 * h + 256)
            slopes = cot[i, :, lanes].astype(F32) * gelu_slope(pre[i, :, lanes].astype(F32))
            out_refs[i][0:128, lanes] = dot(table[...], slopes.astype(BF16)).astype(BF16)
            out_refs[i][128:256, lanes] = dot(table[...], fields[i, :, lanes]).astype(BF16)


def sum_y_kernel(*refs):
    in_refs, out_ref = refs[:4], refs[4]
    total = in_refs[0][...].astype(F32)
    for ref in in_refs[1:]:
        total = total + ref[...].astype(F32)
    low = total.astype(BF16)
    out = None
    for h in range(2):
        moves = row_moves((512, 256), [(8, 64, 1), (2, 2, 128), (1, 2, 64)], [(4, 2, h)])
        part = dot(moves, low[:, 256 * h : 256 * h + 256])
        out = part if out is None else out + part
    out_ref[...] = out.reshape(64, 8, 256).astype(BF16)


def modes_kernel(factor, in_ref, w_ref, out_ref, *rest):
    side_refs, chunks = rest[:4], rest[4]
    x, w_mine, zl_mine, y_mine = (lax.axis_index(name) for name in ("x", "w", "zl", "y"))
    total = jnp.sum(in_ref[...].astype(F32).reshape(16, 4, 8, 256), axis=1).reshape(128, 256)
    first_mode = (x == 0) & (w_mine == 0) & (zl_mine == 0)
    is_u = (lax.broadcasted_iota(jnp.int32, (128, 256), 0) & 2) != 0
    g_scale = jnp.where(first_mode, factor, 2.0 * factor)
    low = (total * jnp.where(is_u, factor, g_scale)).astype(BF16)
    digits = [(32, 2, 2), (8, 4, 8), (4, 2, 1), (1, 4, 32)]
    both = [dot(row_moves((64, 128), digits, base=4 * h), low) for h in range(2)]
    both = jnp.concatenate(both, axis=1)
    g, u = both[:32], both[32:]
    g_low = g.astype(BF16)
    g_turned = dot(turned(32), g_low).astype(BF16)
    grad = (dot(g_low, w_ref[0], NT) + dot(g_turned, w_ref[1], NT)).astype(BF16)
    out = None
    for q in range(4):
        moves = row_moves((128, 32), [(32, 4, 1), (8, 4, 8), (1, 2, 4)], [(2, 4, q)])
        part = dot(moves, grad[:, 128 * q : 128 * q + 128])
        out = part if out is None else out + part
    out = out.reshape(16, 8, 128).astype(BF16)
    for zl in range(4):
        out_ref[:, zl] = out
    for y in range(4):
        lanes = slice(128 * y, 128 * y + 128)
        chunks[y] = jnp.concatenate([g[8 * w : 8 * w + 8, lanes] for w in range(4)], axis=1)
    for t in range(4):
        chunk = chunks[(y_mine + t) & 3]
        side_refs[t][...] = jnp.concatenate([u, chunk], axis=0).astype(BF16)


def relay_kernel(*refs):
    side_refs, send_refs, chunks = refs[:4], refs[4:8], refs[8]
    mine = [ref[32:40, :].astype(F32) for ref in side_refs]
    for zl in range(4):
        chunks[zl] = jnp.concatenate([gather_lanes(m, zl) for m in mine], axis=1)
    for t in range(4):
        for q in range(4):
            send_refs[t][32 * q : 32 * q + 32, :] = side_refs[q][0:32, :]
        send_refs[t][128:136, :] = chunks[(lax.axis_index("zl") + t) & 3].astype(BF16)


def weight_kernel(*refs):
    in_refs, weight_ref = refs[:4], refs[4]
    g = jnp.concatenate([ref[128:136, :].astype(F32) for ref in in_refs], axis=0)
    g_turned = dot(turned(32), g.astype(BF16))
    lane = lax.broadcasted_iota(jnp.int32, (32, 128), 1)
    left = []
    for q in range(4):
        one, two = (v[:, 128 * q : 128 * q + 128] for v in (g, g_turned))
        for w in range(4):
            a = pltpu.roll(one, (128 - 32 * w) % 128, 1) if w else one
            b = pltpu.roll(two, (160 - 32 * w) % 128, 1) if w != 1 else two
            left.append(jnp.where(lane < 32, a, b))
    for t in range(4):
        mine = jnp.concatenate([rows[8 * t : 8 * t + 8] for rows in left], axis=0)
        grad = dot(mine.astype(BF16), in_refs[t][0:128, :], TN)
        ki = (lax.axis_index("zl") - t) & 3
        weight_ref[ki, 0] = grad[0:32]
        weight_ref[ki, 1] = grad[32:64]


def field_kernel(factor, step, in_ref, *rest):
    if step == 0:
        field_hbm, table_ref, out, sem = rest
        points = table_ref.shape[0]
        offset = (lax.axis_index("y") * 4 + lax.axis_index("zl")) * points
        table_ref[...] = table_of(points, True, offset)
    else:
        table_ref, _, field_hbm, out, sem = rest
    blocks = in_ref[...].astype(F32).reshape(512, 128).astype(BF16)
    b = (lax.axis_index("y") - step) & 3
    copies = []
    for h in range(2):
        modes = []
        for q in (2 * h, 2 * h + 1):
            row = lax.broadcasted_iota(jnp.int32, (128, 512), 0)
            col = lax.broadcasted_iota(jnp.int32, (128, 512), 1)
            source = ((row & 63) << 3) + (row >> 6) + 2 * q
            modes.append(dot(jnp.where(source == col, 1.0, 0.0).astype(BF16), blocks))
        modes = jnp.concatenate(modes, axis=1).astype(BF16)
        out[h] = (dot(table_ref[...], modes) * factor).astype(BF16)
        lanes = slice(256 * h, 256 * h + 256)
        copies.append(pltpu.make_async_copy(out.at[h], field_hbm.at[b, :, lanes], sem.at[h]))
        copies[-1].start()
    for copy in copies:
        copy.wait()


def shifted(value, axis, distance):
    return lax.ppermute(value, axis, [(i, (i + distance) % 4) for i in range(4)])


def cost(flops, bytes_accessed):
    return pl.CostEstimate(flops=flops, bytes_accessed=bytes_accessed, transcendentals=0)


def shards(fields, pre_act, cotangent, weights):
    total = fields.shape[1] * lax.axis_size("y") * lax.axis_size("zl")
    factor = float(total) ** (-0.5)
    vmem = pl.BlockSpec(memory_space=pltpu.VMEM)
    hbm = pl.BlockSpec(memory_space=pltpu.HBM)
    params = pltpu.CompilerParams(vmem_limit_bytes=40 * 2**20)

    def block(*shape):
        return jax.ShapeDtypeStruct(shape, BF16)

    def spectra(steps, after):
        n = len(steps)
        return pl.pallas_call(
            functools.partial(spectra_kernel, steps),
            in_specs=[hbm] * 4,
            out_specs=[vmem] * n,
            out_shape=[block(256, 512)] * n,
            scratch_shapes=[pltpu.VMEM((n, 512, 512), BF16)] * 3
            + [pltpu.VMEM((128, 512), BF16), pltpu.SemaphoreType.DMA((3, n))],
            compiler_params=pltpu.CompilerParams(vmem_limit_bytes=SPECTRA_VMEM),
            cost_estimate=cost(2**28 * n, 2**22 * n),
            name="spectra",
        )(fields, pre_act, cotangent, after)

    (two,) = spectra((2,), fields)
    one, three = spectra((1, 3), two)
    (own,) = spectra((0,), one)
    one, two, three = shifted(one, "y", 1), shifted(two, "y", 2), shifted(three, "y", 3)
    send = pl.pallas_call(
        sum_y_kernel,
        in_specs=[vmem] * 4,
        out_specs=vmem,
        out_shape=block(64, 8, 256),
        compiler_params=params,
        name="sum_y",
    )(own, one, two, three)
    got = lax.all_to_all(send, OTHERS, 0, 0, tiled=True)
    mine = lax.dynamic_index_in_dim(weights, lax.axis_index("zl"), 0, keepdims=False)
    send, *sides = pl.pallas_call(
        functools.partial(modes_kernel, factor),
        in_specs=[vmem, vmem],
        out_specs=[vmem] * 5,
        out_shape=[block(16, 4, 8, 128)] + [block(40, 512)] * 4,
        scratch_shapes=[pltpu.VMEM((4, 8, 512), F32)],
        compiler_params=params,
        name="modes",
    )(got, mine)
    sides = [sides[0]] + [shifted(sides[t], "y", t) for t in range(1, 4)]
    got = lax.all_to_all(send.reshape(64, 8, 128), OTHERS, 0, 0, tiled=True)
    sides = pl.pallas_call(
        relay_kernel,
        in_specs=[vmem] * 4,
        out_specs=[vmem] * 4,
        out_shape=[block(136, 512)] * 4,
        scratch_shapes=[pltpu.VMEM((4, 8, 512), F32)],
        compiler_params=params,
        cost_estimate=cost(2**26, 2**20),
        name="relay",
    )(*sides)
    sides = [sides[0]] + [shifted(sides[t], "zl", t) for t in range(1, 4)]
    weight_grad = pl.pallas_call(
        weight_kernel,
        in_specs=[vmem] * 4,
        out_specs=vmem,
        out_shape=jax.ShapeDtypeStruct((4, 2, 32, 512), F32),
        compiler_params=params,
        cost_estimate=cost(2**27, 2**21),
        name="weight",
    )(*sides)
    scratch = [pltpu.VMEM((2, 512, 256), BF16), pltpu.SemaphoreType.DMA((2,))]
    received = {t: shifted(got, "y", t) for t in (2, 1, 3)}
    field_grad, table = pl.pallas_call(
        functools.partial(field_kernel, factor, 0),
        in_specs=[vmem],
        out_specs=[hbm, vmem],
        out_shape=[block(4, 512, 512), block(512, 128)],
        scratch_shapes=scratch,
        compiler_params=params,
        cost_estimate=cost(2**27, 2**20),
        name="field",
    )(got)
    for t in (1, 3, 2):
        field_grad = pl.pallas_call(
            functools.partial(field_kernel, factor, t),
            in_specs=[vmem, vmem, hbm],
            out_specs=hbm,
            out_shape=block(4, 512, 512),
            scratch_shapes=scratch,
            input_output_aliases={2: 0},
            compiler_params=params,
            cost_estimate=cost(2**27, 2**20),
            name="field",
        )(received[t], table, field_grad)
    return field_grad, jnp.swapaxes(weight_grad, 2, 3)


def solution(mesh):
    grid = Mesh(mesh.devices.reshape(4, 4, 4, 4), ("y", "zl", "x", "w"))
    space, mode = ("y", "zl"), ("x", "w")
    whole = P(mode, space, None)
    return jax.shard_map(
        shards,
        mesh=grid,
        in_specs=(whole, whole, whole, P(mode, None, None, None)),
        out_specs=(whole, P(mode, None, None, space)),
        check_vma=False,
    )
```

time: 87 us -> 83.8 us (0.963); the launches traced: 86.5 us -> 82.4 us
  blocking collectives: 23.7 us -> 0 us
  starting transfers between devices: 23.6 us -> 37.2 us
  Pallas kernels: 12.1 us -> 19.3 us
  waiting for transfers between devices: 25.1 us -> 22.7 us
  local copies, waits for them, and re-layouts: 1.29 us -> 2.25 us
    all_to_all x1 -> x0, blocking collectives: 23.7 us -> none  [shards(): got = lax.all_to_all(send, FIRST, 0, 0, tiled=True)]
    ppermute x6 -> x12, starting transfers between devices: 6.07 us -> 18.8 us  [shifted(): lax.ppermute(value, axis, [(i, (i + distance) % 4) for i in range(4)])]
    all_to_all x3 -> x2, waiting for transfers between devices: 22.4 us -> 11.5 us  [the longest x1 11.5 us: shards(): got = lax.all_to_all(send, OTHERS, 0, 0, tiled=True)]
    ppermute x6 -> x12, waiting for transfers between devices: 2.7 us -> 11.1 us  [shifted(): lax.ppermute(value, axis, [(i, (i + distance) % 4) for i in range(4)])]
    pallas_call x5 -> x10, Pallas kernels: 11 us -> 17.8 us  [the longest x3 9.07 us: spectra(): pl.pallas_call(functools.partial(spectra_kernel, steps), in_specs=[hbm] *...]
    unnamed x0 -> x2, local copies, waits for them, and re-layouts: none -> 0.95 us
    all_to_all x3 -> x2, starting transfers between devices: 17.5 us -> 18.4 us  [the longest x1 13.3 us: shards(): got = lax.all_to_all(send, OTHERS, 0, 0, tiled=True)]
  transfers between devices with their start and end apart: 9 -> 14, of which waited for: 6 -> 5; matrix products, arithmetic and copies ran while one was open for 1% -> 2% of each run, Pallas kernels for 3% -> 15%
where the time goes in v4:
time: 83.8 us; the launch traced here: 82.4 us
  starting transfers between devices  37.2 us (44%)
  waiting for transfers between devices  22.7 us (27%)
  Pallas kernels  19.3 us (23%)
  local copies, waits for them, and re-layouts  2.25 us (3%)
  between operations  0.9 us (1%)
    ppermute x12, starting transfers between devices, shifted(): lax.ppermute(value, axis, [(i, (i + distance) % 4) for i in range(4)])  18.8 us
    all_to_all x1, starting transfers between devices, shards(): got = lax.all_to_all(send, OTHERS, 0, 0, tiled=True)  13.3 us
    all_to_all x1, waiting for transfers between devices, shards(): got = lax.all_to_all(send, OTHERS, 0, 0, tiled=True)  11.5 us
    ppermute x12, waiting for transfers between devices, shifted(): lax.ppermute(value, axis, [(i, (i + distance) % 4) for i in range(4)])  11.1 us
    pallas_call x3, Pallas kernels, spectra(): pl.pallas_call(functools.partial(spectra_kernel, steps), in_specs=[hbm] *...  9.07 us
    all_to_all x1, starting transfers between devices, shards(): got = lax.all_to_all(send.reshape(64, 8, 128), OTHERS, 0, 0, tiled=True)  5.09 us
    pallas_call x3, Pallas kernels, shards(): pl.pallas_call(functools.partial(field_kernel, factor, t), in_specs=[vmem...  4.57 us
  transfers between devices with their start and end apart: 14, of which 5 were waited for; matrix products, arithmetic and copies ran while one was open for 2% of the time, Pallas kernels for 15%

profile of v4, /device:TPU:1, one launch (start us, length us, event | category | flops | bytes accessed | tf_op | source)
XLA Modules:
  0.0 82.4 jit_solution(13294781443169743312)
XLA Ops:
  0.6 2.8 %spectra.3._ = bf16[256,512]{1,0:T(8,128)(2,1)} custom-call(bf16[4,512,512]{2,1,0:T(8,128)(2,1)} %fields_hbm.5, bf16[4,512,512]{2,1,0:T(8,128)(2,1)} %pre_hbm.5, bf16[4,512,512]{2,1,0:T(8,128)(2,1)} %cot_hbm.5, bf16[4,512,512]{2,1,0:T(8,128)(2,1)} %fields_hbm.5), custom_call_target="tpu_custom_call" | custom-call | flops 268435456 | bytes 4194304 | tf_op jit(solution)/shard_map/spectra/pallas_call | solution.py:232
  3.4 3.8 %collective-permute-start.1 = (bf16[256,512]{1,0:T(8,128)(2,1)}, bf16[256,512]{1,0:T(8,128)(2,1)S(1)}, u32[]{:S(2)}, u32[]{:S(2)}) collective-permute-start(bf16[256,512]{1,0:T(8,128)(2,1)} %spectra.3._), channel_id=1, source_target_pairs={{0,128},{64,192},{128,0},{192,64},{1,129},{65,193},{129,1},{193,65... | collective-permute-start | bytes 786440 | tf_op jit(solution)/shard_map/ppermute | solution.py:213
  7.2 3.5 %spectra.4 = (bf16[256,512]{1,0:T(8,128)(2,1)}, bf16[256,512]{1,0:T(8,128)(2,1)}) custom-call(bf16[4,512,512]{2,1,0:T(8,128)(2,1)} %fields_hbm.5, bf16[4,512,512]{2,1,0:T(8,128)(2,1)} %pre_hbm.5, bf16[4,512,512]{2,1,0:T(8,128)(2,1)} %cot_hbm.5, bf16[256,512]{1,0:T(8,128)(2,1)} %spectra.3._), custom_call_target="tpu_custom_call" | custom-call | flops 536870912 | bytes 8388608 | tf_op jit(solution)/shard_map/spectra/pallas_call | solution.py:232
  10.8 0.5 collective-permute-start
  11.3 2.3 %collective-permute-start.2 = (bf16[256,512]{1,0:T(8,128)(2,1)}, bf16[256,512]{1,0:T(8,128)(2,1)S(1)}, u32[]{:S(2)}, u32[]{:S(2)}) collective-permute-start(bf16[256,512]{1,0:T(8,128)(2,1)} %get-tuple-element.16), channel_id=1, source_target_pairs={{0,192},{64,0},{128,64},{192,128},{1,193},{65,1},{129,65},{193,129... | collective-permute-start | bytes 786440 | tf_op jit(solution)/shard_map/ppermute | solution.py:213
  13.5 2.8 %spectra.5.refs_0_ = bf16[256,512]{1,0:T(8,128)(2,1)} custom-call(bf16[4,512,512]{2,1,0:T(8,128)(2,1)} %fields_hbm.5, bf16[4,512,512]{2,1,0:T(8,128)(2,1)} %pre_hbm.5, bf16[4,512,512]{2,1,0:T(8,128)(2,1)} %cot_hbm.5, bf16[256,512]{1,0:T(8,128)(2,1)} %get-tuple-element.15._), custom_call_target="tpu_custom_call" | custom-call | flops 268435456 | bytes 4194304 | tf_op jit(solution)/shard_map/spectra/pallas_call | solution.py:232
  16.3 2.8 %collective-permute-done.refs_1_ = bf16[256,512]{1,0:T(8,128)(2,1)S(1)} collective-permute-done((bf16[256,512]{1,0:T(8,128)(2,1)}, bf16[256,512]{1,0:T(8,128)(2,1)S(1)}, u32[]{:S(2)}, u32[]{:S(2)}) %collective-permute-start) | collective-permute-done | bytes 262176 | tf_op jit(solution)/shard_map/ppermute | solution.py:213
  19.1 0.0 collective-permute-done.1.refs_2_
  19.1 0.9 %copy-done = bf16[256,512]{1,0:T(8,128)(2,1)S(1)} copy-done((bf16[256,512]{1,0:T(8,128)(2,1)S(1)}, bf16[256,512]{1,0:T(8,128)(2,1)}, u32[]{:S(2)}) %copy-start) | copy-done | bytes 262168
  20.1 1.2 %sum_y.1 = bf16[64,8,256]{2,1,0:T(8,128)(2,1)} custom-call(bf16[256,512]{1,0:T(8,128)(2,1)S(1)} %copy-done, bf16[256,512]{1,0:T(8,128)(2,1)S(1)} %collective-permute-done.refs_1_, bf16[256,512]{1,0:T(8,128)(2,1)S(1)} %collective-permute-done.1.refs_2_, bf16[256,512]{1,0:T(8,128)(2,1)S(1)} %collective-permute-done.2.refs_3_), custom_call_target="tpu_custom_call" | custom-call | tf_op jit(solution)/shard_map/sum_y/pallas_call | solution.py:248
  21.2 13.3 %all-to-all-start = ((bf16[64,8,256]{2,1,0:T(8,128)(2,1)}), bf16[64,8,256]{2,1,0:T(8,128)(2,1)S(1)}, u32[]{:S(2)}, u32[]{:S(2)}) async-start(bf16[64,8,256]{2,1,0:T(8,128)(2,1)} %sum_y.1), calls=%async_computation | async-start | bytes 524288 | tf_op jit(solution)/shard_map/all_to_all | solution.py:256
  34.6 1.3 %dynamic-slice_bitcast_fusion.w_ref = bf16[2,512,512]{2,1,0:T(8,128)(2,1)S(1)} fusion(bf16[4,2,512,512]{3,2,1,0:T(8,128)(2,1)} %param.7, s32[]{:T(128)S(6)} %select_n.4), kind=kLoop, calls=%fused_computation | loop fusion | bytes 2097156 | tf_op jit(solution)/shard_map/jit(dynamic_index_in_dim)/squeeze | solution.py:257
  35.9 11.5 %all-to-all-done.in_ref = bf16[64,8,256]{2,1,0:T(8,128)(2,1)S(1)} async-done(((bf16[64,8,256]{2,1,0:T(8,128)(2,1)}), bf16[64,8,256]{2,1,0:T(8,128)(2,1)S(1)}, u32[]{:S(2)}, u32[]{:S(2)}) %all-to-all-start) | async-done | bytes 262176 | tf_op jit(solution)/shard_map/all_to_all | solution.py:256
  47.4 1.5 %modes.1 = (bf16[16,4,8,128]{3,2,1,0:T(8,128)(2,1)}, bf16[40,512]{1,0:T(8,128)(2,1)S(1)}, bf16[40,512]{1,0:T(8,128)(2,1)S(1)}, bf16[40,512]{1,0:T(8,128)(2,1)S(1)}, bf16[40,512]{1,0:T(8,128)(2,1)S(1)}) custom-call(bf16[64,8,256]{2,1,0:T(8,128)(2,1)S(1)} %all-to-all-done.in_ref, bf16[2,512,512]{2,1,0:T(8,128)(2,1)S(1)} %dynamic-slice_bitcast_fusion.w_ref), custom_call_target="tpu_custom_call" | custom-call | tf_op jit(solution)/shard_map/modes/pallas_call | solution.py:258
  48.9 5.1 %all-to-all-start.1 = ((bf16[64,8,128]{2,1,0:T(8,128)(2,1)}), bf16[64,8,128]{2,1,0:T(8,128)(2,1)S(1)}, u32[]{:S(2)}, u32[]{:S(2)}) async-start(bf16[64,8,128]{2,1,0:T(8,128)(2,1)} %bitcast.1), calls=%async_computation.1 | async-start | bytes 262144 | tf_op jit(solution)/shard_map/all_to_all | solution.py:268
  54.0 0.9 %collective-permute-start.6 = (bf16[40,512]{1,0:T(8,128)(2,1)S(1)}, bf16[40,512]{1,0:T(8,128)(2,1)S(1)}, u32[]{:S(2)}, u32[]{:S(2)}) collective-permute-start(bf16[40,512]{1,0:T(8,128)(2,1)S(1)} %get-tuple-element.21), channel_id=1, source_target_pairs={{0,64},{64,128},{128,192},{192,0},{1,65},{65,129},{129,193},{193,1... | collective-permute-start | bytes 122888 | tf_op jit(solution)/shard_map/ppermute | solution.py:213
  54.9 3.0 %collective-permute-start.7 = (bf16[40,512]{1,0:T(8,128)(2,1)S(1)}, bf16[40,512]{1,0:T(8,128)(2,1)S(1)}, u32[]{:S(2)}, u32[]{:S(2)}) collective-permute-start(bf16[40,512]{1,0:T(8,128)(2,1)S(1)} %get-tuple-element.22), channel_id=1, source_target_pairs={{0,128},{64,192},{128,0},{192,64},{1,129},{65,193},{129,1},{193,65... | collective-permute-start | bytes 122888 | tf_op jit(solution)/shard_map/ppermute | solution.py:213
  58.0 0.5 collective-permute-start.8
  58.5 1.6 %collective-permute-done.7.refs_2_ = bf16[40,512]{1,0:T(8,128)(2,1)S(1)} collective-permute-done((bf16[40,512]{1,0:T(8,128)(2,1)S(1)}, bf16[40,512]{1,0:T(8,128)(2,1)S(1)}, u32[]{:S(2)}, u32[]{:S(2)}) %collective-permute-start.7) | collective-permute-done | bytes 40992 | tf_op jit(solution)/shard_map/ppermute | solution.py:213
  60.1 1.0 %collective-permute-done.8.refs_3_ = bf16[40,512]{1,0:T(8,128)(2,1)S(1)} collective-permute-done((bf16[40,512]{1,0:T(8,128)(2,1)S(1)}, bf16[40,512]{1,0:T(8,128)(2,1)S(1)}, u32[]{:S(2)}, u32[]{:S(2)}) %collective-permute-start.8) | collective-permute-done | bytes 40992 | tf_op jit(solution)/shard_map/ppermute | solution.py:213
  61.1 0.1 relay.1
  61.2 1.5 %collective-permute-start.9 = (bf16[136,512]{1,0:T(8,128)(2,1)S(1)}, bf16[136,512]{1,0:T(8,128)(2,1)S(1)}, u32[]{:S(2)}, u32[]{:S(2)}) collective-permute-start(bf16[136,512]{1,0:T(8,128)(2,1)S(1)} %get-tuple-element.25), channel_id=1, source_target_pairs={{0,16},{16,32},{32,48},{48,0},{1,17},{17,33},{33,49},{49,1},{2,18}... | collective-permute-start | bytes 417800 | tf_op jit(solution)/shard_map/ppermute | solution.py:213
  62.7 2.1 %collective-permute-start.10 = (bf16[136,512]{1,0:T(8,128)(2,1)S(1)}, bf16[136,512]{1,0:T(8,128)(2,1)S(1)}, u32[]{:S(2)}, u32[]{:S(2)}) collective-permute-start(bf16[136,512]{1,0:T(8,128)(2,1)S(1)} %get-tuple-element.26), channel_id=1, source_target_pairs={{0,32},{16,48},{32,0},{48,16},{1,33},{17,49},{33,1},{49,17},{2,34}... | collective-permute-start | bytes 417800 | tf_op jit(solution)/shard_map/ppermute | solution.py:213
  64.8 1.2 %collective-permute-start.11 = (bf16[136,512]{1,0:T(8,128)(2,1)S(1)}, bf16[136,512]{1,0:T(8,128)(2,1)S(1)}, u32[]{:S(2)}, u32[]{:S(2)}) collective-permute-start(bf16[136,512]{1,0:T(8,128)(2,1)S(1)} %get-tuple-element.27), channel_id=1, source_target_pairs={{0,48},{16,0},{32,16},{48,32},{1,49},{17,1},{33,17},{49,33},{2,50}... | collective-permute-start | bytes 417800 | tf_op jit(solution)/shard_map/ppermute | solution.py:213
  65.9 2.7 %collective-permute-start.4 = (bf16[64,8,128]{2,1,0:T(8,128)(2,1)S(1)}, bf16[64,8,128]{2,1,0:T(8,128)(2,1)S(1)}, u32[]{:S(2)}, u32[]{:S(2)}) collective-permute-start(bf16[64,8,128]{2,1,0:T(8,128)(2,1)S(1)} %all-to-all-done.1.in_ref), channel_id=1, source_target_pairs={{0,192},{64,0},{128,64},{192,128},{1,193},{65,1},{129,65},{193,129... | collective-permute-start | bytes 393224 | tf_op jit(solution)/shard_map/ppermute | solution.py:213
  68.6 0.4 collective-permute-start.3
  69.0 5.7 %collective-permute-done.10.refs_2_ = bf16[136,512]{1,0:T(8,128)(2,1)S(1)} collective-permute-done((bf16[136,512]{1,0:T(8,128)(2,1)S(1)}, bf16[136,512]{1,0:T(8,128)(2,1)S(1)}, u32[]{:S(2)}, u32[]{:S(2)}) %collective-permute-start.10) | collective-permute-done | bytes 139296 | tf_op jit(solution)/shard_map/ppermute | solution.py:213
  74.7 1.3 %weight.1 = f32[4,2,32,512]{3,2,1,0:T(8,128)} custom-call(bf16[136,512]{1,0:T(8,128)(2,1)S(1)} %get-tuple-element.24.refs_0_, bf16[136,512]{1,0:T(8,128)(2,1)S(1)} %collective-permute-done.9.refs_1_, bf16[136,512]{1,0:T(8,128)(2,1)S(1)} %collective-permute-done.10.refs_2_, bf16[136,512]{1,0:T(8,128)(2,1)S(1)} %collective-permute-done.11.refs_3_), custom_call_target="tpu_custom_call" | custom-call | flops 134217728 | bytes 2097152 | tf_op jit(solution)/shard_map/weight/pallas_call | solution.py:280
  76.0 1.6 %field.4 = (bf16[4,512,512]{2,1,0:T(8,128)(2,1)}, bf16[512,128]{1,0:T(8,128)(2,1)S(1)}) custom-call(bf16[64,8,128]{2,1,0:T(8,128)(2,1)S(1)} %all-to-all-done.1.in_ref), custom_call_target="tpu_custom_call" | custom-call | flops 134217728 | bytes 1048576 | tf_op jit(solution)/shard_map/field/pallas_call | solution.py:291
  77.6 1.5 %field.5.rest_1_ = bf16[4,512,512]{2,1,0:T(8,128)(2,1)} custom-call(bf16[64,8,128]{2,1,0:T(8,128)(2,1)S(1)} %collective-permute-done.5.in_ref, bf16[512,128]{1,0:T(8,128)(2,1)S(1)} %get-tuple-element.18.rest_0_, bf16[4,512,512]{2,1,0:T(8,128)(2,1)} %get-tuple-element.19.rest_1_), custom_call_target="tpu_custom_call", output_to_operand_aliasing={{}: (2, {})} | custom-call | flops 134217728 | bytes 1048576 | tf_op jit(solution)/shard_map/field/pallas_call | solution.py:302
  79.2 1.5 %field.6.rest_1_ = bf16[4,512,512]{2,1,0:T(8,128)(2,1)} custom-call(bf16[64,8,128]{2,1,0:T(8,128)(2,1)S(1)} %collective-permute-done.4.in_ref, bf16[512,128]{1,0:T(8,128)(2,1)S(1)} %get-tuple-element.18.rest_0_, bf16[4,512,512]{2,1,0:T(8,128)(2,1)} %field.5.rest_1_), custom_call_target="tpu_custom_call", output_to_operand_aliasing={{}: (2, {})} | custom-call | flops 134217728 | bytes 1048576 | tf_op jit(solution)/shard_map/field/pallas_call | solution.py:302
  80.7 1.5 %field.7 = bf16[4,512,512]{2,1,0:T(8,128)(2,1)} custom-call(bf16[64,8,128]{2,1,0:T(8,128)(2,1)S(1)} %collective-permute-done.3.in_ref, bf16[512,128]{1,0:T(8,128)(2,1)S(1)} %get-tuple-element.18.rest_0_, bf16[4,512,512]{2,1,0:T(8,128)(2,1)} %field.6.rest_1_), custom_call_target="tpu_custom_call", output_to_operand_aliasing={{}: (2, {})} | custom-call | flops 134217728 | bytes 1048576 | tf_op jit(solution)/shard_map/field/pallas_call | solution.py:302
  (10 shorter events, 0.0 us)
Async XLA Ops:
  3.4 15.7 %collective-permute-start.1 = (bf16[256,512]{1,0:T(8,128)(2,1)}, bf16[256,512]{1,0:T(8,128)(2,1)S(1)}, u32[]{:S(2)}, u32[]{:S(2)}) collective-permute-start(bf16[256,512]{1,0:T(8,128)(2,1)} %spectra.3._), channel_id=1, source_target_pairs={{0,128},{64,192},{128,0},{192,64},{1,129},{65,193},{129,1},{193,65... | collective-permute-start | bytes 786440 | tf_op jit(solution)/shard_map/ppermute | solution.py:213
  10.8 8.4 %collective-permute-start = (bf16[256,512]{1,0:T(8,128)(2,1)}, bf16[256,512]{1,0:T(8,128)(2,1)S(1)}, u32[]{:S(2)}, u32[]{:S(2)}) collective-permute-start(bf16[256,512]{1,0:T(8,128)(2,1)} %get-tuple-element.15._), channel_id=1, source_target_pairs={{0,64},{64,128},{128,192},{192,0},{1,65},{65,129},{129,193},{193,1... | collective-permute-start | bytes 786440 | tf_op jit(solution)/shard_map/ppermute | solution.py:213
  11.3 7.9 %collective-permute-start.2 = (bf16[256,512]{1,0:T(8,128)(2,1)}, bf16[256,512]{1,0:T(8,128)(2,1)S(1)}, u32[]{:S(2)}, u32[]{:S(2)}) collective-permute-start(bf16[256,512]{1,0:T(8,128)(2,1)} %get-tuple-element.16), channel_id=1, source_target_pairs={{0,192},{64,0},{128,64},{192,128},{1,193},{65,1},{129,65},{193,129... | collective-permute-start | bytes 786440 | tf_op jit(solution)/shard_map/ppermute | solution.py:213
  19.1 1.0 %copy-start = (bf16[256,512]{1,0:T(8,128)(2,1)S(1)}, bf16[256,512]{1,0:T(8,128)(2,1)}, u32[]{:S(2)}) copy-start(bf16[256,512]{1,0:T(8,128)(2,1)} %spectra.5.refs_0_) | copy-start | bytes 786436
  21.2 26.2 %all-to-all-start = ((bf16[64,8,256]{2,1,0:T(8,128)(2,1)}), bf16[64,8,256]{2,1,0:T(8,128)(2,1)S(1)}, u32[]{:S(2)}, u32[]{:S(2)}) async-start(bf16[64,8,256]{2,1,0:T(8,128)(2,1)} %sum_y.1), calls=%async_computation | async-start | bytes 524288 | tf_op jit(solution)/shard_map/all_to_all | solution.py:256
  48.9 17.0 %all-to-all-start.1 = ((bf16[64,8,128]{2,1,0:T(8,128)(2,1)}), bf16[64,8,128]{2,1,0:T(8,128)(2,1)S(1)}, u32[]{:S(2)}, u32[]{:S(2)}) async-start(bf16[64,8,128]{2,1,0:T(8,128)(2,1)} %bitcast.1), calls=%async_computation.1 | async-start | bytes 262144 | tf_op jit(solution)/shard_map/all_to_all | solution.py:268
  54.0 4.5 %collective-permute-start.6 = (bf16[40,512]{1,0:T(8,128)(2,1)S(1)}, bf16[40,512]{1,0:T(8,128)(2,1)S(1)}, u32[]{:S(2)}, u32[]{:S(2)}) collective-permute-start(bf16[40,512]{1,0:T(8,128)(2,1)S(1)} %get-tuple-element.21), channel_id=1, source_target_pairs={{0,64},{64,128},{128,192},{192,0},{1,65},{65,129},{129,193},{193,1... | collective-permute-start | bytes 122888 | tf_op jit(solution)/shard_map/ppermute | solution.py:213
  54.9 5.1 %collective-permute-start.7 = (bf16[40,512]{1,0:T(8,128)(2,1)S(1)}, bf16[40,512]{1,0:T(8,128)(2,1)S(1)}, u32[]{:S(2)}, u32[]{:S(2)}) collective-permute-start(bf16[40,512]{1,0:T(8,128)(2,1)S(1)} %get-tuple-element.22), channel_id=1, source_target_pairs={{0,128},{64,192},{128,0},{192,64},{1,129},{65,193},{129,1},{193,65... | collective-permute-start | bytes 122888 | tf_op jit(solution)/shard_map/ppermute | solution.py:213
  58.0 3.1 %collective-permute-start.8 = (bf16[40,512]{1,0:T(8,128)(2,1)S(1)}, bf16[40,512]{1,0:T(8,128)(2,1)S(1)}, u32[]{:S(2)}, u32[]{:S(2)}) collective-permute-start(bf16[40,512]{1,0:T(8,128)(2,1)S(1)} %get-tuple-element.23), channel_id=1, source_target_pairs={{0,192},{64,0},{128,64},{192,128},{1,193},{65,1},{129,65},{193,129... | collective-permute-start | bytes 122888 | tf_op jit(solution)/shard_map/ppermute | solution.py:213
  61.2 7.4 %collective-permute-start.9 = (bf16[136,512]{1,0:T(8,128)(2,1)S(1)}, bf16[136,512]{1,0:T(8,128)(2,1)S(1)}, u32[]{:S(2)}, u32[]{:S(2)}) collective-permute-start(bf16[136,512]{1,0:T(8,128)(2,1)S(1)} %get-tuple-element.25), channel_id=1, source_target_pairs={{0,16},{16,32},{32,48},{48,0},{1,17},{17,33},{33,49},{49,1},{2,18}... | collective-permute-start | bytes 417800 | tf_op jit(solution)/shard_map/ppermute | solution.py:213
  62.7 12.0 %collective-permute-start.10 = (bf16[136,512]{1,0:T(8,128)(2,1)S(1)}, bf16[136,512]{1,0:T(8,128)(2,1)S(1)}, u32[]{:S(2)}, u32[]{:S(2)}) collective-permute-start(bf16[136,512]{1,0:T(8,128)(2,1)S(1)} %get-tuple-element.26), channel_id=1, source_target_pairs={{0,32},{16,48},{32,0},{48,16},{1,33},{17,49},{33,1},{49,17},{2,34}... | collective-permute-start | bytes 417800 | tf_op jit(solution)/shard_map/ppermute | solution.py:213
  64.8 9.9 %collective-permute-start.11 = (bf16[136,512]{1,0:T(8,128)(2,1)S(1)}, bf16[136,512]{1,0:T(8,128)(2,1)S(1)}, u32[]{:S(2)}, u32[]{:S(2)}) collective-permute-start(bf16[136,512]{1,0:T(8,128)(2,1)S(1)} %get-tuple-element.27), channel_id=1, source_target_pairs={{0,48},{16,0},{32,16},{48,32},{1,49},{17,1},{33,17},{49,33},{2,50}... | collective-permute-start | bytes 417800 | tf_op jit(solution)/shard_map/ppermute | solution.py:213
  65.9 11.7 %collective-permute-start.5 = (bf16[64,8,128]{2,1,0:T(8,128)(2,1)S(1)}, bf16[64,8,128]{2,1,0:T(8,128)(2,1)S(1)}, u32[]{:S(2)}, u32[]{:S(2)}) collective-permute-start(bf16[64,8,128]{2,1,0:T(8,128)(2,1)S(1)} %all-to-all-done.1.in_ref), channel_id=1, source_target_pairs={{0,64},{64,128},{128,192},{192,0},{1,65},{65,129},{129,193},{193,1... | collective-permute-start | bytes 393224 | tf_op jit(solution)/shard_map/ppermute | solution.py:213
  65.9 13.2 %collective-permute-start.4 = (bf16[64,8,128]{2,1,0:T(8,128)(2,1)S(1)}, bf16[64,8,128]{2,1,0:T(8,128)(2,1)S(1)}, u32[]{:S(2)}, u32[]{:S(2)}) collective-permute-start(bf16[64,8,128]{2,1,0:T(8,128)(2,1)S(1)} %all-to-all-done.1.in_ref), channel_id=1, source_target_pairs={{0,192},{64,0},{128,64},{192,128},{1,193},{65,1},{129,65},{193,129... | collective-permute-start | bytes 393224 | tf_op jit(solution)/shard_map/ppermute | solution.py:213
  68.6 12.1 %collective-permute-start.3 = (bf16[64,8,128]{2,1,0:T(8,128)(2,1)S(1)}, bf16[64,8,128]{2,1,0:T(8,128)(2,1)S(1)}, u32[]{:S(2)}, u32[]{:S(2)}) collective-permute-start(bf16[64,8,128]{2,1,0:T(8,128)(2,1)S(1)} %all-to-all-done.1.in_ref), channel_id=1, source_target_pairs={{0,128},{64,192},{128,0},{192,64},{1,129},{65,193},{129,1},{193,65... | collective-permute-start | bytes 393224 | tf_op jit(solution)/shard_map/ppermute | solution.py:213

commit v5 on v4

--- a/solution.py
+++ b/solution.py
@@ -68,50 +68,40 @@
     return jnp.where((row ^ 4) == col, sign, 0.0).astype(BF16)
 
 
-def gather_lanes(values, quarter):
-    lane = lax.broadcasted_iota(jnp.int32, (values.shape[0], 128), 1) >> 5
-    out = None
-    for j in range(4):
-        block = values[:, 128 * j : 128 * j + 128]
-        shift = (32 * (j - quarter)) % 128
-        if shift:
-            block = pltpu.roll(block, shift, 1)
-        out = block if out is None else jnp.where(lane == j, block, out)
-    return out
-
-
 def spectra_kernel(steps, fields_hbm, pre_hbm, cot_hbm, _, *rest):
     out_refs, (fields, pre, cot, table, sems) = rest[: len(steps)], rest[len(steps) :]
     y = lax.axis_index("y")
 
-    def copies(i):
+    def copies(i, h):
         b = (y + steps[i]) & 3
+        at = slice(256 * h, 256 * h + 256)
         return [
-            pltpu.make_async_copy(hbm.at[b], vmem.at[i], sems.at[n, i])
+            pltpu.make_async_copy(hbm.at[b, :, at], vmem.at[i, :, at], sems.at[n, i, h])
             for n, (hbm, vmem) in enumerate(((pre_hbm, pre), (cot_hbm, cot), (fields_hbm, fields)))
         ]
 
     for i in range(len(steps)):
-        for copy in copies(i):
-            copy.start()
+        for h in range(2):
+            for copy in copies(i, h):
+                copy.start()
     points = table.shape[1]
     table[...] = table_of(points, False, (y * 4 + lax.axis_index("zl")) * points)
     for i in range(len(steps)):
-        for copy in copies(i):
-            copy.wait()
         for h in range(2):
+            for copy in copies(i, h):
+                copy.wait()
             lanes = slice(256 * h, 256 * h + 256)
             slopes = cot[i, :, lanes].astype(F32) * gelu_slope(pre[i, :, lanes].astype(F32))
             out_refs[i][0:128, lanes] = dot(table[...], slopes.astype(BF16)).astype(BF16)
             out_refs[i][128:256, lanes] = dot(table[...], fields[i, :, lanes]).astype(BF16)
 
 
-def sum_y_kernel(*refs):
-    in_refs, out_ref = refs[:4], refs[4]
-    total = in_refs[0][...].astype(F32)
-    for ref in in_refs[1:]:
-        total = total + ref[...].astype(F32)
-    low = total.astype(BF16)
+def sum_y_kernel(own_hbm, one_ref, two_ref, three_ref, out_ref, own, sem):
+    copy = pltpu.make_async_copy(own_hbm, own, sem)
+    copy.start()
+    total = one_ref[...].astype(F32) + two_ref[...].astype(F32) + three_ref[...].astype(F32)
+    copy.wait()
+    low = (total + own[...].astype(F32)).astype(BF16)
     out = None
     for h in range(2):
         moves = row_moves((512, 256), [(8, 64, 1), (2, 2, 128), (1, 2, 64)], [(4, 2, h)])
@@ -151,55 +141,45 @@
         side_refs[t][...] = jnp.concatenate([u, chunk], axis=0).astype(BF16)
 
 
-def relay_kernel(*refs):
-    side_refs, send_refs, chunks = refs[:4], refs[4:8], refs[8]
-    mine = [ref[32:40, :].astype(F32) for ref in side_refs]
-    for zl in range(4):
-        chunks[zl] = jnp.concatenate([gather_lanes(m, zl) for m in mine], axis=1)
-    for t in range(4):
-        for q in range(4):
-            send_refs[t][32 * q : 32 * q + 32, :] = side_refs[q][0:32, :]
-        send_refs[t][128:136, :] = chunks[(lax.axis_index("zl") + t) & 3].astype(BF16)
-
-
 def weight_kernel(*refs):
-    in_refs, weight_ref = refs[:4], refs[4]
-    g = jnp.concatenate([ref[128:136, :].astype(F32) for ref in in_refs], axis=0)
-    g_turned = dot(turned(32), g.astype(BF16))
-    lane = lax.broadcasted_iota(jnp.int32, (32, 128), 1)
-    left = []
-    for q in range(4):
-        one, two = (v[:, 128 * q : 128 * q + 128] for v in (g, g_turned))
-        for w in range(4):
-            a = pltpu.roll(one, (128 - 32 * w) % 128, 1) if w else one
-            b = pltpu.roll(two, (160 - 32 * w) % 128, 1) if w != 1 else two
-            left.append(jnp.where(lane < 32, a, b))
-    for t in range(4):
-        mine = jnp.concatenate([rows[8 * t : 8 * t + 8] for rows in left], axis=0)
-        grad = dot(mine.astype(BF16), in_refs[t][0:128, :], TN)
-        ki = (lax.axis_index("zl") - t) & 3
-        weight_ref[ki, 0] = grad[0:32]
-        weight_ref[ki, 1] = grad[32:64]
+    in_refs, own_ref, send_refs, result = refs[:4], refs[4], refs[5:8], refs[8]
+    u = jnp.concatenate([ref[0:32, :] for ref in in_refs], axis=0)
+    g = jnp.concatenate(
+        [ref[32:40, 128 * w : 128 * w + 128].astype(F32) for ref in in_refs for w in range(4)],
+        axis=0,
+    ).astype(BF16)
+    both = jnp.concatenate([g, dot(turned(128), g).astype(BF16)], axis=1)
+    result[...] = dot(both, u, TN).reshape(2, 4, 32, 512)
+    zl_mine = lax.axis_index("zl")
+    own_ref[...] = result[:, zl_mine]
+    for t in range(1, 4):
+        send_refs[t - 1][...] = result[:, (zl_mine + t) & 3].reshape(64, 512).astype(BF16)
+
+
+def place_kernel(_, own_ref, *refs):
+    weight_ref = refs[3]
+    zl_mine = lax.axis_index("zl")
+    weight_ref[zl_mine] = own_ref[...]
+    for t in range(1, 4):
+        weight_ref[(zl_mine - t) & 3] = refs[t - 1][...].astype(F32).reshape(2, 32, 512)
 
 
 def field_kernel(factor, step, in_ref, *rest):
     if step == 0:
-        field_hbm, table_ref, out, sem = rest
+        field_hbm, table_ref, rows, out, sem = rest
         points = table_ref.shape[0]
         offset = (lax.axis_index("y") * 4 + lax.axis_index("zl")) * points
         table_ref[...] = table_of(points, True, offset)
     else:
-        table_ref, _, field_hbm, out, sem = rest
-    blocks = in_ref[...].astype(F32).reshape(512, 128).astype(BF16)
+        table_ref, _, field_hbm, rows, out, sem = rest
+    rows[...] = in_ref[...].astype(F32).reshape(512, 128)
     b = (lax.axis_index("y") - step) & 3
     copies = []
     for h in range(2):
-        modes = []
-        for q in (2 * h, 2 * h + 1):
-            row = lax.broadcasted_iota(jnp.int32, (128, 512), 0)
-            col = lax.broadcasted_iota(jnp.int32, (128, 512), 1)
-            source = ((row & 63) << 3) + (row >> 6) + 2 * q
-            modes.append(dot(jnp.where(source == col, 1.0, 0.0).astype(BF16), blocks))
+        modes = [
+            jnp.concatenate([rows[pl.ds(2 * q + p, 64, stride=8), :] for p in range(2)], axis=0)
+            for q in (2 * h, 2 * h + 1)
+        ]
         modes = jnp.concatenate(modes, axis=1).astype(BF16)
         out[h] = (dot(table_ref[...], modes) * factor).astype(BF16)
         lanes = slice(256 * h, 256 * h + 256)
@@ -235,7 +215,7 @@
             out_specs=[vmem] * n,
             out_shape=[block(256, 512)] * n,
             scratch_shapes=[pltpu.VMEM((n, 512, 512), BF16)] * 3
-            + [pltpu.VMEM((128, 512), BF16), pltpu.SemaphoreType.DMA((3, n))],
+            + [pltpu.VMEM((128, 512), BF16), pltpu.SemaphoreType.DMA((3, n, 2))],
             compiler_params=pltpu.CompilerParams(vmem_limit_bytes=SPECTRA_VMEM),
             cost_estimate=cost(2**28 * n, 2**22 * n),
             name="spectra",
@@ -247,9 +227,10 @@
     one, two, three = shifted(one, "y", 1), shifted(two, "y", 2), shifted(three, "y", 3)
     send = pl.pallas_call(
         sum_y_kernel,
-        in_specs=[vmem] * 4,
+        in_specs=[hbm] + [vmem] * 3,
         out_specs=vmem,
         out_shape=block(64, 8, 256),
+        scratch_shapes=[pltpu.VMEM((256, 512), BF16), pltpu.SemaphoreType.DMA],
         compiler_params=params,
         name="sum_y",
     )(own, one, two, three)
@@ -266,27 +247,19 @@
     )(got, mine)
     sides = [sides[0]] + [shifted(sides[t], "y", t) for t in range(1, 4)]
     got = lax.all_to_all(send.reshape(64, 8, 128), OTHERS, 0, 0, tiled=True)
-    sides = pl.pallas_call(
-        relay_kernel,
+    own_weight, *sides = pl.pallas_call(
+        weight_kernel,
         in_specs=[vmem] * 4,
         out_specs=[vmem] * 4,
-        out_shape=[block(136, 512)] * 4,
-        scratch_shapes=[pltpu.VMEM((4, 8, 512), F32)],
+        out_shape=[jax.ShapeDtypeStruct((2, 32, 512), F32)] + [block(64, 512)] * 3,
+        scratch_shapes=[pltpu.VMEM((2, 4, 32, 512), F32)],
         compiler_params=params,
         cost_estimate=cost(2**26, 2**20),
-        name="relay",
-    )(*sides)
-    sides = [sides[0]] + [shifted(sides[t], "zl", t) for t in range(1, 4)]
-    weight_grad = pl.pallas_call(
-        weight_kernel,
-        in_specs=[vmem] * 4,
-        out_specs=vmem,
-        out_shape=jax.ShapeDtypeStruct((4, 2, 32, 512), F32),
-        compiler_params=params,
-        cost_estimate=cost(2**27, 2**21),
         name="weight",
     )(*sides)
-    scratch = [pltpu.VMEM((2, 512, 256), BF16), pltpu.SemaphoreType.DMA((2,))]
+    sides = [shifted(sides[t - 1], "zl", t) for t in range(1, 4)]
+    scratch = [pltpu.VMEM((512, 128), F32), pltpu.VMEM((2, 512, 256), BF16)]
+    scratch = scratch + [pltpu.SemaphoreType.DMA((2,))]
     received = {t: shifted(got, "y", t) for t in (2, 1, 3)}
     field_grad, table = pl.pallas_call(
         functools.partial(field_kernel, factor, 0),
@@ -298,6 +271,15 @@
         cost_estimate=cost(2**27, 2**20),
         name="field",
     )(got)
+    weight_grad = pl.pallas_call(
+        place_kernel,
+        in_specs=[hbm] + [vmem] * 4,
+        out_specs=vmem,
+        out_shape=jax.ShapeDtypeStruct((4, 2, 32, 512), F32),
+        compiler_params=params,
+        cost_estimate=cost(2**20, 2**20),
+        name="place",
+    )(table, own_weight, *sides)
     for t in (1, 3, 2):
         field_grad = pl.pallas_call(
             functools.partial(field_kernel, factor, t),

time: 83.8 us -> 79.4 us (0.947); the launches traced: 82.4 us -> 79.1 us
  waiting for transfers between devices: 22.7 us -> 20.6 us
  Pallas kernels: 19.3 us -> 17.8 us
    ppermute x12, waiting for transfers between devices: 11.1 us -> 7.27 us  [shifted(): lax.ppermute(value, axis, [(i, (i + distance) % 4) for i in range(4)])]
    all_to_all x1, waiting for transfers between devices: 0.01 us -> 1.74 us  [shards(): got = lax.all_to_all(send.reshape(64, 8, 128), OTHERS, 0, 0, tiled=True)]
    pallas_call x3, Pallas kernels: 4.57 us -> 3.38 us  [shards(): pl.pallas_call(functools.partial(field_kernel, factor, t), in_specs=[vmem...]
  transfers between devices with their start and end apart: 14 -> 14, of which waited for: 5 -> 7; matrix products, arithmetic and copies ran while one was open for 2% -> 2% of each run, Pallas kernels for 15% -> 14%
where the time goes in v5:
time: 79.4 us; the launch traced here: 79.1 us
  starting transfers between devices  37.5 us (47%)
  waiting for transfers between devices  20.6 us (26%)
  Pallas kernels  17.8 us (22%)
  local copies, waits for them, and re-layouts  2.25 us (3%)
  between operations  0.91 us (1%)
    ppermute x12, starting transfers between devices, shifted(): lax.ppermute(value, axis, [(i, (i + distance) % 4) for i in range(4)])  19.1 us
    all_to_all x1, starting transfers between devices, shards(): got = lax.all_to_all(send, OTHERS, 0, 0, tiled=True)  13.4 us
    all_to_all x1, waiting for transfers between devices, shards(): got = lax.all_to_all(send, OTHERS, 0, 0, tiled=True)  11.5 us
    pallas_call x3, Pallas kernels, spectra(): pl.pallas_call(functools.partial(spectra_kernel, steps), in_specs=[hbm] *...  9.05 us
    ppermute x12, waiting for transfers between devices, shifted(): lax.ppermute(value, axis, [(i, (i + distance) % 4) for i in range(4)])  7.27 us
    all_to_all x1, starting transfers between devices, shards(): got = lax.all_to_all(send.reshape(64, 8, 128), OTHERS, 0, 0, tiled=True)  5.09 us
    pallas_call x3, Pallas kernels, shards(): pl.pallas_call(functools.partial(field_kernel, factor, t), in_specs=[vmem...  3.38 us
    all_to_all x1, waiting for transfers between devices, shards(): got = lax.all_to_all(send.reshape(64, 8, 128), OTHERS, 0, 0, tiled=True)  1.74 us
  transfers between devices with their start and end apart: 14, of which 7 were waited for; matrix products, arithmetic and copies ran while one was open for 2% of the time, Pallas kernels for 14%

profile of v5, /device:TPU:1, one launch (start us, length us, event | category | flops | bytes accessed | tf_op | source)
XLA Modules:
  0.0 79.1 jit_solution(355347061323512931)
XLA Ops:
  0.6 2.7 %spectra.3._ = bf16[256,512]{1,0:T(8,128)(2,1)} custom-call(bf16[4,512,512]{2,1,0:T(8,128)(2,1)} %fields_hbm.5, bf16[4,512,512]{2,1,0:T(8,128)(2,1)} %pre_hbm.5, bf16[4,512,512]{2,1,0:T(8,128)(2,1)} %cot_hbm.5, bf16[4,512,512]{2,1,0:T(8,128)(2,1)} %fields_hbm.5), custom_call_target="tpu_custom_call" | custom-call | flops 268435456 | bytes 4194304 | tf_op jit(solution)/shard_map/spectra/pallas_call | solution.py:212
  3.4 3.8 %collective-permute-start.1 = (bf16[256,512]{1,0:T(8,128)(2,1)}, bf16[256,512]{1,0:T(8,128)(2,1)S(1)}, u32[]{:S(2)}, u32[]{:S(2)}) collective-permute-start(bf16[256,512]{1,0:T(8,128)(2,1)} %spectra.3._), channel_id=1, source_target_pairs={{0,128},{64,192},{128,0},{192,64},{1,129},{65,193},{129,1},{193,65... | collective-permute-start | bytes 786440 | tf_op jit(solution)/shard_map/ppermute | solution.py:193
  7.2 3.6 %spectra.4 = (bf16[256,512]{1,0:T(8,128)(2,1)}, bf16[256,512]{1,0:T(8,128)(2,1)}) custom-call(bf16[4,512,512]{2,1,0:T(8,128)(2,1)} %fields_hbm.5, bf16[4,512,512]{2,1,0:T(8,128)(2,1)} %pre_hbm.5, bf16[4,512,512]{2,1,0:T(8,128)(2,1)} %cot_hbm.5, bf16[256,512]{1,0:T(8,128)(2,1)} %spectra.3._), custom_call_target="tpu_custom_call" | custom-call | flops 536870912 | bytes 8388608 | tf_op jit(solution)/shard_map/spectra/pallas_call | solution.py:212
  10.8 0.5 collective-permute-start
  11.3 2.3 %collective-permute-start.2 = (bf16[256,512]{1,0:T(8,128)(2,1)}, bf16[256,512]{1,0:T(8,128)(2,1)S(1)}, u32[]{:S(2)}, u32[]{:S(2)}) collective-permute-start(bf16[256,512]{1,0:T(8,128)(2,1)} %get-tuple-element.16), channel_id=1, source_target_pairs={{0,192},{64,0},{128,64},{192,128},{1,193},{65,1},{129,65},{193,129... | collective-permute-start | bytes 786440 | tf_op jit(solution)/shard_map/ppermute | solution.py:193
  13.6 2.7 %spectra.5.own_hbm = bf16[256,512]{1,0:T(8,128)(2,1)} custom-call(bf16[4,512,512]{2,1,0:T(8,128)(2,1)} %fields_hbm.5, bf16[4,512,512]{2,1,0:T(8,128)(2,1)} %pre_hbm.5, bf16[4,512,512]{2,1,0:T(8,128)(2,1)} %cot_hbm.5, bf16[256,512]{1,0:T(8,128)(2,1)} %get-tuple-element.15._), custom_call_target="tpu_custom_call" | custom-call | flops 268435456 | bytes 4194304 | tf_op jit(solution)/shard_map/spectra/pallas_call | solution.py:212
  16.3 2.9 %collective-permute-done.one_ref = bf16[256,512]{1,0:T(8,128)(2,1)S(1)} collective-permute-done((bf16[256,512]{1,0:T(8,128)(2,1)}, bf16[256,512]{1,0:T(8,128)(2,1)S(1)}, u32[]{:S(2)}, u32[]{:S(2)}) %collective-permute-start) | collective-permute-done | bytes 262176 | tf_op jit(solution)/shard_map/ppermute | solution.py:193
  19.2 0.9 %copy-done = bf16[256,512]{1,0:T(8,128)(2,1)S(1)} copy-done((bf16[256,512]{1,0:T(8,128)(2,1)S(1)}, bf16[256,512]{1,0:T(8,128)(2,1)}, u32[]{:S(2)}) %copy-start) | copy-done | bytes 262168
  20.1 1.3 %sum_y.1 = bf16[64,8,256]{2,1,0:T(8,128)(2,1)} custom-call(bf16[256,512]{1,0:T(8,128)(2,1)S(1)} %copy-done, bf16[256,512]{1,0:T(8,128)(2,1)S(1)} %collective-permute-done.one_ref, bf16[256,512]{1,0:T(8,128)(2,1)S(1)} %collective-permute-done.1.two_ref, bf16[256,512]{1,0:T(8,128)(2,1)S(1)} %collective-permute-done.2.three_ref), custom_call_target="tpu_custom_call" | custom-call | tf_op jit(solution)/shard_map/sum_y/pallas_call | solution.py:228
  21.4 13.4 %all-to-all-start = ((bf16[64,8,256]{2,1,0:T(8,128)(2,1)}), bf16[64,8,256]{2,1,0:T(8,128)(2,1)S(1)}, u32[]{:S(2)}, u32[]{:S(2)}) async-start(bf16[64,8,256]{2,1,0:T(8,128)(2,1)} %sum_y.1), calls=%async_computation | async-start | bytes 524288 | tf_op jit(solution)/shard_map/all_to_all | solution.py:237
  34.8 1.3 %dynamic-slice_bitcast_fusion.w_ref = bf16[2,512,512]{2,1,0:T(8,128)(2,1)S(1)} fusion(bf16[4,2,512,512]{3,2,1,0:T(8,128)(2,1)} %param.7, s32[]{:T(128)S(6)} %select_n.4), kind=kLoop, calls=%fused_computation | loop fusion | bytes 2097156 | tf_op jit(solution)/shard_map/jit(dynamic_index_in_dim)/squeeze | solution.py:238
  36.1 11.5 %all-to-all-done.in_ref = bf16[64,8,256]{2,1,0:T(8,128)(2,1)S(1)} async-done(((bf16[64,8,256]{2,1,0:T(8,128)(2,1)}), bf16[64,8,256]{2,1,0:T(8,128)(2,1)S(1)}, u32[]{:S(2)}, u32[]{:S(2)}) %all-to-all-start) | async-done | bytes 262176 | tf_op jit(solution)/shard_map/all_to_all | solution.py:237
  47.6 1.5 %modes.1 = (bf16[16,4,8,128]{3,2,1,0:T(8,128)(2,1)}, bf16[40,512]{1,0:T(8,128)(2,1)S(1)}, bf16[40,512]{1,0:T(8,128)(2,1)S(1)}, bf16[40,512]{1,0:T(8,128)(2,1)S(1)}, bf16[40,512]{1,0:T(8,128)(2,1)S(1)}) custom-call(bf16[64,8,256]{2,1,0:T(8,128)(2,1)S(1)} %all-to-all-done.in_ref, bf16[2,512,512]{2,1,0:T(8,128)(2,1)S(1)} %dynamic-slice_bitcast_fusion.w_ref), custom_call_target="tpu_custom_call" | custom-call | tf_op jit(solution)/shard_map/modes/pallas_call | solution.py:239
  49.1 5.1 %all-to-all-start.1 = ((bf16[64,8,128]{2,1,0:T(8,128)(2,1)}), bf16[64,8,128]{2,1,0:T(8,128)(2,1)S(1)}, u32[]{:S(2)}, u32[]{:S(2)}) async-start(bf16[64,8,128]{2,1,0:T(8,128)(2,1)} %bitcast.1), calls=%async_computation.1 | async-start | bytes 262144 | tf_op jit(solution)/shard_map/all_to_all | solution.py:249
  54.2 0.8 collective-permute-start.6
  55.0 3.2 %collective-permute-start.7 = (bf16[40,512]{1,0:T(8,128)(2,1)S(1)}, bf16[40,512]{1,0:T(8,128)(2,1)S(1)}, u32[]{:S(2)}, u32[]{:S(2)}) collective-permute-start(bf16[40,512]{1,0:T(8,128)(2,1)S(1)} %get-tuple-element.22), channel_id=1, source_target_pairs={{0,128},{64,192},{128,0},{192,64},{1,129},{65,193},{129,1},{193,65... | collective-permute-start | bytes 122888 | tf_op jit(solution)/shard_map/ppermute | solution.py:193
  58.1 0.4 collective-permute-start.8
  58.7 1.6 %collective-permute-done.7.refs_2_ = bf16[40,512]{1,0:T(8,128)(2,1)S(1)} collective-permute-done((bf16[40,512]{1,0:T(8,128)(2,1)S(1)}, bf16[40,512]{1,0:T(8,128)(2,1)S(1)}, u32[]{:S(2)}, u32[]{:S(2)}) %collective-permute-start.7) | collective-permute-done | bytes 40992 | tf_op jit(solution)/shard_map/ppermute | solution.py:193
  60.3 1.0 %collective-permute-done.8.refs_3_ = bf16[40,512]{1,0:T(8,128)(2,1)S(1)} collective-permute-done((bf16[40,512]{1,0:T(8,128)(2,1)S(1)}, bf16[40,512]{1,0:T(8,128)(2,1)S(1)}, u32[]{:S(2)}, u32[]{:S(2)}) %collective-permute-start.8) | collective-permute-done | bytes 40992 | tf_op jit(solution)/shard_map/ppermute | solution.py:193
  61.7 1.6 %collective-permute-start.9 = (bf16[64,512]{1,0:T(8,128)(2,1)S(1)}, bf16[64,512]{1,0:T(8,128)(2,1)S(1)}, u32[]{:S(2)}, u32[]{:S(2)}) collective-permute-start(bf16[64,512]{1,0:T(8,128)(2,1)S(1)} %get-tuple-element.25), channel_id=1, source_target_pairs={{0,16},{16,32},{32,48},{48,0},{1,17},{17,33},{33,49},{49,1},{2,18}... | collective-permute-start | bytes 196616 | tf_op jit(solution)/shard_map/ppermute | solution.py:193
  63.3 1.7 %all-to-all-done.1.in_ref = bf16[64,8,128]{2,1,0:T(8,128)(2,1)S(1)} async-done(((bf16[64,8,128]{2,1,0:T(8,128)(2,1)}), bf16[64,8,128]{2,1,0:T(8,128)(2,1)S(1)}, u32[]{:S(2)}, u32[]{:S(2)}) %all-to-all-start.1) | async-done | bytes 131104 | tf_op jit(solution)/shard_map/all_to_all | solution.py:249
  65.1 0.7 collective-permute-start.5
  65.8 2.0 %collective-permute-start.4 = (bf16[64,8,128]{2,1,0:T(8,128)(2,1)S(1)}, bf16[64,8,128]{2,1,0:T(8,128)(2,1)S(1)}, u32[]{:S(2)}, u32[]{:S(2)}) collective-permute-start(bf16[64,8,128]{2,1,0:T(8,128)(2,1)S(1)} %all-to-all-done.1.in_ref), channel_id=1, source_target_pairs={{0,192},{64,0},{128,64},{192,128},{1,193},{65,1},{129,65},{193,129... | collective-permute-start | bytes 393224 | tf_op jit(solution)/shard_map/ppermute | solution.py:193
  67.8 1.2 %collective-permute-start.3 = (bf16[64,8,128]{2,1,0:T(8,128)(2,1)S(1)}, bf16[64,8,128]{2,1,0:T(8,128)(2,1)S(1)}, u32[]{:S(2)}, u32[]{:S(2)}) collective-permute-start(bf16[64,8,128]{2,1,0:T(8,128)(2,1)S(1)} %all-to-all-done.1.in_ref), channel_id=1, source_target_pairs={{0,128},{64,192},{128,0},{192,64},{1,129},{65,193},{129,1},{193,65... | collective-permute-start | bytes 393224 | tf_op jit(solution)/shard_map/ppermute | solution.py:193
  68.9 0.7 collective-permute-start.10
  69.6 1.9 %collective-permute-start.11 = (bf16[64,512]{1,0:T(8,128)(2,1)S(1)}, bf16[64,512]{1,0:T(8,128)(2,1)S(1)}, u32[]{:S(2)}, u32[]{:S(2)}) collective-permute-start(bf16[64,512]{1,0:T(8,128)(2,1)S(1)} %get-tuple-element.27), channel_id=1, source_target_pairs={{0,48},{16,0},{32,16},{48,32},{1,49},{17,1},{33,17},{49,33},{2,50}... | collective-permute-start | bytes 196616 | tf_op jit(solution)/shard_map/ppermute | solution.py:193
  71.6 1.4 %field.4 = (bf16[4,512,512]{2,1,0:T(8,128)(2,1)}, bf16[512,128]{1,0:T(8,128)(2,1)S(1)}) custom-call(bf16[64,8,128]{2,1,0:T(8,128)(2,1)S(1)} %all-to-all-done.1.in_ref), custom_call_target="tpu_custom_call" | custom-call | flops 134217728 | bytes 1048576 | tf_op jit(solution)/shard_map/field/pallas_call | solution.py:264
  73.0 1.6 %collective-permute-done.10.refs_1_ = bf16[64,512]{1,0:T(8,128)(2,1)S(1)} collective-permute-done((bf16[64,512]{1,0:T(8,128)(2,1)S(1)}, bf16[64,512]{1,0:T(8,128)(2,1)S(1)}, u32[]{:S(2)}, u32[]{:S(2)}) %collective-permute-start.10) | collective-permute-done | bytes 65568 | tf_op jit(solution)/shard_map/ppermute | solution.py:193
  74.6 0.8 %place.1 = f32[4,2,32,512]{3,2,1,0:T(8,128)} custom-call(bf16[512,128]{1,0:T(8,128)(2,1)S(1)} %get-tuple-element.18.rest_0_._, f32[2,32,512]{2,1,0:T(8,128)S(1)} %get-tuple-element.24.own_ref, bf16[64,512]{1,0:T(8,128)(2,1)S(1)} %collective-permute-done.9.refs_0_, bf16[64,512]{1,0:T(8,128)(2,1)S(1)} %collective-permute-done.10.refs_1_, ...), custom_call_target="tpu_custom_call" | custom-call | flops 1048576 | bytes 1048576 | tf_op jit(solution)/shard_map/place/pallas_call | solution.py:274
  75.5 1.1 %field.5.rest_1_ = bf16[4,512,512]{2,1,0:T(8,128)(2,1)} custom-call(bf16[64,8,128]{2,1,0:T(8,128)(2,1)S(1)} %collective-permute-done.5.in_ref, bf16[512,128]{1,0:T(8,128)(2,1)S(1)} %get-tuple-element.18.rest_0_._, bf16[4,512,512]{2,1,0:T(8,128)(2,1)} %get-tuple-element.19.rest_1_), custom_call_target="tpu_custom_call", output_to_operand_aliasing={{}: (2, {})} | custom-call | flops 134217728 | bytes 1048576 | tf_op jit(solution)/shard_map/field/pallas_call | solution.py:284
  76.6 1.1 %field.6.rest_1_ = bf16[4,512,512]{2,1,0:T(8,128)(2,1)} custom-call(bf16[64,8,128]{2,1,0:T(8,128)(2,1)S(1)} %collective-permute-done.4.in_ref, bf16[512,128]{1,0:T(8,128)(2,1)S(1)} %get-tuple-element.18.rest_0_._, bf16[4,512,512]{2,1,0:T(8,128)(2,1)} %field.5.rest_1_), custom_call_target="tpu_custom_call", output_to_operand_aliasing={{}: (2, {})} | custom-call | flops 134217728 | bytes 1048576 | tf_op jit(solution)/shard_map/field/pallas_call | solution.py:284
  77.8 1.1 %field.7 = bf16[4,512,512]{2,1,0:T(8,128)(2,1)} custom-call(bf16[64,8,128]{2,1,0:T(8,128)(2,1)S(1)} %collective-permute-done.3.in_ref, bf16[512,128]{1,0:T(8,128)(2,1)S(1)} %get-tuple-element.18.rest_0_._, bf16[4,512,512]{2,1,0:T(8,128)(2,1)} %field.6.rest_1_), custom_call_target="tpu_custom_call", output_to_operand_aliasing={{}: (2, {})} | custom-call | flops 134217728 | bytes 1048576 | tf_op jit(solution)/shard_map/field/pallas_call | solution.py:284
  (10 shorter events, 0.5 us)
Async XLA Ops:
  3.4 15.8 %collective-permute-start.1 = (bf16[256,512]{1,0:T(8,128)(2,1)}, bf16[256,512]{1,0:T(8,128)(2,1)S(1)}, u32[]{:S(2)}, u32[]{:S(2)}) collective-permute-start(bf16[256,512]{1,0:T(8,128)(2,1)} %spectra.3._), channel_id=1, source_target_pairs={{0,128},{64,192},{128,0},{192,64},{1,129},{65,193},{129,1},{193,65... | collective-permute-start | bytes 786440 | tf_op jit(solution)/shard_map/ppermute | solution.py:193
  10.8 8.4 %collective-permute-start = (bf16[256,512]{1,0:T(8,128)(2,1)}, bf16[256,512]{1,0:T(8,128)(2,1)S(1)}, u32[]{:S(2)}, u32[]{:S(2)}) collective-permute-start(bf16[256,512]{1,0:T(8,128)(2,1)} %get-tuple-element.15._), channel_id=1, source_target_pairs={{0,64},{64,128},{128,192},{192,0},{1,65},{65,129},{129,193},{193,1... | collective-permute-start | bytes 786440 | tf_op jit(solution)/shard_map/ppermute | solution.py:193
  11.3 7.9 %collective-permute-start.2 = (bf16[256,512]{1,0:T(8,128)(2,1)}, bf16[256,512]{1,0:T(8,128)(2,1)S(1)}, u32[]{:S(2)}, u32[]{:S(2)}) collective-permute-start(bf16[256,512]{1,0:T(8,128)(2,1)} %get-tuple-element.16), channel_id=1, source_target_pairs={{0,192},{64,0},{128,64},{192,128},{1,193},{65,1},{129,65},{193,129... | collective-permute-start | bytes 786440 | tf_op jit(solution)/shard_map/ppermute | solution.py:193
  19.2 1.0 %copy-start = (bf16[256,512]{1,0:T(8,128)(2,1)S(1)}, bf16[256,512]{1,0:T(8,128)(2,1)}, u32[]{:S(2)}) copy-start(bf16[256,512]{1,0:T(8,128)(2,1)} %spectra.5.own_hbm) | copy-start | bytes 786436
  21.4 26.2 %all-to-all-start = ((bf16[64,8,256]{2,1,0:T(8,128)(2,1)}), bf16[64,8,256]{2,1,0:T(8,128)(2,1)S(1)}, u32[]{:S(2)}, u32[]{:S(2)}) async-start(bf16[64,8,256]{2,1,0:T(8,128)(2,1)} %sum_y.1), calls=%async_computation | async-start | bytes 524288 | tf_op jit(solution)/shard_map/all_to_all | solution.py:237
  49.1 16.0 %all-to-all-start.1 = ((bf16[64,8,128]{2,1,0:T(8,128)(2,1)}), bf16[64,8,128]{2,1,0:T(8,128)(2,1)S(1)}, u32[]{:S(2)}, u32[]{:S(2)}) async-start(bf16[64,8,128]{2,1,0:T(8,128)(2,1)} %bitcast.1), calls=%async_computation.1 | async-start | bytes 262144 | tf_op jit(solution)/shard_map/all_to_all | solution.py:249
  54.2 4.4 %collective-permute-start.6 = (bf16[40,512]{1,0:T(8,128)(2,1)S(1)}, bf16[40,512]{1,0:T(8,128)(2,1)S(1)}, u32[]{:S(2)}, u32[]{:S(2)}) collective-permute-start(bf16[40,512]{1,0:T(8,128)(2,1)S(1)} %get-tuple-element.21), channel_id=1, source_target_pairs={{0,64},{64,128},{128,192},{192,0},{1,65},{65,129},{129,193},{193,1... | collective-permute-start | bytes 122888 | tf_op jit(solution)/shard_map/ppermute | solution.py:193
  55.0 5.3 %collective-permute-start.7 = (bf16[40,512]{1,0:T(8,128)(2,1)S(1)}, bf16[40,512]{1,0:T(8,128)(2,1)S(1)}, u32[]{:S(2)}, u32[]{:S(2)}) collective-permute-start(bf16[40,512]{1,0:T(8,128)(2,1)S(1)} %get-tuple-element.22), channel_id=1, source_target_pairs={{0,128},{64,192},{128,0},{192,64},{1,129},{65,193},{129,1},{193,65... | collective-permute-start | bytes 122888 | tf_op jit(solution)/shard_map/ppermute | solution.py:193
  58.1 3.1 %collective-permute-start.8 = (bf16[40,512]{1,0:T(8,128)(2,1)S(1)}, bf16[40,512]{1,0:T(8,128)(2,1)S(1)}, u32[]{:S(2)}, u32[]{:S(2)}) collective-permute-start(bf16[40,512]{1,0:T(8,128)(2,1)S(1)} %get-tuple-element.23), channel_id=1, source_target_pairs={{0,192},{64,0},{128,64},{192,128},{1,193},{65,1},{129,65},{193,129... | collective-permute-start | bytes 122888 | tf_op jit(solution)/shard_map/ppermute | solution.py:193
  61.7 7.9 %collective-permute-start.9 = (bf16[64,512]{1,0:T(8,128)(2,1)S(1)}, bf16[64,512]{1,0:T(8,128)(2,1)S(1)}, u32[]{:S(2)}, u32[]{:S(2)}) collective-permute-start(bf16[64,512]{1,0:T(8,128)(2,1)S(1)} %get-tuple-element.25), channel_id=1, source_target_pairs={{0,16},{16,32},{32,48},{48,0},{1,17},{17,33},{33,49},{49,1},{2,18}... | collective-permute-start | bytes 196616 | tf_op jit(solution)/shard_map/ppermute | solution.py:193
  65.1 10.4 %collective-permute-start.5 = (bf16[64,8,128]{2,1,0:T(8,128)(2,1)S(1)}, bf16[64,8,128]{2,1,0:T(8,128)(2,1)S(1)}, u32[]{:S(2)}, u32[]{:S(2)}) collective-permute-start(bf16[64,8,128]{2,1,0:T(8,128)(2,1)S(1)} %all-to-all-done.1.in_ref), channel_id=1, source_target_pairs={{0,64},{64,128},{128,192},{192,0},{1,65},{65,129},{129,193},{193,1... | collective-permute-start | bytes 393224 | tf_op jit(solution)/shard_map/ppermute | solution.py:193
  65.8 10.8 %collective-permute-start.4 = (bf16[64,8,128]{2,1,0:T(8,128)(2,1)S(1)}, bf16[64,8,128]{2,1,0:T(8,128)(2,1)S(1)}, u32[]{:S(2)}, u32[]{:S(2)}) collective-permute-start(bf16[64,8,128]{2,1,0:T(8,128)(2,1)S(1)} %all-to-all-done.1.in_ref), channel_id=1, source_target_pairs={{0,192},{64,0},{128,64},{192,128},{1,193},{65,1},{129,65},{193,129... | collective-permute-start | bytes 393224 | tf_op jit(solution)/shard_map/ppermute | solution.py:193
  67.8 10.0 %collective-permute-start.3 = (bf16[64,8,128]{2,1,0:T(8,128)(2,1)S(1)}, bf16[64,8,128]{2,1,0:T(8,128)(2,1)S(1)}, u32[]{:S(2)}, u32[]{:S(2)}) collective-permute-start(bf16[64,8,128]{2,1,0:T(8,128)(2,1)S(1)} %all-to-all-done.1.in_ref), channel_id=1, source_target_pairs={{0,128},{64,192},{128,0},{192,64},{1,129},{65,193},{129,1},{193,65... | collective-permute-start | bytes 393224 | tf_op jit(solution)/shard_map/ppermute | solution.py:193
  68.9 5.7 %collective-permute-start.10 = (bf16[64,512]{1,0:T(8,128)(2,1)S(1)}, bf16[64,512]{1,0:T(8,128)(2,1)S(1)}, u32[]{:S(2)}, u32[]{:S(2)}) collective-permute-start(bf16[64,512]{1,0:T(8,128)(2,1)S(1)} %get-tuple-element.26), channel_id=1, source_target_pairs={{0,32},{16,48},{32,0},{48,16},{1,33},{17,49},{33,1},{49,17},{2,34}... | collective-permute-start | bytes 196616 | tf_op jit(solution)/shard_map/ppermute | solution.py:193
  69.6 5.0 %collective-permute-start.11 = (bf16[64,512]{1,0:T(8,128)(2,1)S(1)}, bf16[64,512]{1,0:T(8,128)(2,1)S(1)}, u32[]{:S(2)}, u32[]{:S(2)}) collective-permute-start(bf16[64,512]{1,0:T(8,128)(2,1)S(1)} %get-tuple-element.27), channel_id=1, source_target_pairs={{0,48},{16,0},{32,16},{48,32},{1,49},{17,1},{33,17},{49,33},{2,50}... | collective-permute-start | bytes 196616 | tf_op jit(solution)/shard_map/ppermute | solution.py:193

commit v6 on v5

--- a/solution.py
+++ b/solution.py
@@ -69,24 +69,26 @@
 
 
 def spectra_kernel(steps, fields_hbm, pre_hbm, cot_hbm, _, *rest):
-    out_refs, (fields, pre, cot, table, sems) = rest[: len(steps)], rest[len(steps) :]
+    n = len(steps)
+    out_hbms, out_refs, (fields, pre, cot, table, sems, out_sems) = rest[:n], rest[n : 2 * n], rest[2 * n :]
     y = lax.axis_index("y")
 
     def copies(i, h):
         b = (y + steps[i]) & 3
         at = slice(256 * h, 256 * h + 256)
         return [
-            pltpu.make_async_copy(hbm.at[b, :, at], vmem.at[i, :, at], sems.at[n, i, h])
-            for n, (hbm, vmem) in enumerate(((pre_hbm, pre), (cot_hbm, cot), (fields_hbm, fields)))
+            pltpu.make_async_copy(hbm.at[b, :, at], vmem.at[i, :, at], sems.at[j, i, h])
+            for j, (hbm, vmem) in enumerate(((pre_hbm, pre), (cot_hbm, cot), (fields_hbm, fields)))
         ]
 
-    for i in range(len(steps)):
+    for i in range(n):
         for h in range(2):
             for copy in copies(i, h):
                 copy.start()
     points = table.shape[1]
     table[...] = table_of(points, False, (y * 4 + lax.axis_index("zl")) * points)
-    for i in range(len(steps)):
+    sent = []
+    for i in range(n):
         for h in range(2):
             for copy in copies(i, h):
                 copy.wait()
@@ -94,6 +96,11 @@
             slopes = cot[i, :, lanes].astype(F32) * gelu_slope(pre[i, :, lanes].astype(F32))
             out_refs[i][0:128, lanes] = dot(table[...], slopes.astype(BF16)).astype(BF16)
             out_refs[i][128:256, lanes] = dot(table[...], fields[i, :, lanes]).astype(BF16)
+            source, target = out_refs[i].at[:, lanes], out_hbms[i].at[:, lanes]
+            sent.append(pltpu.make_async_copy(source, target, out_sems.at[i, h]))
+            sent[-1].start()
+    for copy in sent:
+        copy.wait()
 
 
 def sum_y_kernel(own_hbm, one_ref, two_ref, three_ref, out_ref, own, sem):
@@ -156,22 +163,7 @@
         send_refs[t - 1][...] = result[:, (zl_mine + t) & 3].reshape(64, 512).astype(BF16)
 
 
-def place_kernel(_, own_ref, *refs):
-    weight_ref = refs[3]
-    zl_mine = lax.axis_index("zl")
-    weight_ref[zl_mine] = own_ref[...]
-    for t in range(1, 4):
-        weight_ref[(zl_mine - t) & 3] = refs[t - 1][...].astype(F32).reshape(2, 32, 512)
-
-
-def field_kernel(factor, step, in_ref, *rest):
-    if step == 0:
-        field_hbm, table_ref, rows, out, sem = rest
-        points = table_ref.shape[0]
-        offset = (lax.axis_index("y") * 4 + lax.axis_index("zl")) * points
-        table_ref[...] = table_of(points, True, offset)
-    else:
-        table_ref, _, field_hbm, rows, out, sem = rest
+def transform(factor, step, in_ref, table_ref, rows, out, field_hbm, sem):
     rows[...] = in_ref[...].astype(F32).reshape(512, 128)
     b = (lax.axis_index("y") - step) & 3
     copies = []
@@ -185,6 +177,30 @@
         lanes = slice(256 * h, 256 * h + 256)
         copies.append(pltpu.make_async_copy(out.at[h], field_hbm.at[b, :, lanes], sem.at[h]))
         copies[-1].start()
+    return copies
+
+
+def own_field_kernel(factor, in_ref, field_hbm, table_ref, rows, out, sem):
+    points = table_ref.shape[0]
+    offset = (lax.axis_index("y") * 4 + lax.axis_index("zl")) * points
+    table_ref[...] = table_of(points, True, offset)
+    for copy in transform(factor, 0, in_ref, table_ref, rows, out, field_hbm, sem):
+        copy.wait()
+
+
+def last_kernel(factor, *refs):
+    in_refs, table_ref, own_ref, weight_in = refs[:3], refs[3], refs[4], refs[5:8]
+    field_hbm, weight_hbm, rows, out, weights, sem, weight_sem = refs[9:]
+    zl_mine = lax.axis_index("zl")
+    copies = [pltpu.make_async_copy(own_ref, weight_hbm.at[zl_mine], weight_sem.at[0])]
+    copies[0].start()
+    for t in range(1, 4):
+        weights[t - 1] = weight_in[t - 1][...].astype(F32).reshape(2, 32, 512)
+        target = weight_hbm.at[(zl_mine - t) & 3]
+        copies.append(pltpu.make_async_copy(weights.at[t - 1], target, weight_sem.at[t]))
+        copies[-1].start()
+    for i, t in enumerate((1, 3, 2)):
+        copies += transform(factor, t, in_refs[i], table_ref, rows.at[i], out.at[i], field_hbm, sem.at[i])
     for copy in copies:
         copy.wait()
 
@@ -212,10 +228,12 @@
         return pl.pallas_call(
             functools.partial(spectra_kernel, steps),
             in_specs=[hbm] * 4,
-            out_specs=[vmem] * n,
+            out_specs=[hbm] * n,
             out_shape=[block(256, 512)] * n,
-            scratch_shapes=[pltpu.VMEM((n, 512, 512), BF16)] * 3
-            + [pltpu.VMEM((128, 512), BF16), pltpu.SemaphoreType.DMA((3, n, 2))],
+            scratch_shapes=[pltpu.VMEM((256, 512), BF16)] * n
+            + [pltpu.VMEM((n, 512, 512), BF16)] * 3
+            + [pltpu.VMEM((128, 512), BF16), pltpu.SemaphoreType.DMA((3, n, 2))]
+            + [pltpu.SemaphoreType.DMA((n, 2))],
             compiler_params=pltpu.CompilerParams(vmem_limit_bytes=SPECTRA_VMEM),
             cost_estimate=cost(2**28 * n, 2**22 * n),
             name="spectra",
@@ -258,40 +276,37 @@
         name="weight",
     )(*sides)
     sides = [shifted(sides[t - 1], "zl", t) for t in range(1, 4)]
-    scratch = [pltpu.VMEM((512, 128), F32), pltpu.VMEM((2, 512, 256), BF16)]
-    scratch = scratch + [pltpu.SemaphoreType.DMA((2,))]
-    received = {t: shifted(got, "y", t) for t in (2, 1, 3)}
+    received = [shifted(got, "y", t) for t in (1, 3, 2)]
     field_grad, table = pl.pallas_call(
-        functools.partial(field_kernel, factor, 0),
+        functools.partial(own_field_kernel, factor),
         in_specs=[vmem],
         out_specs=[hbm, vmem],
         out_shape=[block(4, 512, 512), block(512, 128)],
-        scratch_shapes=scratch,
+        scratch_shapes=[
+            pltpu.VMEM((512, 128), F32),
+            pltpu.VMEM((2, 512, 256), BF16),
+            pltpu.SemaphoreType.DMA((2,)),
+        ],
         compiler_params=params,
         cost_estimate=cost(2**27, 2**20),
-        name="field",
+        name="own_field",
     )(got)
-    weight_grad = pl.pallas_call(
-        place_kernel,
-        in_specs=[hbm] + [vmem] * 4,
-        out_specs=vmem,
-        out_shape=jax.ShapeDtypeStruct((4, 2, 32, 512), F32),
-        compiler_params=params,
-        cost_estimate=cost(2**20, 2**20),
-        name="place",
-    )(table, own_weight, *sides)
-    for t in (1, 3, 2):
-        field_grad = pl.pallas_call(
-            functools.partial(field_kernel, factor, t),
-            in_specs=[vmem, vmem, hbm],
-            out_specs=hbm,
-            out_shape=block(4, 512, 512),
-            scratch_shapes=scratch,
-            input_output_aliases={2: 0},
-            compiler_params=params,
-            cost_estimate=cost(2**27, 2**20),
-            name="field",
-        )(received[t], table, field_grad)
+    field_grad, weight_grad = pl.pallas_call(
+        functools.partial(last_kernel, factor),
+        in_specs=[vmem] * 8 + [hbm],
+        out_specs=[hbm, hbm],
+        out_shape=[block(4, 512, 512), jax.ShapeDtypeStruct((4, 2, 32, 512), F32)],
+        scratch_shapes=[
+            pltpu.VMEM((3, 512, 128), F32),
+            pltpu.VMEM((3, 2, 512, 256), BF16),
+            pltpu.VMEM((3, 2, 32, 512), F32),
+            pltpu.SemaphoreType.DMA((3, 2)),
+            pltpu.SemaphoreType.DMA((4,)),
+        ],
+        input_output_aliases={8: 0},
+        compiler_params=params,
+        name="last",
+    )(*received, table, own_weight, *sides, field_grad)
     return field_grad, jnp.swapaxes(weight_grad, 2, 3)
 
 

time: 79.4 us -> 77.6 us (0.977)
  waiting for transfers between devices: 20.6 us -> 24 us
  starting transfers between devices: 37.5 us -> 34.9 us
  Pallas kernels: 17.8 us -> 15.3 us
    ppermute x12, starting transfers between devices: 19.1 us -> 16.1 us  [shifted(): lax.ppermute(value, axis, [(i, (i + distance) % 4) for i in range(4)])]
    pallas_call x5 -> x2, Pallas kernels: 5.62 us -> 3.11 us  [the longest x1 1.72 us: shards(): pl.pallas_call(functools.partial(last_kernel, factor), in_specs=[vmem] *...]
    ppermute x12, waiting for transfers between devices: 7.27 us -> 9.34 us  [shifted(): lax.ppermute(value, axis, [(i, (i + distance) % 4) for i in range(4)])]
    all_to_all x1, waiting for transfers between devices: 1.74 us -> 3.15 us  [shards(): got = lax.all_to_all(send.reshape(64, 8, 128), OTHERS, 0, 0, tiled=True)]
  transfers between devices with their start and end apart: 14 -> 14, of which waited for: 7 -> 10; matrix products, arithmetic and copies ran while one was open for 2% -> 2% of each run, Pallas kernels for 14% -> 10%
where the time goes in v6:
time: 77.6 us; the launch traced here: 77.3 us
  starting transfers between devices  34.9 us (45%)
  waiting for transfers between devices  24 us (31%)
  Pallas kernels  15.3 us (20%)
  local copies, waits for them, and re-layouts  2.25 us (3%)
  between operations  0.89 us (1%)
    ppermute x12, starting transfers between devices, shifted(): lax.ppermute(value, axis, [(i, (i + distance) % 4) for i in range(4)])  16.1 us
    all_to_all x1, starting transfers between devices, shards(): got = lax.all_to_all(send, OTHERS, 0, 0, tiled=True)  13.7 us
    all_to_all x1, waiting for transfers between devices, shards(): got = lax.all_to_all(send, OTHERS, 0, 0, tiled=True)  11.5 us
    ppermute x12, waiting for transfers between devices, shifted(): lax.ppermute(value, axis, [(i, (i + distance) % 4) for i in range(4)])  9.34 us
    pallas_call x3, Pallas kernels, spectra(): pl.pallas_call(functools.partial(spectra_kernel, steps), in_specs=[hbm] *...  8.99 us
    all_to_all x1, starting transfers between devices, shards(): got = lax.all_to_all(send.reshape(64, 8, 128), OTHERS, 0, 0, tiled=True)  5.09 us
    all_to_all x1, waiting for transfers between devices, shards(): got = lax.all_to_all(send.reshape(64, 8, 128), OTHERS, 0, 0, tiled=True)  3.15 us
    pallas_call x1, Pallas kernels, shards(): pl.pallas_call(functools.partial(last_kernel, factor), in_specs=[vmem] *...  1.72 us
  transfers between devices with their start and end apart: 14, of which 10 were waited for; matrix products, arithmetic and copies ran while one was open for 2% of the time, Pallas kernels for 10%

profile of v6, /device:TPU:1, one launch (start us, length us, event | category | flops | bytes accessed | tf_op | source)
XLA Modules:
  0.0 77.3 jit_solution(8271804543989145274)
XLA Ops:
  0.6 2.7 %spectra.3._ = bf16[256,512]{1,0:T(8,128)(2,1)} custom-call(bf16[4,512,512]{2,1,0:T(8,128)(2,1)} %fields_hbm.5, bf16[4,512,512]{2,1,0:T(8,128)(2,1)} %pre_hbm.5, bf16[4,512,512]{2,1,0:T(8,128)(2,1)} %cot_hbm.5, bf16[4,512,512]{2,1,0:T(8,128)(2,1)} %fields_hbm.5), custom_call_target="tpu_custom_call" | custom-call | flops 268435456 | bytes 4194304 | tf_op jit(solution)/shard_map/spectra/pallas_call | solution.py:228
  3.3 3.8 %collective-permute-start.1 = (bf16[256,512]{1,0:T(8,128)(2,1)}, bf16[256,512]{1,0:T(8,128)(2,1)S(1)}, u32[]{:S(2)}, u32[]{:S(2)}) collective-permute-start(bf16[256,512]{1,0:T(8,128)(2,1)} %spectra.3._), channel_id=1, source_target_pairs={{0,128},{64,192},{128,0},{192,64},{1,129},{65,193},{129,1},{193,65... | collective-permute-start | bytes 786440 | tf_op jit(solution)/shard_map/ppermute | solution.py:209
  7.2 3.6 %spectra.4 = (bf16[256,512]{1,0:T(8,128)(2,1)}, bf16[256,512]{1,0:T(8,128)(2,1)}) custom-call(bf16[4,512,512]{2,1,0:T(8,128)(2,1)} %fields_hbm.5, bf16[4,512,512]{2,1,0:T(8,128)(2,1)} %pre_hbm.5, bf16[4,512,512]{2,1,0:T(8,128)(2,1)} %cot_hbm.5, bf16[256,512]{1,0:T(8,128)(2,1)} %spectra.3._), custom_call_target="tpu_custom_call" | custom-call | flops 536870912 | bytes 8388608 | tf_op jit(solution)/shard_map/spectra/pallas_call | solution.py:228
  10.8 0.9 %collective-permute-start.2 = (bf16[256,512]{1,0:T(8,128)(2,1)}, bf16[256,512]{1,0:T(8,128)(2,1)S(1)}, u32[]{:S(2)}, u32[]{:S(2)}) collective-permute-start(bf16[256,512]{1,0:T(8,128)(2,1)} %get-tuple-element.18), channel_id=1, source_target_pairs={{0,192},{64,0},{128,64},{192,128},{1,193},{65,1},{129,65},{193,129... | collective-permute-start | bytes 786440 | tf_op jit(solution)/shard_map/ppermute | solution.py:209
  11.6 0.7 collective-permute-start
  12.3 2.7 %spectra.5.own_hbm = bf16[256,512]{1,0:T(8,128)(2,1)} custom-call(bf16[4,512,512]{2,1,0:T(8,128)(2,1)} %fields_hbm.5, bf16[4,512,512]{2,1,0:T(8,128)(2,1)} %pre_hbm.5, bf16[4,512,512]{2,1,0:T(8,128)(2,1)} %cot_hbm.5, bf16[256,512]{1,0:T(8,128)(2,1)} %get-tuple-element.17._), custom_call_target="tpu_custom_call" | custom-call | flops 268435456 | bytes 4194304 | tf_op jit(solution)/shard_map/spectra/pallas_call | solution.py:228
  15.0 4.4 %collective-permute-done.2.three_ref = bf16[256,512]{1,0:T(8,128)(2,1)S(1)} collective-permute-done((bf16[256,512]{1,0:T(8,128)(2,1)}, bf16[256,512]{1,0:T(8,128)(2,1)S(1)}, u32[]{:S(2)}, u32[]{:S(2)}) %collective-permute-start.2) | collective-permute-done | bytes 262176 | tf_op jit(solution)/shard_map/ppermute | solution.py:209
  19.6 0.9 %copy-done = bf16[256,512]{1,0:T(8,128)(2,1)S(1)} copy-done((bf16[256,512]{1,0:T(8,128)(2,1)S(1)}, bf16[256,512]{1,0:T(8,128)(2,1)}, u32[]{:S(2)}) %copy-start) | copy-done | bytes 262168
  20.6 1.3 %sum_y.1 = bf16[64,8,256]{2,1,0:T(8,128)(2,1)} custom-call(bf16[256,512]{1,0:T(8,128)(2,1)S(1)} %copy-done, bf16[256,512]{1,0:T(8,128)(2,1)S(1)} %collective-permute-done.one_ref, bf16[256,512]{1,0:T(8,128)(2,1)S(1)} %collective-permute-done.1.two_ref, bf16[256,512]{1,0:T(8,128)(2,1)S(1)} %collective-permute-done.2.three_ref), custom_call_target="tpu_custom_call" | custom-call | tf_op jit(solution)/shard_map/sum_y/pallas_call | solution.py:246
  21.8 13.7 %all-to-all-start = ((bf16[64,8,256]{2,1,0:T(8,128)(2,1)}), bf16[64,8,256]{2,1,0:T(8,128)(2,1)S(1)}, u32[]{:S(2)}, u32[]{:S(2)}) async-start(bf16[64,8,256]{2,1,0:T(8,128)(2,1)} %sum_y.1), calls=%async_computation | async-start | bytes 524288 | tf_op jit(solution)/shard_map/all_to_all | solution.py:255
  35.5 1.3 %dynamic-slice_bitcast_fusion.w_ref = bf16[2,512,512]{2,1,0:T(8,128)(2,1)S(1)} fusion(bf16[4,2,512,512]{3,2,1,0:T(8,128)(2,1)} %param.7, s32[]{:T(128)S(6)} %select_n.4), kind=kLoop, calls=%fused_computation | loop fusion | bytes 2097156 | tf_op jit(solution)/shard_map/jit(dynamic_index_in_dim)/squeeze | solution.py:256
  36.8 11.5 %all-to-all-done.in_ref = bf16[64,8,256]{2,1,0:T(8,128)(2,1)S(1)} async-done(((bf16[64,8,256]{2,1,0:T(8,128)(2,1)}), bf16[64,8,256]{2,1,0:T(8,128)(2,1)S(1)}, u32[]{:S(2)}, u32[]{:S(2)}) %all-to-all-start) | async-done | bytes 262176 | tf_op jit(solution)/shard_map/all_to_all | solution.py:255
  48.4 1.5 %modes.1 = (bf16[16,4,8,128]{3,2,1,0:T(8,128)(2,1)}, bf16[40,512]{1,0:T(8,128)(2,1)S(1)}, bf16[40,512]{1,0:T(8,128)(2,1)S(1)}, bf16[40,512]{1,0:T(8,128)(2,1)S(1)}, bf16[40,512]{1,0:T(8,128)(2,1)S(1)}) custom-call(bf16[64,8,256]{2,1,0:T(8,128)(2,1)S(1)} %all-to-all-done.in_ref, bf16[2,512,512]{2,1,0:T(8,128)(2,1)S(1)} %dynamic-slice_bitcast_fusion.w_ref), custom_call_target="tpu_custom_call" | custom-call | tf_op jit(solution)/shard_map/modes/pallas_call | solution.py:257
  49.8 5.1 %all-to-all-start.1 = ((bf16[64,8,128]{2,1,0:T(8,128)(2,1)}), bf16[64,8,128]{2,1,0:T(8,128)(2,1)S(1)}, u32[]{:S(2)}, u32[]{:S(2)}) async-start(bf16[64,8,128]{2,1,0:T(8,128)(2,1)} %bitcast.1), calls=%async_computation.1 | async-start | bytes 262144 | tf_op jit(solution)/shard_map/all_to_all | solution.py:267
  55.0 2.4 %collective-permute-start.7 = (bf16[40,512]{1,0:T(8,128)(2,1)S(1)}, bf16[40,512]{1,0:T(8,128)(2,1)S(1)}, u32[]{:S(2)}, u32[]{:S(2)}) collective-permute-start(bf16[40,512]{1,0:T(8,128)(2,1)S(1)} %get-tuple-element.23), channel_id=1, source_target_pairs={{0,128},{64,192},{128,0},{192,64},{1,129},{65,193},{129,1},{193,65... | collective-permute-start | bytes 122888 | tf_op jit(solution)/shard_map/ppermute | solution.py:209
  57.5 1.1 %collective-permute-start.8 = (bf16[40,512]{1,0:T(8,128)(2,1)S(1)}, bf16[40,512]{1,0:T(8,128)(2,1)S(1)}, u32[]{:S(2)}, u32[]{:S(2)}) collective-permute-start(bf16[40,512]{1,0:T(8,128)(2,1)S(1)} %get-tuple-element.24), channel_id=1, source_target_pairs={{0,192},{64,0},{128,64},{192,128},{1,193},{65,1},{129,65},{193,129... | collective-permute-start | bytes 122888 | tf_op jit(solution)/shard_map/ppermute | solution.py:209
  58.5 0.9 %collective-permute-done.6.refs_1_ = bf16[40,512]{1,0:T(8,128)(2,1)S(1)} collective-permute-done((bf16[40,512]{1,0:T(8,128)(2,1)S(1)}, bf16[40,512]{1,0:T(8,128)(2,1)S(1)}, u32[]{:S(2)}, u32[]{:S(2)}) %collective-permute-start.6) | collective-permute-done | bytes 40992 | tf_op jit(solution)/shard_map/ppermute | solution.py:209
  59.4 0.5 collective-permute-done.7.refs_2_
  59.9 0.7 collective-permute-done.8.refs_3_
  60.6 0.4 weight.1
  61.0 1.6 %collective-permute-start.9 = (bf16[64,512]{1,0:T(8,128)(2,1)S(1)}, bf16[64,512]{1,0:T(8,128)(2,1)S(1)}, u32[]{:S(2)}, u32[]{:S(2)}) collective-permute-start(bf16[64,512]{1,0:T(8,128)(2,1)S(1)} %get-tuple-element.26), channel_id=1, source_target_pairs={{0,16},{16,32},{32,48},{48,0},{1,17},{17,33},{33,49},{49,1},{2,18}... | collective-permute-start | bytes 196616 | tf_op jit(solution)/shard_map/ppermute | solution.py:209
  62.7 3.2 %all-to-all-done.1.in_ref = bf16[64,8,128]{2,1,0:T(8,128)(2,1)S(1)} async-done(((bf16[64,8,128]{2,1,0:T(8,128)(2,1)}), bf16[64,8,128]{2,1,0:T(8,128)(2,1)S(1)}, u32[]{:S(2)}, u32[]{:S(2)}) %all-to-all-start.1) | async-done | bytes 131104 | tf_op jit(solution)/shard_map/all_to_all | solution.py:267
  65.8 1.4 %collective-permute-start.5 = (bf16[64,8,128]{2,1,0:T(8,128)(2,1)S(1)}, bf16[64,8,128]{2,1,0:T(8,128)(2,1)S(1)}, u32[]{:S(2)}, u32[]{:S(2)}) collective-permute-start(bf16[64,8,128]{2,1,0:T(8,128)(2,1)S(1)} %all-to-all-done.1.in_ref), channel_id=1, source_target_pairs={{0,128},{64,192},{128,0},{192,64},{1,129},{65,193},{129,1},{193,65... | collective-permute-start | bytes 393224 | tf_op jit(solution)/shard_map/ppermute | solution.py:209
  67.2 0.9 %collective-permute-start.4 = (bf16[64,8,128]{2,1,0:T(8,128)(2,1)S(1)}, bf16[64,8,128]{2,1,0:T(8,128)(2,1)S(1)}, u32[]{:S(2)}, u32[]{:S(2)}) collective-permute-start(bf16[64,8,128]{2,1,0:T(8,128)(2,1)S(1)} %all-to-all-done.1.in_ref), channel_id=1, source_target_pairs={{0,192},{64,0},{128,64},{192,128},{1,193},{65,1},{129,65},{193,129... | collective-permute-start | bytes 393224 | tf_op jit(solution)/shard_map/ppermute | solution.py:209
  68.1 0.6 collective-permute-start.3
  68.7 0.7 collective-permute-start.10
  69.4 1.9 %collective-permute-start.11 = (bf16[64,512]{1,0:T(8,128)(2,1)S(1)}, bf16[64,512]{1,0:T(8,128)(2,1)S(1)}, u32[]{:S(2)}, u32[]{:S(2)}) collective-permute-start(bf16[64,512]{1,0:T(8,128)(2,1)S(1)} %get-tuple-element.28), channel_id=1, source_target_pairs={{0,48},{16,0},{32,16},{48,32},{1,49},{17,1},{33,17},{49,33},{2,50}... | collective-permute-start | bytes 196616 | tf_op jit(solution)/shard_map/ppermute | solution.py:209
  71.4 1.4 %own_field.1 = (bf16[4,512,512]{2,1,0:T(8,128)(2,1)}, bf16[512,128]{1,0:T(8,128)(2,1)S(1)}) custom-call(bf16[64,8,128]{2,1,0:T(8,128)(2,1)S(1)} %all-to-all-done.1.in_ref), custom_call_target="tpu_custom_call" | custom-call | flops 134217728 | bytes 1048576 | tf_op jit(solution)/shard_map/own_field/pallas_call | solution.py:280
  72.8 1.2 %collective-permute-done.10.refs_6_ = bf16[64,512]{1,0:T(8,128)(2,1)S(1)} collective-permute-done((bf16[64,512]{1,0:T(8,128)(2,1)S(1)}, bf16[64,512]{1,0:T(8,128)(2,1)S(1)}, u32[]{:S(2)}, u32[]{:S(2)}) %collective-permute-start.10) | collective-permute-done | bytes 65568 | tf_op jit(solution)/shard_map/ppermute | solution.py:209
  73.9 0.3 collective-permute-done.4.refs_1_
  74.2 1.2 %collective-permute-done.3.refs_0_ = bf16[64,8,128]{2,1,0:T(8,128)(2,1)S(1)} collective-permute-done((bf16[64,8,128]{2,1,0:T(8,128)(2,1)S(1)}, bf16[64,8,128]{2,1,0:T(8,128)(2,1)S(1)}, u32[]{:S(2)}, u32[]{:S(2)}) %collective-permute-start.3) | collective-permute-done | bytes 131104 | tf_op jit(solution)/shard_map/ppermute | solution.py:209
  75.4 1.7 %last.1 = (bf16[4,512,512]{2,1,0:T(8,128)(2,1)}, f32[4,2,32,512]{3,2,1,0:T(8,128)}) custom-call(bf16[64,8,128]{2,1,0:T(8,128)(2,1)S(1)} %collective-permute-done.3.refs_0_, bf16[64,8,128]{2,1,0:T(8,128)(2,1)S(1)} %collective-permute-done.4.refs_1_, bf16[64,8,128]{2,1,0:T(8,128)(2,1)S(1)} %collective-permute-done.5.refs_2_, ...), custom_call_target="tpu_custom_call", output_to_operand_aliasing={{0}: (8, {})} | custom-call | tf_op jit(solution)/shard_map/last/pallas_call | solution.py:294
  (7 shorter events, 0.2 us)
Async XLA Ops:
  3.3 11.7 %collective-permute-start.1 = (bf16[256,512]{1,0:T(8,128)(2,1)}, bf16[256,512]{1,0:T(8,128)(2,1)S(1)}, u32[]{:S(2)}, u32[]{:S(2)}) collective-permute-start(bf16[256,512]{1,0:T(8,128)(2,1)} %spectra.3._), channel_id=1, source_target_pairs={{0,128},{64,192},{128,0},{192,64},{1,129},{65,193},{129,1},{193,65... | collective-permute-start | bytes 786440 | tf_op jit(solution)/shard_map/ppermute | solution.py:209
  10.8 8.7 %collective-permute-start.2 = (bf16[256,512]{1,0:T(8,128)(2,1)}, bf16[256,512]{1,0:T(8,128)(2,1)S(1)}, u32[]{:S(2)}, u32[]{:S(2)}) collective-permute-start(bf16[256,512]{1,0:T(8,128)(2,1)} %get-tuple-element.18), channel_id=1, source_target_pairs={{0,192},{64,0},{128,64},{192,128},{1,193},{65,1},{129,65},{193,129... | collective-permute-start | bytes 786440 | tf_op jit(solution)/shard_map/ppermute | solution.py:209
  11.6 8.0 %collective-permute-start = (bf16[256,512]{1,0:T(8,128)(2,1)}, bf16[256,512]{1,0:T(8,128)(2,1)S(1)}, u32[]{:S(2)}, u32[]{:S(2)}) collective-permute-start(bf16[256,512]{1,0:T(8,128)(2,1)} %get-tuple-element.17._), channel_id=1, source_target_pairs={{0,64},{64,128},{128,192},{192,0},{1,65},{65,129},{129,193},{193,1... | collective-permute-start | bytes 786440 | tf_op jit(solution)/shard_map/ppermute | solution.py:209
  19.6 1.0 %copy-start = (bf16[256,512]{1,0:T(8,128)(2,1)S(1)}, bf16[256,512]{1,0:T(8,128)(2,1)}, u32[]{:S(2)}) copy-start(bf16[256,512]{1,0:T(8,128)(2,1)} %spectra.5.own_hbm) | copy-start | bytes 786436
  21.8 26.5 %all-to-all-start = ((bf16[64,8,256]{2,1,0:T(8,128)(2,1)}), bf16[64,8,256]{2,1,0:T(8,128)(2,1)S(1)}, u32[]{:S(2)}, u32[]{:S(2)}) async-start(bf16[64,8,256]{2,1,0:T(8,128)(2,1)} %sum_y.1), calls=%async_computation | async-start | bytes 524288 | tf_op jit(solution)/shard_map/all_to_all | solution.py:255
  49.8 16.0 %all-to-all-start.1 = ((bf16[64,8,128]{2,1,0:T(8,128)(2,1)}), bf16[64,8,128]{2,1,0:T(8,128)(2,1)S(1)}, u32[]{:S(2)}, u32[]{:S(2)}) async-start(bf16[64,8,128]{2,1,0:T(8,128)(2,1)} %bitcast.1), calls=%async_computation.1 | async-start | bytes 262144 | tf_op jit(solution)/shard_map/all_to_all | solution.py:267
  54.9 4.4 %collective-permute-start.6 = (bf16[40,512]{1,0:T(8,128)(2,1)S(1)}, bf16[40,512]{1,0:T(8,128)(2,1)S(1)}, u32[]{:S(2)}, u32[]{:S(2)}) collective-permute-start(bf16[40,512]{1,0:T(8,128)(2,1)S(1)} %get-tuple-element.22), channel_id=1, source_target_pairs={{0,64},{64,128},{128,192},{192,0},{1,65},{65,129},{129,193},{193,1... | collective-permute-start | bytes 122888 | tf_op jit(solution)/shard_map/ppermute | solution.py:209
  55.0 4.9 %collective-permute-start.7 = (bf16[40,512]{1,0:T(8,128)(2,1)S(1)}, bf16[40,512]{1,0:T(8,128)(2,1)S(1)}, u32[]{:S(2)}, u32[]{:S(2)}) collective-permute-start(bf16[40,512]{1,0:T(8,128)(2,1)S(1)} %get-tuple-element.23), channel_id=1, source_target_pairs={{0,128},{64,192},{128,0},{192,64},{1,129},{65,193},{129,1},{193,65... | collective-permute-start | bytes 122888 | tf_op jit(solution)/shard_map/ppermute | solution.py:209
  57.5 3.1 %collective-permute-start.8 = (bf16[40,512]{1,0:T(8,128)(2,1)S(1)}, bf16[40,512]{1,0:T(8,128)(2,1)S(1)}, u32[]{:S(2)}, u32[]{:S(2)}) collective-permute-start(bf16[40,512]{1,0:T(8,128)(2,1)S(1)} %get-tuple-element.24), channel_id=1, source_target_pairs={{0,192},{64,0},{128,64},{192,128},{1,193},{65,1},{129,65},{193,129... | collective-permute-start | bytes 122888 | tf_op jit(solution)/shard_map/ppermute | solution.py:209
  61.0 8.4 %collective-permute-start.9 = (bf16[64,512]{1,0:T(8,128)(2,1)S(1)}, bf16[64,512]{1,0:T(8,128)(2,1)S(1)}, u32[]{:S(2)}, u32[]{:S(2)}) collective-permute-start(bf16[64,512]{1,0:T(8,128)(2,1)S(1)} %get-tuple-element.26), channel_id=1, source_target_pairs={{0,16},{16,32},{32,48},{48,0},{1,17},{17,33},{33,49},{49,1},{2,18}... | collective-permute-start | bytes 196616 | tf_op jit(solution)/shard_map/ppermute | solution.py:209
  65.8 8.1 %collective-permute-start.5 = (bf16[64,8,128]{2,1,0:T(8,128)(2,1)S(1)}, bf16[64,8,128]{2,1,0:T(8,128)(2,1)S(1)}, u32[]{:S(2)}, u32[]{:S(2)}) collective-permute-start(bf16[64,8,128]{2,1,0:T(8,128)(2,1)S(1)} %all-to-all-done.1.in_ref), channel_id=1, source_target_pairs={{0,128},{64,192},{128,0},{192,64},{1,129},{65,193},{129,1},{193,65... | collective-permute-start | bytes 393224 | tf_op jit(solution)/shard_map/ppermute | solution.py:209
  67.2 7.0 %collective-permute-start.4 = (bf16[64,8,128]{2,1,0:T(8,128)(2,1)S(1)}, bf16[64,8,128]{2,1,0:T(8,128)(2,1)S(1)}, u32[]{:S(2)}, u32[]{:S(2)}) collective-permute-start(bf16[64,8,128]{2,1,0:T(8,128)(2,1)S(1)} %all-to-all-done.1.in_ref), channel_id=1, source_target_pairs={{0,192},{64,0},{128,64},{192,128},{1,193},{65,1},{129,65},{193,129... | collective-permute-start | bytes 393224 | tf_op jit(solution)/shard_map/ppermute | solution.py:209
  68.1 7.3 %collective-permute-start.3 = (bf16[64,8,128]{2,1,0:T(8,128)(2,1)S(1)}, bf16[64,8,128]{2,1,0:T(8,128)(2,1)S(1)}, u32[]{:S(2)}, u32[]{:S(2)}) collective-permute-start(bf16[64,8,128]{2,1,0:T(8,128)(2,1)S(1)} %all-to-all-done.1.in_ref), channel_id=1, source_target_pairs={{0,64},{64,128},{128,192},{192,0},{1,65},{65,129},{129,193},{193,1... | collective-permute-start | bytes 393224 | tf_op jit(solution)/shard_map/ppermute | solution.py:209
  68.7 5.2 %collective-permute-start.10 = (bf16[64,512]{1,0:T(8,128)(2,1)S(1)}, bf16[64,512]{1,0:T(8,128)(2,1)S(1)}, u32[]{:S(2)}, u32[]{:S(2)}) collective-permute-start(bf16[64,512]{1,0:T(8,128)(2,1)S(1)} %get-tuple-element.27), channel_id=1, source_target_pairs={{0,32},{16,48},{32,0},{48,16},{1,33},{17,49},{33,1},{49,17},{2,34}... | collective-permute-start | bytes 196616 | tf_op jit(solution)/shard_map/ppermute | solution.py:209
  69.4 4.5 %collective-permute-start.11 = (bf16[64,512]{1,0:T(8,128)(2,1)S(1)}, bf16[64,512]{1,0:T(8,128)(2,1)S(1)}, u32[]{:S(2)}, u32[]{:S(2)}) collective-permute-start(bf16[64,512]{1,0:T(8,128)(2,1)S(1)} %get-tuple-element.28), channel_id=1, source_target_pairs={{0,48},{16,0},{32,16},{48,32},{1,49},{17,1},{33,17},{49,33},{2,50}... | collective-permute-start | bytes 196616 | tf_op jit(solution)/shard_map/ppermute | solution.py:209

commit v7 on v6

--- a/solution.py
+++ b/solution.py
@@ -11,7 +11,6 @@
 
 F32, BF16 = jnp.float32, jnp.bfloat16
 OTHERS = ("x", "w", "zl")
-SPECTRA_VMEM = 60 * 2**20
 NT = (((1,), (1,)), ((), ()))
 TN = (((0,), (0,)), ((), ()))
 
@@ -37,9 +36,19 @@
 
 
 def gelu_slope(values):
-    normal_cdf = 0.5 * (1.0 + lax.erf(values * (1.0 / math.sqrt(2.0))))
-    density = jnp.exp(-0.5 * values * values) * (1.0 / math.sqrt(2.0 * math.pi))
-    return normal_cdf + values * density
+    size = jnp.abs(values)
+    t = 1.0 / (1.0 + 0.28 * size)
+    m = -0.10580839289759565
+    for c in (
+        0.38987462028162295,
+        -0.23699444704250228,
+        0.26891093471374405,
+        0.06749644895015629,
+        0.11652082672551742,
+    ):
+        m = m * t + c
+    below = jnp.exp(-0.5 * values * values) * (m * t - size * (1.0 / math.sqrt(2.0 * math.pi)))
+    return jnp.where(values >= 0.0, 1.0 - below, below)
 
 
 def dot(a, b, dims=None):
@@ -70,7 +79,12 @@
 
 def spectra_kernel(steps, fields_hbm, pre_hbm, cot_hbm, _, *rest):
     n = len(steps)
-    out_hbms, out_refs, (fields, pre, cot, table, sems, out_sems) = rest[:n], rest[n : 2 * n], rest[2 * n :]
+    token_ref, *rest = rest
+    token_ref[...] = jnp.zeros_like(token_ref)
+    out_hbms, rest = rest[:n], rest[n:]
+    if steps == (0,):
+        moves_ref, *rest = rest
+    out_refs, (fields, pre, cot, table, sems, out_sems) = rest[:n], rest[n:]
     y = lax.axis_index("y")
 
     def copies(i, h):
@@ -87,6 +101,10 @@
                 copy.start()
     points = table.shape[1]
     table[...] = table_of(points, False, (y * 4 + lax.axis_index("zl")) * points)
+    if steps == (0,):
+        for h in range(2):
+            digits = [(8, 64, 1), (2, 2, 128), (1, 2, 64)]
+            moves_ref[h] = row_moves((512, 256), digits, [(4, 2, h)])
     sent = []
     for i in range(n):
         for h in range(2):
@@ -103,17 +121,10 @@
         copy.wait()
 
 
-def sum_y_kernel(own_hbm, one_ref, two_ref, three_ref, out_ref, own, sem):
-    copy = pltpu.make_async_copy(own_hbm, own, sem)
-    copy.start()
+def sum_y_kernel(moves_ref, own_ref, one_ref, two_ref, three_ref, out_ref):
     total = one_ref[...].astype(F32) + two_ref[...].astype(F32) + three_ref[...].astype(F32)
-    copy.wait()
-    low = (total + own[...].astype(F32)).astype(BF16)
-    out = None
-    for h in range(2):
-        moves = row_moves((512, 256), [(8, 64, 1), (2, 2, 128), (1, 2, 64)], [(4, 2, h)])
-        part = dot(moves, low[:, 256 * h : 256 * h + 256])
-        out = part if out is None else out + part
+    low = (total + own_ref[...].astype(F32)).astype(BF16)
+    out = dot(moves_ref[0], low[:, :256]) + dot(moves_ref[1], low[:, 256:])
     out_ref[...] = out.reshape(64, 8, 256).astype(BF16)
 
 
@@ -225,33 +236,33 @@
 
     def spectra(steps, after):
         n = len(steps)
+        moves = [block(2, 512, 256)] if steps == (0,) else []
         return pl.pallas_call(
             functools.partial(spectra_kernel, steps),
             in_specs=[hbm] * 4,
-            out_specs=[hbm] * n,
-            out_shape=[block(256, 512)] * n,
+            out_specs=[vmem] + [hbm] * n + [vmem] * len(moves),
+            out_shape=[jax.ShapeDtypeStruct((8, 128), F32)] + [block(256, 512)] * n + moves,
             scratch_shapes=[pltpu.VMEM((256, 512), BF16)] * n
             + [pltpu.VMEM((n, 512, 512), BF16)] * 3
             + [pltpu.VMEM((128, 512), BF16), pltpu.SemaphoreType.DMA((3, n, 2))]
             + [pltpu.SemaphoreType.DMA((n, 2))],
-            compiler_params=pltpu.CompilerParams(vmem_limit_bytes=SPECTRA_VMEM),
+            compiler_params=pltpu.CompilerParams(vmem_limit_bytes=52 * 2**20),
             cost_estimate=cost(2**28 * n, 2**22 * n),
             name="spectra",
         )(fields, pre_act, cotangent, after)
 
-    (two,) = spectra((2,), fields)
-    one, three = spectra((1, 3), two)
-    (own,) = spectra((0,), one)
+    token, two = spectra((2,), fields)
+    token, one, three = spectra((1, 3), token)
+    _, own, moves = spectra((0,), token)
     one, two, three = shifted(one, "y", 1), shifted(two, "y", 2), shifted(three, "y", 3)
     send = pl.pallas_call(
         sum_y_kernel,
-        in_specs=[hbm] + [vmem] * 3,
+        in_specs=[vmem] * 5,
         out_specs=vmem,
         out_shape=block(64, 8, 256),
-        scratch_shapes=[pltpu.VMEM((256, 512), BF16), pltpu.SemaphoreType.DMA],
         compiler_params=params,
         name="sum_y",
-    )(own, one, two, three)
+    )(moves, own, one, two, three)
     got = lax.all_to_all(send, OTHERS, 0, 0, tiled=True)
     mine = lax.dynamic_index_in_dim(weights, lax.axis_index("zl"), 0, keepdims=False)
     send, *sides = pl.pallas_call(

time: 77.6 us -> 75.9 us (0.978)
  waiting for transfers between devices: 24 us -> 21.2 us
  starting transfers between devices: 34.9 us -> 36.6 us
  local copies, waits for them, and re-layouts: 2.25 us -> 1.3 us
    ppermute x12, starting transfers between devices: 16.1 us -> 18.1 us  [shifted(): lax.ppermute(value, axis, [(i, (i + distance) % 4) for i in range(4)])]
    ppermute x12, waiting for transfers between devices: 9.34 us -> 7.74 us  [shifted(): lax.ppermute(value, axis, [(i, (i + distance) % 4) for i in range(4)])]
    all_to_all x1, waiting for transfers between devices: 3.15 us -> 1.92 us  [shards(): got = lax.all_to_all(send.reshape(64, 8, 128), OTHERS, 0, 0, tiled=True)]
    unnamed x2 -> x0, local copies, waits for them, and re-layouts: 0.95 us -> none
  transfers between devices with their start and end apart: 14 -> 14, of which waited for: 10 -> 8; matrix products, arithmetic and copies ran while one was open for 2% -> 2% of each run, Pallas kernels for 10% -> 12%
where the time goes in v7:
time: 75.9 us; the launch traced here: 75.6 us
  starting transfers between devices  36.6 us (48%)
  waiting for transfers between devices  21.2 us (28%)
  Pallas kernels  15.6 us (21%)
  local copies, waits for them, and re-layouts  1.3 us (2%)
  between operations  0.87 us (1%)
    ppermute x12, starting transfers between devices, shifted(): lax.ppermute(value, axis, [(i, (i + distance) % 4) for i in range(4)])  18.1 us
    all_to_all x1, starting transfers between devices, shards(): got = lax.all_to_all(send, OTHERS, 0, 0, tiled=True)  13.4 us
    all_to_all x1, waiting for transfers between devices, shards(): got = lax.all_to_all(send, OTHERS, 0, 0, tiled=True)  11.5 us
    pallas_call x3, Pallas kernels, spectra(): pl.pallas_call(functools.partial(spectra_kernel, steps), in_specs=[hbm] *...  9.53 us
    ppermute x12, waiting for transfers between devices, shifted(): lax.ppermute(value, axis, [(i, (i + distance) % 4) for i in range(4)])  7.74 us
    all_to_all x1, starting transfers between devices, shards(): got = lax.all_to_all(send.reshape(64, 8, 128), OTHERS, 0, 0, tiled=True)  5.09 us
    all_to_all x1, waiting for transfers between devices, shards(): got = lax.all_to_all(send.reshape(64, 8, 128), OTHERS, 0, 0, tiled=True)  1.92 us
    pallas_call x1, Pallas kernels, shards(): pl.pallas_call(functools.partial(last_kernel, factor), in_specs=[vmem] *...  1.72 us
  transfers between devices with their start and end apart: 14, of which 8 were waited for; matrix products, arithmetic and copies ran while one was open for 2% of the time, Pallas kernels for 12%

profile of v7, /device:TPU:1, one launch (start us, length us, event | category | flops | bytes accessed | tf_op | source)
XLA Modules:
  0.0 75.6 jit_solution(6702255027793661795)
XLA Ops:
  0.6 2.5 %spectra.3 = (f32[8,128]{1,0:T(8,128)S(1)}, bf16[256,512]{1,0:T(8,128)(2,1)S(1)}) custom-call(bf16[4,512,512]{2,1,0:T(8,128)(2,1)} %fields_hbm.5, bf16[4,512,512]{2,1,0:T(8,128)(2,1)} %pre_hbm.5, bf16[4,512,512]{2,1,0:T(8,128)(2,1)} %cot_hbm.5, bf16[4,512,512]{2,1,0:T(8,128)(2,1)} %fields_hbm.5), custom_call_target="tpu_custom_call" | custom-call | flops 268435456 | bytes 4194304 | tf_op jit(solution)/shard_map/spectra/pallas_call | solution.py:240
  3.2 3.8 %collective-permute-start.1 = (bf16[256,512]{1,0:T(8,128)(2,1)S(1)}, bf16[256,512]{1,0:T(8,128)(2,1)S(1)}, u32[]{:S(2)}, u32[]{:S(2)}) collective-permute-start(bf16[256,512]{1,0:T(8,128)(2,1)S(1)} %get-tuple-element.27), channel_id=1, source_target_pairs={{0,128},{64,192},{128,0},{192,64},{1,129},{65,193},{129,1},{193,65... | collective-permute-start | bytes 786440 | tf_op jit(solution)/shard_map/ppermute | solution.py:220
  7.0 3.9 %spectra.4 = (f32[8,128]{1,0:T(8,128)S(1)}, bf16[256,512]{1,0:T(8,128)(2,1)S(1)}, bf16[256,512]{1,0:T(8,128)(2,1)S(1)}) custom-call(bf16[4,512,512]{2,1,0:T(8,128)(2,1)} %fields_hbm.5, bf16[4,512,512]{2,1,0:T(8,128)(2,1)} %pre_hbm.5, bf16[4,512,512]{2,1,0:T(8,128)(2,1)} %cot_hbm.5, f32[8,128]{1,0:T(8,128)S(1)} %get-tuple-element.22._), custom_call_target="tpu_custom_call" | custom-call | flops 536870912 | bytes 8388608 | tf_op jit(solution)/shard_map/spectra/pallas_call | solution.py:240
  10.9 0.5 collective-permute-start
  11.4 2.3 %collective-permute-start.2 = (bf16[256,512]{1,0:T(8,128)(2,1)S(1)}, bf16[256,512]{1,0:T(8,128)(2,1)S(1)}, u32[]{:S(2)}, u32[]{:S(2)}) collective-permute-start(bf16[256,512]{1,0:T(8,128)(2,1)S(1)} %get-tuple-element.28), channel_id=1, source_target_pairs={{0,192},{64,0},{128,64},{192,128},{1,193},{65,1},{129,65},{193,129... | collective-permute-start | bytes 786440 | tf_op jit(solution)/shard_map/ppermute | solution.py:220
  13.7 3.1 %spectra.5 = (f32[8,128]{1,0:T(8,128)}, bf16[256,512]{1,0:T(8,128)(2,1)S(1)}, bf16[2,512,256]{2,1,0:T(8,128)(2,1)S(1)}) custom-call(bf16[4,512,512]{2,1,0:T(8,128)(2,1)} %fields_hbm.5, bf16[4,512,512]{2,1,0:T(8,128)(2,1)} %pre_hbm.5, bf16[4,512,512]{2,1,0:T(8,128)(2,1)} %cot_hbm.5, f32[8,128]{1,0:T(8,128)S(1)} %get-tuple-element.23._), custom_call_target="tpu_custom_call" | custom-call | flops 268435456 | bytes 4194304 | tf_op jit(solution)/shard_map/spectra/pallas_call | solution.py:240
  16.8 2.3 %collective-permute-done.one_ref = bf16[256,512]{1,0:T(8,128)(2,1)S(1)} collective-permute-done((bf16[256,512]{1,0:T(8,128)(2,1)S(1)}, bf16[256,512]{1,0:T(8,128)(2,1)S(1)}, u32[]{:S(2)}, u32[]{:S(2)}) %collective-permute-start) | collective-permute-done | bytes 262176 | tf_op jit(solution)/shard_map/ppermute | solution.py:220
  19.0 0.0 collective-permute-done.2.three_ref
  19.0 1.1 %sum_y.1 = bf16[64,8,256]{2,1,0:T(8,128)(2,1)} custom-call(bf16[2,512,256]{2,1,0:T(8,128)(2,1)S(1)} %get-tuple-element.24.moves_ref, bf16[256,512]{1,0:T(8,128)(2,1)S(1)} %get-tuple-element.25.own_ref, bf16[256,512]{1,0:T(8,128)(2,1)S(1)} %collective-permute-done.one_ref, bf16[256,512]{1,0:T(8,128)(2,1)S(1)} %collective-permute-done.1.two_ref, ...), custom_call_target="tpu_custom_call" | custom-call | tf_op jit(solution)/shard_map/sum_y/pallas_call | solution.py:258
  20.1 13.4 %all-to-all-start = ((bf16[64,8,256]{2,1,0:T(8,128)(2,1)}), bf16[64,8,256]{2,1,0:T(8,128)(2,1)S(1)}, u32[]{:S(2)}, u32[]{:S(2)}) async-start(bf16[64,8,256]{2,1,0:T(8,128)(2,1)} %sum_y.1), calls=%async_computation | async-start | bytes 524288 | tf_op jit(solution)/shard_map/all_to_all | solution.py:266
  33.5 1.3 %dynamic-slice_bitcast_fusion.w_ref = bf16[2,512,512]{2,1,0:T(8,128)(2,1)S(1)} fusion(bf16[4,2,512,512]{3,2,1,0:T(8,128)(2,1)} %param.7, s32[]{:T(128)S(6)} %select_n.4), kind=kLoop, calls=%fused_computation | loop fusion | bytes 2097156 | tf_op jit(solution)/shard_map/jit(dynamic_index_in_dim)/squeeze | solution.py:267
  34.8 11.5 %all-to-all-done.in_ref = bf16[64,8,256]{2,1,0:T(8,128)(2,1)S(1)} async-done(((bf16[64,8,256]{2,1,0:T(8,128)(2,1)}), bf16[64,8,256]{2,1,0:T(8,128)(2,1)S(1)}, u32[]{:S(2)}, u32[]{:S(2)}) %all-to-all-start) | async-done | bytes 262176 | tf_op jit(solution)/shard_map/all_to_all | solution.py:266
  46.4 1.5 %modes.1 = (bf16[16,4,8,128]{3,2,1,0:T(8,128)(2,1)}, bf16[40,512]{1,0:T(8,128)(2,1)S(1)}, bf16[40,512]{1,0:T(8,128)(2,1)S(1)}, bf16[40,512]{1,0:T(8,128)(2,1)S(1)}, bf16[40,512]{1,0:T(8,128)(2,1)S(1)}) custom-call(bf16[64,8,256]{2,1,0:T(8,128)(2,1)S(1)} %all-to-all-done.in_ref, bf16[2,512,512]{2,1,0:T(8,128)(2,1)S(1)} %dynamic-slice_bitcast_fusion.w_ref), custom_call_target="tpu_custom_call" | custom-call | tf_op jit(solution)/shard_map/modes/pallas_call | solution.py:268
  47.8 5.1 %all-to-all-start.1 = ((bf16[64,8,128]{2,1,0:T(8,128)(2,1)}), bf16[64,8,128]{2,1,0:T(8,128)(2,1)S(1)}, u32[]{:S(2)}, u32[]{:S(2)}) async-start(bf16[64,8,128]{2,1,0:T(8,128)(2,1)} %bitcast.1), calls=%async_computation.1 | async-start | bytes 262144 | tf_op jit(solution)/shard_map/all_to_all | solution.py:278
  52.9 0.5 collective-permute-start.6
  53.4 3.4 %collective-permute-start.7 = (bf16[40,512]{1,0:T(8,128)(2,1)S(1)}, bf16[40,512]{1,0:T(8,128)(2,1)S(1)}, u32[]{:S(2)}, u32[]{:S(2)}) collective-permute-start(bf16[40,512]{1,0:T(8,128)(2,1)S(1)} %get-tuple-element.33), channel_id=1, source_target_pairs={{0,128},{64,192},{128,0},{192,64},{1,129},{65,193},{129,1},{193,65... | collective-permute-start | bytes 122888 | tf_op jit(solution)/shard_map/ppermute | solution.py:220
  56.9 0.1 collective-permute-start.8
  57.0 0.4 collective-permute-done.6.refs_1_
  57.4 1.6 %collective-permute-done.7.refs_2_ = bf16[40,512]{1,0:T(8,128)(2,1)S(1)} collective-permute-done((bf16[40,512]{1,0:T(8,128)(2,1)S(1)}, bf16[40,512]{1,0:T(8,128)(2,1)S(1)}, u32[]{:S(2)}, u32[]{:S(2)}) %collective-permute-start.7) | collective-permute-done | bytes 40992 | tf_op jit(solution)/shard_map/ppermute | solution.py:220
  59.0 1.0 %collective-permute-done.8.refs_3_ = bf16[40,512]{1,0:T(8,128)(2,1)S(1)} collective-permute-done((bf16[40,512]{1,0:T(8,128)(2,1)S(1)}, bf16[40,512]{1,0:T(8,128)(2,1)S(1)}, u32[]{:S(2)}, u32[]{:S(2)}) %collective-permute-start.8) | collective-permute-done | bytes 40992 | tf_op jit(solution)/shard_map/ppermute | solution.py:220
  60.0 0.4 weight.1
  60.4 1.5 %collective-permute-start.9 = (bf16[64,512]{1,0:T(8,128)(2,1)S(1)}, bf16[64,512]{1,0:T(8,128)(2,1)S(1)}, u32[]{:S(2)}, u32[]{:S(2)}) collective-permute-start(bf16[64,512]{1,0:T(8,128)(2,1)S(1)} %get-tuple-element.36), channel_id=1, source_target_pairs={{0,16},{16,32},{32,48},{48,0},{1,17},{17,33},{33,49},{49,1},{2,18}... | collective-permute-start | bytes 196616 | tf_op jit(solution)/shard_map/ppermute | solution.py:220
  61.9 1.9 %all-to-all-done.1.in_ref = bf16[64,8,128]{2,1,0:T(8,128)(2,1)S(1)} async-done(((bf16[64,8,128]{2,1,0:T(8,128)(2,1)}), bf16[64,8,128]{2,1,0:T(8,128)(2,1)S(1)}, u32[]{:S(2)}, u32[]{:S(2)}) %all-to-all-start.1) | async-done | bytes 131104 | tf_op jit(solution)/shard_map/all_to_all | solution.py:278
  63.8 1.9 %collective-permute-start.5 = (bf16[64,8,128]{2,1,0:T(8,128)(2,1)S(1)}, bf16[64,8,128]{2,1,0:T(8,128)(2,1)S(1)}, u32[]{:S(2)}, u32[]{:S(2)}) collective-permute-start(bf16[64,8,128]{2,1,0:T(8,128)(2,1)S(1)} %all-to-all-done.1.in_ref), channel_id=1, source_target_pairs={{0,128},{64,192},{128,0},{192,64},{1,129},{65,193},{129,1},{193,65... | collective-permute-start | bytes 393224 | tf_op jit(solution)/shard_map/ppermute | solution.py:220
  65.7 0.9 %collective-permute-start.4 = (bf16[64,8,128]{2,1,0:T(8,128)(2,1)S(1)}, bf16[64,8,128]{2,1,0:T(8,128)(2,1)S(1)}, u32[]{:S(2)}, u32[]{:S(2)}) collective-permute-start(bf16[64,8,128]{2,1,0:T(8,128)(2,1)S(1)} %all-to-all-done.1.in_ref), channel_id=1, source_target_pairs={{0,192},{64,0},{128,64},{192,128},{1,193},{65,1},{129,65},{193,129... | collective-permute-start | bytes 393224 | tf_op jit(solution)/shard_map/ppermute | solution.py:220
  66.6 0.6 collective-permute-start.3
  67.2 0.7 collective-permute-start.10
  67.9 2.0 %collective-permute-start.11 = (bf16[64,512]{1,0:T(8,128)(2,1)S(1)}, bf16[64,512]{1,0:T(8,128)(2,1)S(1)}, u32[]{:S(2)}, u32[]{:S(2)}) collective-permute-start(bf16[64,512]{1,0:T(8,128)(2,1)S(1)} %get-tuple-element.38), channel_id=1, source_target_pairs={{0,48},{16,0},{32,16},{48,32},{1,49},{17,1},{33,17},{49,33},{2,50}... | collective-permute-start | bytes 196616 | tf_op jit(solution)/shard_map/ppermute | solution.py:220
  69.8 1.4 %own_field.1 = (bf16[4,512,512]{2,1,0:T(8,128)(2,1)}, bf16[512,128]{1,0:T(8,128)(2,1)S(1)}) custom-call(bf16[64,8,128]{2,1,0:T(8,128)(2,1)S(1)} %all-to-all-done.1.in_ref), custom_call_target="tpu_custom_call" | custom-call | flops 134217728 | bytes 1048576 | tf_op jit(solution)/shard_map/own_field/pallas_call | solution.py:291
  71.3 1.1 %collective-permute-done.10.refs_6_ = bf16[64,512]{1,0:T(8,128)(2,1)S(1)} collective-permute-done((bf16[64,512]{1,0:T(8,128)(2,1)S(1)}, bf16[64,512]{1,0:T(8,128)(2,1)S(1)}, u32[]{:S(2)}, u32[]{:S(2)}) %collective-permute-start.10) | collective-permute-done | bytes 65568 | tf_op jit(solution)/shard_map/ppermute | solution.py:220
  72.4 1.3 %collective-permute-done.4.refs_1_ = bf16[64,8,128]{2,1,0:T(8,128)(2,1)S(1)} collective-permute-done((bf16[64,8,128]{2,1,0:T(8,128)(2,1)S(1)}, bf16[64,8,128]{2,1,0:T(8,128)(2,1)S(1)}, u32[]{:S(2)}, u32[]{:S(2)}) %collective-permute-start.4) | collective-permute-done | bytes 131104 | tf_op jit(solution)/shard_map/ppermute | solution.py:220
  73.7 1.7 %last.1 = (bf16[4,512,512]{2,1,0:T(8,128)(2,1)}, f32[4,2,32,512]{3,2,1,0:T(8,128)}) custom-call(bf16[64,8,128]{2,1,0:T(8,128)(2,1)S(1)} %collective-permute-done.3.refs_0_, bf16[64,8,128]{2,1,0:T(8,128)(2,1)S(1)} %collective-permute-done.4.refs_1_, bf16[64,8,128]{2,1,0:T(8,128)(2,1)S(1)} %collective-permute-done.5.refs_2_, ...), custom_call_target="tpu_custom_call", output_to_operand_aliasing={{0}: (8, {})} | custom-call | tf_op jit(solution)/shard_map/last/pallas_call | solution.py:305
  (5 shorter events, 0.0 us)
Async XLA Ops:
  3.2 13.6 %collective-permute-start.1 = (bf16[256,512]{1,0:T(8,128)(2,1)S(1)}, bf16[256,512]{1,0:T(8,128)(2,1)S(1)}, u32[]{:S(2)}, u32[]{:S(2)}) collective-permute-start(bf16[256,512]{1,0:T(8,128)(2,1)S(1)} %get-tuple-element.27), channel_id=1, source_target_pairs={{0,128},{64,192},{128,0},{192,64},{1,129},{65,193},{129,1},{193,65... | collective-permute-start | bytes 786440 | tf_op jit(solution)/shard_map/ppermute | solution.py:220
  10.9 8.1 %collective-permute-start = (bf16[256,512]{1,0:T(8,128)(2,1)S(1)}, bf16[256,512]{1,0:T(8,128)(2,1)S(1)}, u32[]{:S(2)}, u32[]{:S(2)}) collective-permute-start(bf16[256,512]{1,0:T(8,128)(2,1)S(1)} %get-tuple-element.26), channel_id=1, source_target_pairs={{0,64},{64,128},{128,192},{192,0},{1,65},{65,129},{129,193},{193,1... | collective-permute-start | bytes 786440 | tf_op jit(solution)/shard_map/ppermute | solution.py:220
  11.4 7.7 %collective-permute-start.2 = (bf16[256,512]{1,0:T(8,128)(2,1)S(1)}, bf16[256,512]{1,0:T(8,128)(2,1)S(1)}, u32[]{:S(2)}, u32[]{:S(2)}) collective-permute-start(bf16[256,512]{1,0:T(8,128)(2,1)S(1)} %get-tuple-element.28), channel_id=1, source_target_pairs={{0,192},{64,0},{128,64},{192,128},{1,193},{65,1},{129,65},{193,129... | collective-permute-start | bytes 786440 | tf_op jit(solution)/shard_map/ppermute | solution.py:220
  20.1 26.2 %all-to-all-start = ((bf16[64,8,256]{2,1,0:T(8,128)(2,1)}), bf16[64,8,256]{2,1,0:T(8,128)(2,1)S(1)}, u32[]{:S(2)}, u32[]{:S(2)}) async-start(bf16[64,8,256]{2,1,0:T(8,128)(2,1)} %sum_y.1), calls=%async_computation | async-start | bytes 524288 | tf_op jit(solution)/shard_map/all_to_all | solution.py:266
  47.8 16.0 %all-to-all-start.1 = ((bf16[64,8,128]{2,1,0:T(8,128)(2,1)}), bf16[64,8,128]{2,1,0:T(8,128)(2,1)S(1)}, u32[]{:S(2)}, u32[]{:S(2)}) async-start(bf16[64,8,128]{2,1,0:T(8,128)(2,1)} %bitcast.1), calls=%async_computation.1 | async-start | bytes 262144 | tf_op jit(solution)/shard_map/all_to_all | solution.py:278
  52.9 4.4 %collective-permute-start.6 = (bf16[40,512]{1,0:T(8,128)(2,1)S(1)}, bf16[40,512]{1,0:T(8,128)(2,1)S(1)}, u32[]{:S(2)}, u32[]{:S(2)}) collective-permute-start(bf16[40,512]{1,0:T(8,128)(2,1)S(1)} %get-tuple-element.32), channel_id=1, source_target_pairs={{0,64},{64,128},{128,192},{192,0},{1,65},{65,129},{129,193},{193,1... | collective-permute-start | bytes 122888 | tf_op jit(solution)/shard_map/ppermute | solution.py:220
  53.4 5.6 %collective-permute-start.7 = (bf16[40,512]{1,0:T(8,128)(2,1)S(1)}, bf16[40,512]{1,0:T(8,128)(2,1)S(1)}, u32[]{:S(2)}, u32[]{:S(2)}) collective-permute-start(bf16[40,512]{1,0:T(8,128)(2,1)S(1)} %get-tuple-element.33), channel_id=1, source_target_pairs={{0,128},{64,192},{128,0},{192,64},{1,129},{65,193},{129,1},{193,65... | collective-permute-start | bytes 122888 | tf_op jit(solution)/shard_map/ppermute | solution.py:220
  56.9 3.1 %collective-permute-start.8 = (bf16[40,512]{1,0:T(8,128)(2,1)S(1)}, bf16[40,512]{1,0:T(8,128)(2,1)S(1)}, u32[]{:S(2)}, u32[]{:S(2)}) collective-permute-start(bf16[40,512]{1,0:T(8,128)(2,1)S(1)} %get-tuple-element.34), channel_id=1, source_target_pairs={{0,192},{64,0},{128,64},{192,128},{1,193},{65,1},{129,65},{193,129... | collective-permute-start | bytes 122888 | tf_op jit(solution)/shard_map/ppermute | solution.py:220
  60.4 7.5 %collective-permute-start.9 = (bf16[64,512]{1,0:T(8,128)(2,1)S(1)}, bf16[64,512]{1,0:T(8,128)(2,1)S(1)}, u32[]{:S(2)}, u32[]{:S(2)}) collective-permute-start(bf16[64,512]{1,0:T(8,128)(2,1)S(1)} %get-tuple-element.36), channel_id=1, source_target_pairs={{0,16},{16,32},{32,48},{48,0},{1,17},{17,33},{33,49},{49,1},{2,18}... | collective-permute-start | bytes 196616 | tf_op jit(solution)/shard_map/ppermute | solution.py:220
  63.8 8.6 %collective-permute-start.5 = (bf16[64,8,128]{2,1,0:T(8,128)(2,1)S(1)}, bf16[64,8,128]{2,1,0:T(8,128)(2,1)S(1)}, u32[]{:S(2)}, u32[]{:S(2)}) collective-permute-start(bf16[64,8,128]{2,1,0:T(8,128)(2,1)S(1)} %all-to-all-done.1.in_ref), channel_id=1, source_target_pairs={{0,128},{64,192},{128,0},{192,64},{1,129},{65,193},{129,1},{193,65... | collective-permute-start | bytes 393224 | tf_op jit(solution)/shard_map/ppermute | solution.py:220
  65.7 8.0 %collective-permute-start.4 = (bf16[64,8,128]{2,1,0:T(8,128)(2,1)S(1)}, bf16[64,8,128]{2,1,0:T(8,128)(2,1)S(1)}, u32[]{:S(2)}, u32[]{:S(2)}) collective-permute-start(bf16[64,8,128]{2,1,0:T(8,128)(2,1)S(1)} %all-to-all-done.1.in_ref), channel_id=1, source_target_pairs={{0,192},{64,0},{128,64},{192,128},{1,193},{65,1},{129,65},{193,129... | collective-permute-start | bytes 393224 | tf_op jit(solution)/shard_map/ppermute | solution.py:220
  66.6 7.1 %collective-permute-start.3 = (bf16[64,8,128]{2,1,0:T(8,128)(2,1)S(1)}, bf16[64,8,128]{2,1,0:T(8,128)(2,1)S(1)}, u32[]{:S(2)}, u32[]{:S(2)}) collective-permute-start(bf16[64,8,128]{2,1,0:T(8,128)(2,1)S(1)} %all-to-all-done.1.in_ref), channel_id=1, source_target_pairs={{0,64},{64,128},{128,192},{192,0},{1,65},{65,129},{129,193},{193,1... | collective-permute-start | bytes 393224 | tf_op jit(solution)/shard_map/ppermute | solution.py:220
  67.2 5.2 %collective-permute-start.10 = (bf16[64,512]{1,0:T(8,128)(2,1)S(1)}, bf16[64,512]{1,0:T(8,128)(2,1)S(1)}, u32[]{:S(2)}, u32[]{:S(2)}) collective-permute-start(bf16[64,512]{1,0:T(8,128)(2,1)S(1)} %get-tuple-element.37), channel_id=1, source_target_pairs={{0,32},{16,48},{32,0},{48,16},{1,33},{17,49},{33,1},{49,17},{2,34}... | collective-permute-start | bytes 196616 | tf_op jit(solution)/shard_map/ppermute | solution.py:220
  67.9 4.5 %collective-permute-start.11 = (bf16[64,512]{1,0:T(8,128)(2,1)S(1)}, bf16[64,512]{1,0:T(8,128)(2,1)S(1)}, u32[]{:S(2)}, u32[]{:S(2)}) collective-permute-start(bf16[64,512]{1,0:T(8,128)(2,1)S(1)} %get-tuple-element.38), channel_id=1, source_target_pairs={{0,48},{16,0},{32,16},{48,32},{1,49},{17,1},{33,17},{49,33},{2,50}... | collective-permute-start | bytes 196616 | tf_op jit(solution)/shard_map/ppermute | solution.py:220

commit v8 on v7

--- a/solution.py
+++ b/solution.py
@@ -36,19 +36,9 @@
 
 
 def gelu_slope(values):
-    size = jnp.abs(values)
-    t = 1.0 / (1.0 + 0.28 * size)
-    m = -0.10580839289759565
-    for c in (
-        0.38987462028162295,
-        -0.23699444704250228,
-        0.26891093471374405,
-        0.06749644895015629,
-        0.11652082672551742,
-    ):
-        m = m * t + c
-    below = jnp.exp(-0.5 * values * values) * (m * t - size * (1.0 / math.sqrt(2.0 * math.pi)))
-    return jnp.where(values >= 0.0, 1.0 - below, below)
+    normal_cdf = 0.5 * (1.0 + lax.erf(values * (1.0 / math.sqrt(2.0))))
+    density = jnp.exp(-0.5 * values * values) * (1.0 / math.sqrt(2.0 * math.pi))
+    return normal_cdf + values * density
 
 
 def dot(a, b, dims=None):
@@ -121,15 +111,22 @@
         copy.wait()
 
 
-def sum_y_kernel(moves_ref, own_ref, one_ref, two_ref, three_ref, out_ref):
+def sum_y_kernel(moves_ref, own_ref, one_ref, two_ref, three_ref, out_hbm, out, sems):
     total = one_ref[...].astype(F32) + two_ref[...].astype(F32) + three_ref[...].astype(F32)
     low = (total + own_ref[...].astype(F32)).astype(BF16)
-    out = dot(moves_ref[0], low[:, :256]) + dot(moves_ref[1], low[:, 256:])
-    out_ref[...] = out.reshape(64, 8, 256).astype(BF16)
-
-
-def modes_kernel(factor, in_ref, w_ref, out_ref, *rest):
-    side_refs, chunks = rest[:4], rest[4]
+    copies = []
+    for i in range(4):
+        rows, blocks = slice(128 * i, 128 * i + 128), slice(16 * i, 16 * i + 16)
+        part = dot(moves_ref[0, rows], low[:, :256]) + dot(moves_ref[1, rows], low[:, 256:])
+        out[blocks] = part.reshape(16, 8, 256).astype(BF16)
+        copies.append(pltpu.make_async_copy(out.at[blocks], out_hbm.at[blocks], sems.at[i]))
+        copies[-1].start()
+    for copy in copies:
+        copy.wait()
+
+
+def modes_kernel(factor, in_ref, w_ref, out_hbm, *rest):
+    side_refs, (chunks, out_ref, sem) = rest[:4], rest[4:]
     x, w_mine, zl_mine, y_mine = (lax.axis_index(name) for name in ("x", "w", "zl", "y"))
     total = jnp.sum(in_ref[...].astype(F32).reshape(16, 4, 8, 256), axis=1).reshape(128, 256)
     first_mode = (x == 0) & (w_mine == 0) & (zl_mine == 0)
@@ -151,12 +148,15 @@
     out = out.reshape(16, 8, 128).astype(BF16)
     for zl in range(4):
         out_ref[:, zl] = out
+    copy = pltpu.make_async_copy(out_ref, out_hbm, sem)
+    copy.start()
     for y in range(4):
         lanes = slice(128 * y, 128 * y + 128)
         chunks[y] = jnp.concatenate([g[8 * w : 8 * w + 8, lanes] for w in range(4)], axis=1)
     for t in range(4):
         chunk = chunks[(y_mine + t) & 3]
         side_refs[t][...] = jnp.concatenate([u, chunk], axis=0).astype(BF16)
+    copy.wait()
 
 
 def weight_kernel(*refs):
@@ -258,8 +258,9 @@
     send = pl.pallas_call(
         sum_y_kernel,
         in_specs=[vmem] * 5,
-        out_specs=vmem,
+        out_specs=hbm,
         out_shape=block(64, 8, 256),
+        scratch_shapes=[pltpu.VMEM((64, 8, 256), BF16), pltpu.SemaphoreType.DMA((4,))],
         compiler_params=params,
         name="sum_y",
     )(moves, own, one, two, three)
@@ -268,9 +269,13 @@
     send, *sides = pl.pallas_call(
         functools.partial(modes_kernel, factor),
         in_specs=[vmem, vmem],
-        out_specs=[vmem] * 5,
+        out_specs=[hbm] + [vmem] * 4,
         out_shape=[block(16, 4, 8, 128)] + [block(40, 512)] * 4,
-        scratch_shapes=[pltpu.VMEM((4, 8, 512), F32)],
+        scratch_shapes=[
+            pltpu.VMEM((4, 8, 512), F32),
+            pltpu.VMEM((16, 4, 8, 128), BF16),
+            pltpu.SemaphoreType.DMA,
+        ],
         compiler_params=params,
         name="modes",
     )(got, mine)

time: 75.9 us -> 75 us (0.988)
  Pallas kernels: 15.6 us -> 13.7 us
  starting transfers between devices: 36.6 us -> 37.7 us
    pallas_call x3, Pallas kernels: 9.53 us -> 7.59 us  [spectra(): pl.pallas_call(functools.partial(spectra_kernel, steps), in_specs=[hbm] *...]
    ppermute x12, starting transfers between devices: 18.1 us -> 19.6 us  [shifted(): lax.ppermute(value, axis, [(i, (i + distance) % 4) for i in range(4)])]
  transfers between devices with their start and end apart: 14 -> 14, of which waited for: 8 -> 7; matrix products, arithmetic and copies ran while one was open for 2% -> 2% of each run, Pallas kernels for 12% -> 10%
where the time goes in v8:
time: 75 us; the launch traced here: 74.7 us
  starting transfers between devices  37.7 us (50%)
  waiting for transfers between devices  21.2 us (28%)
  Pallas kernels  13.7 us (18%)
  local copies, waits for them, and re-layouts  1.3 us (2%)
  between operations  0.89 us (1%)
    ppermute x12, starting transfers between devices, shifted(): lax.ppermute(value, axis, [(i, (i + distance) % 4) for i in range(4)])  19.6 us
    all_to_all x1, starting transfers between devices, shards(): got = lax.all_to_all(send, OTHERS, 0, 0, tiled=True)  13 us
    all_to_all x1, waiting for transfers between devices, shards(): got = lax.all_to_all(send, OTHERS, 0, 0, tiled=True)  11.5 us
    ppermute x12, waiting for transfers between devices, shifted(): lax.ppermute(value, axis, [(i, (i + distance) % 4) for i in range(4)])  8.11 us
    pallas_call x3, Pallas kernels, spectra(): pl.pallas_call(functools.partial(spectra_kernel, steps), in_specs=[hbm] *...  7.59 us
    all_to_all x1, starting transfers between devices, shards(): got = lax.all_to_all(send.reshape(64, 8, 128), OTHERS, 0, 0, tiled=True)  5.1 us
    pallas_call x1, Pallas kernels, shards(): pl.pallas_call(functools.partial(last_kernel, factor), in_specs=[vmem] *...  1.72 us
    all_to_all x1, waiting for transfers between devices, shards(): got = lax.all_to_all(send.reshape(64, 8, 128), OTHERS, 0, 0, tiled=True)  1.51 us
  transfers between devices with their start and end apart: 14, of which 7 were waited for; matrix products, arithmetic and copies ran while one was open for 2% of the time, Pallas kernels for 10%

profile of v8, /device:TPU:1, one launch (start us, length us, event | category | flops | bytes accessed | tf_op | source)
XLA Modules:
  0.0 74.7 jit_solution(12200234489909163859)
XLA Ops:
  0.6 2.0 %spectra.3 = (f32[8,128]{1,0:T(8,128)S(1)}, bf16[256,512]{1,0:T(8,128)(2,1)S(1)}) custom-call(bf16[4,512,512]{2,1,0:T(8,128)(2,1)} %fields_hbm.5, bf16[4,512,512]{2,1,0:T(8,128)(2,1)} %pre_hbm.5, bf16[4,512,512]{2,1,0:T(8,128)(2,1)} %cot_hbm.5, bf16[4,512,512]{2,1,0:T(8,128)(2,1)} %fields_hbm.5), custom_call_target="tpu_custom_call" | custom-call | flops 268435456 | bytes 4194304 | tf_op jit(solution)/shard_map/spectra/pallas_call | solution.py:240
  2.7 3.8 %collective-permute-start.1 = (bf16[256,512]{1,0:T(8,128)(2,1)S(1)}, bf16[256,512]{1,0:T(8,128)(2,1)S(1)}, u32[]{:S(2)}, u32[]{:S(2)}) collective-permute-start(bf16[256,512]{1,0:T(8,128)(2,1)S(1)} %get-tuple-element.27), channel_id=1, source_target_pairs={{0,128},{64,192},{128,0},{192,64},{1,129},{65,193},{129,1},{193,65... | collective-permute-start | bytes 786440 | tf_op jit(solution)/shard_map/ppermute | solution.py:220
  6.5 2.9 %spectra.4 = (f32[8,128]{1,0:T(8,128)S(1)}, bf16[256,512]{1,0:T(8,128)(2,1)S(1)}, bf16[256,512]{1,0:T(8,128)(2,1)S(1)}) custom-call(bf16[4,512,512]{2,1,0:T(8,128)(2,1)} %fields_hbm.5, bf16[4,512,512]{2,1,0:T(8,128)(2,1)} %pre_hbm.5, bf16[4,512,512]{2,1,0:T(8,128)(2,1)} %cot_hbm.5, f32[8,128]{1,0:T(8,128)S(1)} %get-tuple-element.22._), custom_call_target="tpu_custom_call" | custom-call | flops 536870912 | bytes 8388608 | tf_op jit(solution)/shard_map/spectra/pallas_call | solution.py:240
  9.5 0.5 collective-permute-start
  9.9 2.3 %collective-permute-start.2 = (bf16[256,512]{1,0:T(8,128)(2,1)S(1)}, bf16[256,512]{1,0:T(8,128)(2,1)S(1)}, u32[]{:S(2)}, u32[]{:S(2)}) collective-permute-start(bf16[256,512]{1,0:T(8,128)(2,1)S(1)} %get-tuple-element.28), channel_id=1, source_target_pairs={{0,192},{64,0},{128,64},{192,128},{1,193},{65,1},{129,65},{193,129... | collective-permute-start | bytes 786440 | tf_op jit(solution)/shard_map/ppermute | solution.py:220
  12.2 2.6 %spectra.5 = (f32[8,128]{1,0:T(8,128)}, bf16[256,512]{1,0:T(8,128)(2,1)S(1)}, bf16[2,512,256]{2,1,0:T(8,128)(2,1)S(1)}) custom-call(bf16[4,512,512]{2,1,0:T(8,128)(2,1)} %fields_hbm.5, bf16[4,512,512]{2,1,0:T(8,128)(2,1)} %pre_hbm.5, bf16[4,512,512]{2,1,0:T(8,128)(2,1)} %cot_hbm.5, f32[8,128]{1,0:T(8,128)S(1)} %get-tuple-element.23._), custom_call_target="tpu_custom_call" | custom-call | flops 268435456 | bytes 4194304 | tf_op jit(solution)/shard_map/spectra/pallas_call | solution.py:240
  14.8 0.0 collective-permute-done.1.two_ref
  14.8 3.5 %collective-permute-done.one_ref = bf16[256,512]{1,0:T(8,128)(2,1)S(1)} collective-permute-done((bf16[256,512]{1,0:T(8,128)(2,1)S(1)}, bf16[256,512]{1,0:T(8,128)(2,1)S(1)}, u32[]{:S(2)}, u32[]{:S(2)}) %collective-permute-start) | collective-permute-done | bytes 262176 | tf_op jit(solution)/shard_map/ppermute | solution.py:220
  18.3 0.0 collective-permute-done.2.three_ref
  18.3 1.1 %sum_y.1 = bf16[64,8,256]{2,1,0:T(8,128)(2,1)} custom-call(bf16[2,512,256]{2,1,0:T(8,128)(2,1)S(1)} %get-tuple-element.24.moves_ref, bf16[256,512]{1,0:T(8,128)(2,1)S(1)} %get-tuple-element.25.own_ref, bf16[256,512]{1,0:T(8,128)(2,1)S(1)} %collective-permute-done.one_ref, bf16[256,512]{1,0:T(8,128)(2,1)S(1)} %collective-permute-done.1.two_ref, ...), custom_call_target="tpu_custom_call" | custom-call | tf_op jit(solution)/shard_map/sum_y/pallas_call | solution.py:258
  19.4 13.0 %all-to-all-start = ((bf16[64,8,256]{2,1,0:T(8,128)(2,1)}), bf16[64,8,256]{2,1,0:T(8,128)(2,1)S(1)}, u32[]{:S(2)}, u32[]{:S(2)}) async-start(bf16[64,8,256]{2,1,0:T(8,128)(2,1)} %sum_y.1), calls=%async_computation | async-start | bytes 524288 | tf_op jit(solution)/shard_map/all_to_all | solution.py:267
  32.4 1.3 %dynamic-slice_bitcast_fusion.w_ref = bf16[2,512,512]{2,1,0:T(8,128)(2,1)S(1)} fusion(bf16[4,2,512,512]{3,2,1,0:T(8,128)(2,1)} %param.7, s32[]{:T(128)S(6)} %select_n.4), kind=kLoop, calls=%fused_computation | loop fusion | bytes 2097156 | tf_op jit(solution)/shard_map/jit(dynamic_index_in_dim)/squeeze | solution.py:268
  33.7 11.5 %all-to-all-done.in_ref = bf16[64,8,256]{2,1,0:T(8,128)(2,1)S(1)} async-done(((bf16[64,8,256]{2,1,0:T(8,128)(2,1)}), bf16[64,8,256]{2,1,0:T(8,128)(2,1)S(1)}, u32[]{:S(2)}, u32[]{:S(2)}) %all-to-all-start) | async-done | bytes 262176 | tf_op jit(solution)/shard_map/all_to_all | solution.py:267
  45.2 1.5 %modes.1 = (bf16[16,4,8,128]{3,2,1,0:T(8,128)(2,1)}, bf16[40,512]{1,0:T(8,128)(2,1)S(1)}, bf16[40,512]{1,0:T(8,128)(2,1)S(1)}, bf16[40,512]{1,0:T(8,128)(2,1)S(1)}, bf16[40,512]{1,0:T(8,128)(2,1)S(1)}) custom-call(bf16[64,8,256]{2,1,0:T(8,128)(2,1)S(1)} %all-to-all-done.in_ref, bf16[2,512,512]{2,1,0:T(8,128)(2,1)S(1)} %dynamic-slice_bitcast_fusion.w_ref), custom_call_target="tpu_custom_call" | custom-call | tf_op jit(solution)/shard_map/modes/pallas_call | solution.py:269
  46.7 5.1 %all-to-all-start.1 = ((bf16[64,8,128]{2,1,0:T(8,128)(2,1)}), bf16[64,8,128]{2,1,0:T(8,128)(2,1)S(1)}, u32[]{:S(2)}, u32[]{:S(2)}) async-start(bf16[64,8,128]{2,1,0:T(8,128)(2,1)} %bitcast.1), calls=%async_computation.1 | async-start | bytes 262144 | tf_op jit(solution)/shard_map/all_to_all | solution.py:283
  51.8 1.2 %collective-permute-start.6 = (bf16[40,512]{1,0:T(8,128)(2,1)S(1)}, bf16[40,512]{1,0:T(8,128)(2,1)S(1)}, u32[]{:S(2)}, u32[]{:S(2)}) collective-permute-start(bf16[40,512]{1,0:T(8,128)(2,1)S(1)} %get-tuple-element.32), channel_id=1, source_target_pairs={{0,64},{64,128},{128,192},{192,0},{1,65},{65,129},{129,193},{193,1... | collective-permute-start | bytes 122888 | tf_op jit(solution)/shard_map/ppermute | solution.py:220
  53.0 3.0 %collective-permute-start.7 = (bf16[40,512]{1,0:T(8,128)(2,1)S(1)}, bf16[40,512]{1,0:T(8,128)(2,1)S(1)}, u32[]{:S(2)}, u32[]{:S(2)}) collective-permute-start(bf16[40,512]{1,0:T(8,128)(2,1)S(1)} %get-tuple-element.33), channel_id=1, source_target_pairs={{0,128},{64,192},{128,0},{192,64},{1,129},{65,193},{129,1},{193,65... | collective-permute-start | bytes 122888 | tf_op jit(solution)/shard_map/ppermute | solution.py:220
  56.0 0.6 collective-permute-start.8
  56.5 1.6 %collective-permute-done.7.refs_2_ = bf16[40,512]{1,0:T(8,128)(2,1)S(1)} collective-permute-done((bf16[40,512]{1,0:T(8,128)(2,1)S(1)}, bf16[40,512]{1,0:T(8,128)(2,1)S(1)}, u32[]{:S(2)}, u32[]{:S(2)}) %collective-permute-start.7) | collective-permute-done | bytes 40992 | tf_op jit(solution)/shard_map/ppermute | solution.py:220
  58.1 1.0 %collective-permute-done.8.refs_3_ = bf16[40,512]{1,0:T(8,128)(2,1)S(1)} collective-permute-done((bf16[40,512]{1,0:T(8,128)(2,1)S(1)}, bf16[40,512]{1,0:T(8,128)(2,1)S(1)}, u32[]{:S(2)}, u32[]{:S(2)}) %collective-permute-start.8) | collective-permute-done | bytes 40992 | tf_op jit(solution)/shard_map/ppermute | solution.py:220
  59.1 0.4 weight.1
  59.5 1.6 %collective-permute-start.9 = (bf16[64,512]{1,0:T(8,128)(2,1)S(1)}, bf16[64,512]{1,0:T(8,128)(2,1)S(1)}, u32[]{:S(2)}, u32[]{:S(2)}) collective-permute-start(bf16[64,512]{1,0:T(8,128)(2,1)S(1)} %get-tuple-element.36), channel_id=1, source_target_pairs={{0,16},{16,32},{32,48},{48,0},{1,17},{17,33},{33,49},{49,1},{2,18}... | collective-permute-start | bytes 196616 | tf_op jit(solution)/shard_map/ppermute | solution.py:220
  61.2 1.5 %all-to-all-done.1.in_ref = bf16[64,8,128]{2,1,0:T(8,128)(2,1)S(1)} async-done(((bf16[64,8,128]{2,1,0:T(8,128)(2,1)}), bf16[64,8,128]{2,1,0:T(8,128)(2,1)S(1)}, u32[]{:S(2)}, u32[]{:S(2)}) %all-to-all-start.1) | async-done | bytes 131104 | tf_op jit(solution)/shard_map/all_to_all | solution.py:283
  62.7 2.6 %collective-permute-start.5 = (bf16[64,8,128]{2,1,0:T(8,128)(2,1)S(1)}, bf16[64,8,128]{2,1,0:T(8,128)(2,1)S(1)}, u32[]{:S(2)}, u32[]{:S(2)}) collective-permute-start(bf16[64,8,128]{2,1,0:T(8,128)(2,1)S(1)} %all-to-all-done.1.in_ref), channel_id=1, source_target_pairs={{0,128},{64,192},{128,0},{192,64},{1,129},{65,193},{129,1},{193,65... | collective-permute-start | bytes 393224 | tf_op jit(solution)/shard_map/ppermute | solution.py:220
  65.3 0.9 %collective-permute-start.4 = (bf16[64,8,128]{2,1,0:T(8,128)(2,1)S(1)}, bf16[64,8,128]{2,1,0:T(8,128)(2,1)S(1)}, u32[]{:S(2)}, u32[]{:S(2)}) collective-permute-start(bf16[64,8,128]{2,1,0:T(8,128)(2,1)S(1)} %all-to-all-done.1.in_ref), channel_id=1, source_target_pairs={{0,192},{64,0},{128,64},{192,128},{1,193},{65,1},{129,65},{193,129... | collective-permute-start | bytes 393224 | tf_op jit(solution)/shard_map/ppermute | solution.py:220
  66.2 0.5 collective-permute-start.3
  66.7 0.7 collective-permute-start.10
  67.4 1.9 %collective-permute-start.11 = (bf16[64,512]{1,0:T(8,128)(2,1)S(1)}, bf16[64,512]{1,0:T(8,128)(2,1)S(1)}, u32[]{:S(2)}, u32[]{:S(2)}) collective-permute-start(bf16[64,512]{1,0:T(8,128)(2,1)S(1)} %get-tuple-element.38), channel_id=1, source_target_pairs={{0,48},{16,0},{32,16},{48,32},{1,49},{17,1},{33,17},{49,33},{2,50}... | collective-permute-start | bytes 196616 | tf_op jit(solution)/shard_map/ppermute | solution.py:220
  69.4 1.4 %own_field.1 = (bf16[4,512,512]{2,1,0:T(8,128)(2,1)}, bf16[512,128]{1,0:T(8,128)(2,1)S(1)}) custom-call(bf16[64,8,128]{2,1,0:T(8,128)(2,1)S(1)} %all-to-all-done.1.in_ref), custom_call_target="tpu_custom_call" | custom-call | flops 134217728 | bytes 1048576 | tf_op jit(solution)/shard_map/own_field/pallas_call | solution.py:296
  70.8 1.2 %collective-permute-done.10.refs_6_ = bf16[64,512]{1,0:T(8,128)(2,1)S(1)} collective-permute-done((bf16[64,512]{1,0:T(8,128)(2,1)S(1)}, bf16[64,512]{1,0:T(8,128)(2,1)S(1)}, u32[]{:S(2)}, u32[]{:S(2)}) %collective-permute-start.10) | collective-permute-done | bytes 65568 | tf_op jit(solution)/shard_map/ppermute | solution.py:220
  71.9 0.9 %collective-permute-done.4.refs_1_ = bf16[64,8,128]{2,1,0:T(8,128)(2,1)S(1)} collective-permute-done((bf16[64,8,128]{2,1,0:T(8,128)(2,1)S(1)}, bf16[64,8,128]{2,1,0:T(8,128)(2,1)S(1)}, u32[]{:S(2)}, u32[]{:S(2)}) %collective-permute-start.4) | collective-permute-done | bytes 131104 | tf_op jit(solution)/shard_map/ppermute | solution.py:220
  72.8 1.7 %last.1 = (bf16[4,512,512]{2,1,0:T(8,128)(2,1)}, f32[4,2,32,512]{3,2,1,0:T(8,128)}) custom-call(bf16[64,8,128]{2,1,0:T(8,128)(2,1)S(1)} %collective-permute-done.3.refs_0_, bf16[64,8,128]{2,1,0:T(8,128)(2,1)S(1)} %collective-permute-done.4.refs_1_, bf16[64,8,128]{2,1,0:T(8,128)(2,1)S(1)} %collective-permute-done.5.refs_2_, ...), custom_call_target="tpu_custom_call", output_to_operand_aliasing={{0}: (8, {})} | custom-call | tf_op jit(solution)/shard_map/last/pallas_call | solution.py:310
  (5 shorter events, 0.0 us)
Async XLA Ops:
  2.7 12.2 %collective-permute-start.1 = (bf16[256,512]{1,0:T(8,128)(2,1)S(1)}, bf16[256,512]{1,0:T(8,128)(2,1)S(1)}, u32[]{:S(2)}, u32[]{:S(2)}) collective-permute-start(bf16[256,512]{1,0:T(8,128)(2,1)S(1)} %get-tuple-element.27), channel_id=1, source_target_pairs={{0,128},{64,192},{128,0},{192,64},{1,129},{65,193},{129,1},{193,65... | collective-permute-start | bytes 786440 | tf_op jit(solution)/shard_map/ppermute | solution.py:220
  9.5 8.9 %collective-permute-start = (bf16[256,512]{1,0:T(8,128)(2,1)S(1)}, bf16[256,512]{1,0:T(8,128)(2,1)S(1)}, u32[]{:S(2)}, u32[]{:S(2)}) collective-permute-start(bf16[256,512]{1,0:T(8,128)(2,1)S(1)} %get-tuple-element.26), channel_id=1, source_target_pairs={{0,64},{64,128},{128,192},{192,0},{1,65},{65,129},{129,193},{193,1... | collective-permute-start | bytes 786440 | tf_op jit(solution)/shard_map/ppermute | solution.py:220
  9.9 8.4 %collective-permute-start.2 = (bf16[256,512]{1,0:T(8,128)(2,1)S(1)}, bf16[256,512]{1,0:T(8,128)(2,1)S(1)}, u32[]{:S(2)}, u32[]{:S(2)}) collective-permute-start(bf16[256,512]{1,0:T(8,128)(2,1)S(1)} %get-tuple-element.28), channel_id=1, source_target_pairs={{0,192},{64,0},{128,64},{192,128},{1,193},{65,1},{129,65},{193,129... | collective-permute-start | bytes 786440 | tf_op jit(solution)/shard_map/ppermute | solution.py:220
  19.4 25.8 %all-to-all-start = ((bf16[64,8,256]{2,1,0:T(8,128)(2,1)}), bf16[64,8,256]{2,1,0:T(8,128)(2,1)S(1)}, u32[]{:S(2)}, u32[]{:S(2)}) async-start(bf16[64,8,256]{2,1,0:T(8,128)(2,1)} %sum_y.1), calls=%async_computation | async-start | bytes 524288 | tf_op jit(solution)/shard_map/all_to_all | solution.py:267
  46.7 16.0 %all-to-all-start.1 = ((bf16[64,8,128]{2,1,0:T(8,128)(2,1)}), bf16[64,8,128]{2,1,0:T(8,128)(2,1)S(1)}, u32[]{:S(2)}, u32[]{:S(2)}) async-start(bf16[64,8,128]{2,1,0:T(8,128)(2,1)} %bitcast.1), calls=%async_computation.1 | async-start | bytes 262144 | tf_op jit(solution)/shard_map/all_to_all | solution.py:283
  51.8 4.7 %collective-permute-start.6 = (bf16[40,512]{1,0:T(8,128)(2,1)S(1)}, bf16[40,512]{1,0:T(8,128)(2,1)S(1)}, u32[]{:S(2)}, u32[]{:S(2)}) collective-permute-start(bf16[40,512]{1,0:T(8,128)(2,1)S(1)} %get-tuple-element.32), channel_id=1, source_target_pairs={{0,64},{64,128},{128,192},{192,0},{1,65},{65,129},{129,193},{193,1... | collective-permute-start | bytes 122888 | tf_op jit(solution)/shard_map/ppermute | solution.py:220
  53.0 5.1 %collective-permute-start.7 = (bf16[40,512]{1,0:T(8,128)(2,1)S(1)}, bf16[40,512]{1,0:T(8,128)(2,1)S(1)}, u32[]{:S(2)}, u32[]{:S(2)}) collective-permute-start(bf16[40,512]{1,0:T(8,128)(2,1)S(1)} %get-tuple-element.33), channel_id=1, source_target_pairs={{0,128},{64,192},{128,0},{192,64},{1,129},{65,193},{129,1},{193,65... | collective-permute-start | bytes 122888 | tf_op jit(solution)/shard_map/ppermute | solution.py:220
  56.0 3.1 %collective-permute-start.8 = (bf16[40,512]{1,0:T(8,128)(2,1)S(1)}, bf16[40,512]{1,0:T(8,128)(2,1)S(1)}, u32[]{:S(2)}, u32[]{:S(2)}) collective-permute-start(bf16[40,512]{1,0:T(8,128)(2,1)S(1)} %get-tuple-element.34), channel_id=1, source_target_pairs={{0,192},{64,0},{128,64},{192,128},{1,193},{65,1},{129,65},{193,129... | collective-permute-start | bytes 122888 | tf_op jit(solution)/shard_map/ppermute | solution.py:220
  59.5 7.9 %collective-permute-start.9 = (bf16[64,512]{1,0:T(8,128)(2,1)S(1)}, bf16[64,512]{1,0:T(8,128)(2,1)S(1)}, u32[]{:S(2)}, u32[]{:S(2)}) collective-permute-start(bf16[64,512]{1,0:T(8,128)(2,1)S(1)} %get-tuple-element.36), channel_id=1, source_target_pairs={{0,16},{16,32},{32,48},{48,0},{1,17},{17,33},{33,49},{49,1},{2,18}... | collective-permute-start | bytes 196616 | tf_op jit(solution)/shard_map/ppermute | solution.py:220
  62.7 9.3 %collective-permute-start.5 = (bf16[64,8,128]{2,1,0:T(8,128)(2,1)S(1)}, bf16[64,8,128]{2,1,0:T(8,128)(2,1)S(1)}, u32[]{:S(2)}, u32[]{:S(2)}) collective-permute-start(bf16[64,8,128]{2,1,0:T(8,128)(2,1)S(1)} %all-to-all-done.1.in_ref), channel_id=1, source_target_pairs={{0,128},{64,192},{128,0},{192,64},{1,129},{65,193},{129,1},{193,65... | collective-permute-start | bytes 393224 | tf_op jit(solution)/shard_map/ppermute | solution.py:220
  65.3 7.5 %collective-permute-start.4 = (bf16[64,8,128]{2,1,0:T(8,128)(2,1)S(1)}, bf16[64,8,128]{2,1,0:T(8,128)(2,1)S(1)}, u32[]{:S(2)}, u32[]{:S(2)}) collective-permute-start(bf16[64,8,128]{2,1,0:T(8,128)(2,1)S(1)} %all-to-all-done.1.in_ref), channel_id=1, source_target_pairs={{0,192},{64,0},{128,64},{192,128},{1,193},{65,1},{129,65},{193,129... | collective-permute-start | bytes 393224 | tf_op jit(solution)/shard_map/ppermute | solution.py:220
  66.2 6.6 %collective-permute-start.3 = (bf16[64,8,128]{2,1,0:T(8,128)(2,1)S(1)}, bf16[64,8,128]{2,1,0:T(8,128)(2,1)S(1)}, u32[]{:S(2)}, u32[]{:S(2)}) collective-permute-start(bf16[64,8,128]{2,1,0:T(8,128)(2,1)S(1)} %all-to-all-done.1.in_ref), channel_id=1, source_target_pairs={{0,64},{64,128},{128,192},{192,0},{1,65},{65,129},{129,193},{193,1... | collective-permute-start | bytes 393224 | tf_op jit(solution)/shard_map/ppermute | solution.py:220
  66.7 5.2 %collective-permute-start.10 = (bf16[64,512]{1,0:T(8,128)(2,1)S(1)}, bf16[64,512]{1,0:T(8,128)(2,1)S(1)}, u32[]{:S(2)}, u32[]{:S(2)}) collective-permute-start(bf16[64,512]{1,0:T(8,128)(2,1)S(1)} %get-tuple-element.37), channel_id=1, source_target_pairs={{0,32},{16,48},{32,0},{48,16},{1,33},{17,49},{33,1},{49,17},{2,34}... | collective-permute-start | bytes 196616 | tf_op jit(solution)/shard_map/ppermute | solution.py:220
  67.4 4.5 %collective-permute-start.11 = (bf16[64,512]{1,0:T(8,128)(2,1)S(1)}, bf16[64,512]{1,0:T(8,128)(2,1)S(1)}, u32[]{:S(2)}, u32[]{:S(2)}) collective-permute-start(bf16[64,512]{1,0:T(8,128)(2,1)S(1)} %get-tuple-element.38), channel_id=1, source_target_pairs={{0,48},{16,0},{32,16},{48,32},{1,49},{17,1},{33,17},{49,33},{2,50}... | collective-permute-start | bytes 196616 | tf_op jit(solution)/shard_map/ppermute | solution.py:220

commit v9 on v8

--- a/solution.py
+++ b/solution.py
@@ -115,10 +115,10 @@
     total = one_ref[...].astype(F32) + two_ref[...].astype(F32) + three_ref[...].astype(F32)
     low = (total + own_ref[...].astype(F32)).astype(BF16)
     copies = []
-    for i in range(4):
-        rows, blocks = slice(128 * i, 128 * i + 128), slice(16 * i, 16 * i + 16)
+    for i in range(2):
+        rows, blocks = slice(256 * i, 256 * i + 256), slice(32 * i, 32 * i + 32)
         part = dot(moves_ref[0, rows], low[:, :256]) + dot(moves_ref[1, rows], low[:, 256:])
-        out[blocks] = part.reshape(16, 8, 256).astype(BF16)
+        out[blocks] = part.reshape(32, 8, 256).astype(BF16)
         copies.append(pltpu.make_async_copy(out.at[blocks], out_hbm.at[blocks], sems.at[i]))
         copies[-1].start()
     for copy in copies:
@@ -134,11 +134,18 @@
     g_scale = jnp.where(first_mode, factor, 2.0 * factor)
     low = (total * jnp.where(is_u, factor, g_scale)).astype(BF16)
     digits = [(32, 2, 2), (8, 4, 8), (4, 2, 1), (1, 4, 32)]
-    both = [dot(row_moves((64, 128), digits, base=4 * h), low) for h in range(2)]
+    row = lax.broadcasted_iota(jnp.int32, (32, 128), 0)
+    col = lax.broadcasted_iota(jnp.int32, (32, 128), 1)
+    source = ((row >> 3) << 3) + (((row >> 2) & 1) ^ 1) + ((row & 3) << 5)
+    sign = jnp.where((row & 4) == 0, 1.0, -1.0)
+    both = []
+    for h in range(2):
+        turns = jnp.where(source + 4 * h == col, sign, 0.0).astype(BF16)
+        moves = row_moves((64, 128), digits, base=4 * h)
+        both.append(dot(jnp.concatenate([moves, turns], axis=0), low))
     both = jnp.concatenate(both, axis=1)
-    g, u = both[:32], both[32:]
-    g_low = g.astype(BF16)
-    g_turned = dot(turned(32), g_low).astype(BF16)
+    g, u = both[:32], both[32:64]
+    g_low, g_turned = g.astype(BF16), both[64:].astype(BF16)
     grad = (dot(g_low, w_ref[0], NT) + dot(g_turned, w_ref[1], NT)).astype(BF16)
     out = None
     for q in range(4):
@@ -260,7 +267,7 @@
         in_specs=[vmem] * 5,
         out_specs=hbm,
         out_shape=block(64, 8, 256),
-        scratch_shapes=[pltpu.VMEM((64, 8, 256), BF16), pltpu.SemaphoreType.DMA((4,))],
+        scratch_shapes=[pltpu.VMEM((64, 8, 256), BF16), pltpu.SemaphoreType.DMA((2,))],
         compiler_params=params,
         name="sum_y",
     )(moves, own, one, two, three)

time: 75 us -> 74.9 us (level)
  no operation moved by 1% of the time
where the time goes in v9:
time: 74.9 us; the launch traced here: 74.6 us
  starting transfers between devices  37.5 us (50%)
  waiting for transfers between devices  21.3 us (28%)
  Pallas kernels  13.6 us (18%)
  local copies, waits for them, and re-layouts  1.3 us (2%)
  between operations  0.89 us (1%)
    ppermute x12, starting transfers between devices, shifted(): lax.ppermute(value, axis, [(i, (i + distance) % 4) for i in range(4)])  19.5 us
    all_to_all x1, starting transfers between devices, shards(): got = lax.all_to_all(send, OTHERS, 0, 0, tiled=True)  12.9 us
    all_to_all x1, waiting for transfers between devices, shards(): got = lax.all_to_all(send, OTHERS, 0, 0, tiled=True)  11.5 us
    ppermute x12, waiting for transfers between devices, shifted(): lax.ppermute(value, axis, [(i, (i + distance) % 4) for i in range(4)])  8.1 us
    pallas_call x3, Pallas kernels, spectra(): pl.pallas_call(functools.partial(spectra_kernel, steps), in_specs=[hbm] *...  7.59 us
    all_to_all x1, starting transfers between devices, shards(): got = lax.all_to_all(send.reshape(64, 8, 128), OTHERS, 0, 0, tiled=True)  5.1 us
    pallas_call x1, Pallas kernels, shards(): pl.pallas_call(functools.partial(last_kernel, factor), in_specs=[vmem] *...  1.72 us
    all_to_all x1, waiting for transfers between devices, shards(): got = lax.all_to_all(send.reshape(64, 8, 128), OTHERS, 0, 0, tiled=True)  1.68 us
  transfers between devices with their start and end apart: 14, of which 7 were waited for; matrix products, arithmetic and copies ran while one was open for 2% of the time, Pallas kernels for 10%

profile of v9, /device:TPU:1, one launch (start us, length us, event | category | flops | bytes accessed | tf_op | source)
XLA Modules:
  0.0 74.6 jit_solution(10110870303477208411)
XLA Ops:
  0.6 2.0 %spectra.3 = (f32[8,128]{1,0:T(8,128)S(1)}, bf16[256,512]{1,0:T(8,128)(2,1)S(1)}) custom-call(bf16[4,512,512]{2,1,0:T(8,128)(2,1)} %fields_hbm.5, bf16[4,512,512]{2,1,0:T(8,128)(2,1)} %pre_hbm.5, bf16[4,512,512]{2,1,0:T(8,128)(2,1)} %cot_hbm.5, bf16[4,512,512]{2,1,0:T(8,128)(2,1)} %fields_hbm.5), custom_call_target="tpu_custom_call" | custom-call | flops 268435456 | bytes 4194304 | tf_op jit(solution)/shard_map/spectra/pallas_call | solution.py:247
  2.7 3.8 %collective-permute-start.1 = (bf16[256,512]{1,0:T(8,128)(2,1)S(1)}, bf16[256,512]{1,0:T(8,128)(2,1)S(1)}, u32[]{:S(2)}, u32[]{:S(2)}) collective-permute-start(bf16[256,512]{1,0:T(8,128)(2,1)S(1)} %get-tuple-element.27), channel_id=1, source_target_pairs={{0,128},{64,192},{128,0},{192,64},{1,129},{65,193},{129,1},{193,65... | collective-permute-start | bytes 786440 | tf_op jit(solution)/shard_map/ppermute | solution.py:227
  6.5 2.9 %spectra.4 = (f32[8,128]{1,0:T(8,128)S(1)}, bf16[256,512]{1,0:T(8,128)(2,1)S(1)}, bf16[256,512]{1,0:T(8,128)(2,1)S(1)}) custom-call(bf16[4,512,512]{2,1,0:T(8,128)(2,1)} %fields_hbm.5, bf16[4,512,512]{2,1,0:T(8,128)(2,1)} %pre_hbm.5, bf16[4,512,512]{2,1,0:T(8,128)(2,1)} %cot_hbm.5, f32[8,128]{1,0:T(8,128)S(1)} %get-tuple-element.22._), custom_call_target="tpu_custom_call" | custom-call | flops 536870912 | bytes 8388608 | tf_op jit(solution)/shard_map/spectra/pallas_call | solution.py:247
  9.5 0.5 collective-permute-start
  9.9 2.3 %collective-permute-start.2 = (bf16[256,512]{1,0:T(8,128)(2,1)S(1)}, bf16[256,512]{1,0:T(8,128)(2,1)S(1)}, u32[]{:S(2)}, u32[]{:S(2)}) collective-permute-start(bf16[256,512]{1,0:T(8,128)(2,1)S(1)} %get-tuple-element.28), channel_id=1, source_target_pairs={{0,192},{64,0},{128,64},{192,128},{1,193},{65,1},{129,65},{193,129... | collective-permute-start | bytes 786440 | tf_op jit(solution)/shard_map/ppermute | solution.py:227
  12.2 2.6 %spectra.5 = (f32[8,128]{1,0:T(8,128)}, bf16[256,512]{1,0:T(8,128)(2,1)S(1)}, bf16[2,512,256]{2,1,0:T(8,128)(2,1)S(1)}) custom-call(bf16[4,512,512]{2,1,0:T(8,128)(2,1)} %fields_hbm.5, bf16[4,512,512]{2,1,0:T(8,128)(2,1)} %pre_hbm.5, bf16[4,512,512]{2,1,0:T(8,128)(2,1)} %cot_hbm.5, f32[8,128]{1,0:T(8,128)S(1)} %get-tuple-element.23._), custom_call_target="tpu_custom_call" | custom-call | flops 268435456 | bytes 4194304 | tf_op jit(solution)/shard_map/spectra/pallas_call | solution.py:247
  14.8 3.5 %collective-permute-done.one_ref = bf16[256,512]{1,0:T(8,128)(2,1)S(1)} collective-permute-done((bf16[256,512]{1,0:T(8,128)(2,1)S(1)}, bf16[256,512]{1,0:T(8,128)(2,1)S(1)}, u32[]{:S(2)}, u32[]{:S(2)}) %collective-permute-start) | collective-permute-done | bytes 262176 | tf_op jit(solution)/shard_map/ppermute | solution.py:227
  18.3 1.1 %sum_y.1 = bf16[64,8,256]{2,1,0:T(8,128)(2,1)} custom-call(bf16[2,512,256]{2,1,0:T(8,128)(2,1)S(1)} %get-tuple-element.24.moves_ref, bf16[256,512]{1,0:T(8,128)(2,1)S(1)} %get-tuple-element.25.own_ref, bf16[256,512]{1,0:T(8,128)(2,1)S(1)} %collective-permute-done.one_ref, bf16[256,512]{1,0:T(8,128)(2,1)S(1)} %collective-permute-done.1.two_ref, ...), custom_call_target="tpu_custom_call" | custom-call | tf_op jit(solution)/shard_map/sum_y/pallas_call | solution.py:265
  19.4 12.9 %all-to-all-start = ((bf16[64,8,256]{2,1,0:T(8,128)(2,1)}), bf16[64,8,256]{2,1,0:T(8,128)(2,1)S(1)}, u32[]{:S(2)}, u32[]{:S(2)}) async-start(bf16[64,8,256]{2,1,0:T(8,128)(2,1)} %sum_y.1), calls=%async_computation | async-start | bytes 524288 | tf_op jit(solution)/shard_map/all_to_all | solution.py:274
  32.3 1.3 %dynamic-slice_bitcast_fusion.w_ref = bf16[2,512,512]{2,1,0:T(8,128)(2,1)S(1)} fusion(bf16[4,2,512,512]{3,2,1,0:T(8,128)(2,1)} %param.7, s32[]{:T(128)S(6)} %select_n.4), kind=kLoop, calls=%fused_computation | loop fusion | bytes 2097156 | tf_op jit(solution)/shard_map/jit(dynamic_index_in_dim)/squeeze | solution.py:275
  33.6 11.5 %all-to-all-done.in_ref = bf16[64,8,256]{2,1,0:T(8,128)(2,1)S(1)} async-done(((bf16[64,8,256]{2,1,0:T(8,128)(2,1)}), bf16[64,8,256]{2,1,0:T(8,128)(2,1)S(1)}, u32[]{:S(2)}, u32[]{:S(2)}) %all-to-all-start) | async-done | bytes 262176 | tf_op jit(solution)/shard_map/all_to_all | solution.py:274
  45.2 1.4 %modes.1 = (bf16[16,4,8,128]{3,2,1,0:T(8,128)(2,1)}, bf16[40,512]{1,0:T(8,128)(2,1)S(1)}, bf16[40,512]{1,0:T(8,128)(2,1)S(1)}, bf16[40,512]{1,0:T(8,128)(2,1)S(1)}, bf16[40,512]{1,0:T(8,128)(2,1)S(1)}) custom-call(bf16[64,8,256]{2,1,0:T(8,128)(2,1)S(1)} %all-to-all-done.in_ref, bf16[2,512,512]{2,1,0:T(8,128)(2,1)S(1)} %dynamic-slice_bitcast_fusion.w_ref), custom_call_target="tpu_custom_call" | custom-call | tf_op jit(solution)/shard_map/modes/pallas_call | solution.py:276
  46.6 5.1 %all-to-all-start.1 = ((bf16[64,8,128]{2,1,0:T(8,128)(2,1)}), bf16[64,8,128]{2,1,0:T(8,128)(2,1)S(1)}, u32[]{:S(2)}, u32[]{:S(2)}) async-start(bf16[64,8,128]{2,1,0:T(8,128)(2,1)} %bitcast.1), calls=%async_computation.1 | async-start | bytes 262144 | tf_op jit(solution)/shard_map/all_to_all | solution.py:290
  51.7 1.2 %collective-permute-start.6 = (bf16[40,512]{1,0:T(8,128)(2,1)S(1)}, bf16[40,512]{1,0:T(8,128)(2,1)S(1)}, u32[]{:S(2)}, u32[]{:S(2)}) collective-permute-start(bf16[40,512]{1,0:T(8,128)(2,1)S(1)} %get-tuple-element.32), channel_id=1, source_target_pairs={{0,64},{64,128},{128,192},{192,0},{1,65},{65,129},{129,193},{193,1... | collective-permute-start | bytes 122888 | tf_op jit(solution)/shard_map/ppermute | solution.py:227
  52.9 3.0 %collective-permute-start.7 = (bf16[40,512]{1,0:T(8,128)(2,1)S(1)}, bf16[40,512]{1,0:T(8,128)(2,1)S(1)}, u32[]{:S(2)}, u32[]{:S(2)}) collective-permute-start(bf16[40,512]{1,0:T(8,128)(2,1)S(1)} %get-tuple-element.33), channel_id=1, source_target_pairs={{0,128},{64,192},{128,0},{192,64},{1,129},{65,193},{129,1},{193,65... | collective-permute-start | bytes 122888 | tf_op jit(solution)/shard_map/ppermute | solution.py:227
  55.9 0.6 collective-permute-start.8
  56.4 1.6 %collective-permute-done.7.refs_2_ = bf16[40,512]{1,0:T(8,128)(2,1)S(1)} collective-permute-done((bf16[40,512]{1,0:T(8,128)(2,1)S(1)}, bf16[40,512]{1,0:T(8,128)(2,1)S(1)}, u32[]{:S(2)}, u32[]{:S(2)}) %collective-permute-start.7) | collective-permute-done | bytes 40992 | tf_op jit(solution)/shard_map/ppermute | solution.py:227
  58.0 1.0 %collective-permute-done.8.refs_3_ = bf16[40,512]{1,0:T(8,128)(2,1)S(1)} collective-permute-done((bf16[40,512]{1,0:T(8,128)(2,1)S(1)}, bf16[40,512]{1,0:T(8,128)(2,1)S(1)}, u32[]{:S(2)}, u32[]{:S(2)}) %collective-permute-start.8) | collective-permute-done | bytes 40992 | tf_op jit(solution)/shard_map/ppermute | solution.py:227
  59.0 0.4 weight.1
  59.4 1.5 %collective-permute-start.9 = (bf16[64,512]{1,0:T(8,128)(2,1)S(1)}, bf16[64,512]{1,0:T(8,128)(2,1)S(1)}, u32[]{:S(2)}, u32[]{:S(2)}) collective-permute-start(bf16[64,512]{1,0:T(8,128)(2,1)S(1)} %get-tuple-element.36), channel_id=1, source_target_pairs={{0,16},{16,32},{32,48},{48,0},{1,17},{17,33},{33,49},{49,1},{2,18}... | collective-permute-start | bytes 196616 | tf_op jit(solution)/shard_map/ppermute | solution.py:227
  60.9 1.7 %all-to-all-done.1.in_ref = bf16[64,8,128]{2,1,0:T(8,128)(2,1)S(1)} async-done(((bf16[64,8,128]{2,1,0:T(8,128)(2,1)}), bf16[64,8,128]{2,1,0:T(8,128)(2,1)S(1)}, u32[]{:S(2)}, u32[]{:S(2)}) %all-to-all-start.1) | async-done | bytes 131104 | tf_op jit(solution)/shard_map/all_to_all | solution.py:290
  62.6 2.6 %collective-permute-start.5 = (bf16[64,8,128]{2,1,0:T(8,128)(2,1)S(1)}, bf16[64,8,128]{2,1,0:T(8,128)(2,1)S(1)}, u32[]{:S(2)}, u32[]{:S(2)}) collective-permute-start(bf16[64,8,128]{2,1,0:T(8,128)(2,1)S(1)} %all-to-all-done.1.in_ref), channel_id=1, source_target_pairs={{0,128},{64,192},{128,0},{192,64},{1,129},{65,193},{129,1},{193,65... | collective-permute-start | bytes 393224 | tf_op jit(solution)/shard_map/ppermute | solution.py:227
  65.1 0.9 %collective-permute-start.4 = (bf16[64,8,128]{2,1,0:T(8,128)(2,1)S(1)}, bf16[64,8,128]{2,1,0:T(8,128)(2,1)S(1)}, u32[]{:S(2)}, u32[]{:S(2)}) collective-permute-start(bf16[64,8,128]{2,1,0:T(8,128)(2,1)S(1)} %all-to-all-done.1.in_ref), channel_id=1, source_target_pairs={{0,192},{64,0},{128,64},{192,128},{1,193},{65,1},{129,65},{193,129... | collective-permute-start | bytes 393224 | tf_op jit(solution)/shard_map/ppermute | solution.py:227
  66.1 0.5 collective-permute-start.3
  66.6 0.7 collective-permute-start.10
  67.3 0.0 collective-permute-done.9.refs_5_
  67.3 1.9 %collective-permute-start.11 = (bf16[64,512]{1,0:T(8,128)(2,1)S(1)}, bf16[64,512]{1,0:T(8,128)(2,1)S(1)}, u32[]{:S(2)}, u32[]{:S(2)}) collective-permute-start(bf16[64,512]{1,0:T(8,128)(2,1)S(1)} %get-tuple-element.38), channel_id=1, source_target_pairs={{0,48},{16,0},{32,16},{48,32},{1,49},{17,1},{33,17},{49,33},{2,50}... | collective-permute-start | bytes 196616 | tf_op jit(solution)/shard_map/ppermute | solution.py:227
  69.2 1.4 %own_field.1 = (bf16[4,512,512]{2,1,0:T(8,128)(2,1)}, bf16[512,128]{1,0:T(8,128)(2,1)S(1)}) custom-call(bf16[64,8,128]{2,1,0:T(8,128)(2,1)S(1)} %all-to-all-done.1.in_ref), custom_call_target="tpu_custom_call" | custom-call | flops 134217728 | bytes 1048576 | tf_op jit(solution)/shard_map/own_field/pallas_call | solution.py:303
  70.7 1.2 %collective-permute-done.10.refs_6_ = bf16[64,512]{1,0:T(8,128)(2,1)S(1)} collective-permute-done((bf16[64,512]{1,0:T(8,128)(2,1)S(1)}, bf16[64,512]{1,0:T(8,128)(2,1)S(1)}, u32[]{:S(2)}, u32[]{:S(2)}) %collective-permute-start.10) | collective-permute-done | bytes 65568 | tf_op jit(solution)/shard_map/ppermute | solution.py:227
  71.8 0.0 collective-permute-done.11.refs_7_
  71.8 0.9 %collective-permute-done.4.refs_1_ = bf16[64,8,128]{2,1,0:T(8,128)(2,1)S(1)} collective-permute-done((bf16[64,8,128]{2,1,0:T(8,128)(2,1)S(1)}, bf16[64,8,128]{2,1,0:T(8,128)(2,1)S(1)}, u32[]{:S(2)}, u32[]{:S(2)}) %collective-permute-start.4) | collective-permute-done | bytes 131104 | tf_op jit(solution)/shard_map/ppermute | solution.py:227
  72.7 1.7 %last.1 = (bf16[4,512,512]{2,1,0:T(8,128)(2,1)}, f32[4,2,32,512]{3,2,1,0:T(8,128)}) custom-call(bf16[64,8,128]{2,1,0:T(8,128)(2,1)S(1)} %collective-permute-done.3.refs_0_, bf16[64,8,128]{2,1,0:T(8,128)(2,1)S(1)} %collective-permute-done.4.refs_1_, bf16[64,8,128]{2,1,0:T(8,128)(2,1)S(1)} %collective-permute-done.5.refs_2_, ...), custom_call_target="tpu_custom_call", output_to_operand_aliasing={{0}: (8, {})} | custom-call | tf_op jit(solution)/shard_map/last/pallas_call | solution.py:317
  (5 shorter events, 0.0 us)
Async XLA Ops:
  2.7 12.2 %collective-permute-start.1 = (bf16[256,512]{1,0:T(8,128)(2,1)S(1)}, bf16[256,512]{1,0:T(8,128)(2,1)S(1)}, u32[]{:S(2)}, u32[]{:S(2)}) collective-permute-start(bf16[256,512]{1,0:T(8,128)(2,1)S(1)} %get-tuple-element.27), channel_id=1, source_target_pairs={{0,128},{64,192},{128,0},{192,64},{1,129},{65,193},{129,1},{193,65... | collective-permute-start | bytes 786440 | tf_op jit(solution)/shard_map/ppermute | solution.py:227
  9.5 8.9 %collective-permute-start = (bf16[256,512]{1,0:T(8,128)(2,1)S(1)}, bf16[256,512]{1,0:T(8,128)(2,1)S(1)}, u32[]{:S(2)}, u32[]{:S(2)}) collective-permute-start(bf16[256,512]{1,0:T(8,128)(2,1)S(1)} %get-tuple-element.26), channel_id=1, source_target_pairs={{0,64},{64,128},{128,192},{192,0},{1,65},{65,129},{129,193},{193,1... | collective-permute-start | bytes 786440 | tf_op jit(solution)/shard_map/ppermute | solution.py:227
  9.9 8.4 %collective-permute-start.2 = (bf16[256,512]{1,0:T(8,128)(2,1)S(1)}, bf16[256,512]{1,0:T(8,128)(2,1)S(1)}, u32[]{:S(2)}, u32[]{:S(2)}) collective-permute-start(bf16[256,512]{1,0:T(8,128)(2,1)S(1)} %get-tuple-element.28), channel_id=1, source_target_pairs={{0,192},{64,0},{128,64},{192,128},{1,193},{65,1},{129,65},{193,129... | collective-permute-start | bytes 786440 | tf_op jit(solution)/shard_map/ppermute | solution.py:227
  19.4 25.8 %all-to-all-start = ((bf16[64,8,256]{2,1,0:T(8,128)(2,1)}), bf16[64,8,256]{2,1,0:T(8,128)(2,1)S(1)}, u32[]{:S(2)}, u32[]{:S(2)}) async-start(bf16[64,8,256]{2,1,0:T(8,128)(2,1)} %sum_y.1), calls=%async_computation | async-start | bytes 524288 | tf_op jit(solution)/shard_map/all_to_all | solution.py:274
  46.6 16.0 %all-to-all-start.1 = ((bf16[64,8,128]{2,1,0:T(8,128)(2,1)}), bf16[64,8,128]{2,1,0:T(8,128)(2,1)S(1)}, u32[]{:S(2)}, u32[]{:S(2)}) async-start(bf16[64,8,128]{2,1,0:T(8,128)(2,1)} %bitcast.1), calls=%async_computation.1 | async-start | bytes 262144 | tf_op jit(solution)/shard_map/all_to_all | solution.py:290
  51.7 4.7 %collective-permute-start.6 = (bf16[40,512]{1,0:T(8,128)(2,1)S(1)}, bf16[40,512]{1,0:T(8,128)(2,1)S(1)}, u32[]{:S(2)}, u32[]{:S(2)}) collective-permute-start(bf16[40,512]{1,0:T(8,128)(2,1)S(1)} %get-tuple-element.32), channel_id=1, source_target_pairs={{0,64},{64,128},{128,192},{192,0},{1,65},{65,129},{129,193},{193,1... | collective-permute-start | bytes 122888 | tf_op jit(solution)/shard_map/ppermute | solution.py:227
  52.9 5.1 %collective-permute-start.7 = (bf16[40,512]{1,0:T(8,128)(2,1)S(1)}, bf16[40,512]{1,0:T(8,128)(2,1)S(1)}, u32[]{:S(2)}, u32[]{:S(2)}) collective-permute-start(bf16[40,512]{1,0:T(8,128)(2,1)S(1)} %get-tuple-element.33), channel_id=1, source_target_pairs={{0,128},{64,192},{128,0},{192,64},{1,129},{65,193},{129,1},{193,65... | collective-permute-start | bytes 122888 | tf_op jit(solution)/shard_map/ppermute | solution.py:227
  55.9 3.1 %collective-permute-start.8 = (bf16[40,512]{1,0:T(8,128)(2,1)S(1)}, bf16[40,512]{1,0:T(8,128)(2,1)S(1)}, u32[]{:S(2)}, u32[]{:S(2)}) collective-permute-start(bf16[40,512]{1,0:T(8,128)(2,1)S(1)} %get-tuple-element.34), channel_id=1, source_target_pairs={{0,192},{64,0},{128,64},{192,128},{1,193},{65,1},{129,65},{193,129... | collective-permute-start | bytes 122888 | tf_op jit(solution)/shard_map/ppermute | solution.py:227
  59.4 7.9 %collective-permute-start.9 = (bf16[64,512]{1,0:T(8,128)(2,1)S(1)}, bf16[64,512]{1,0:T(8,128)(2,1)S(1)}, u32[]{:S(2)}, u32[]{:S(2)}) collective-permute-start(bf16[64,512]{1,0:T(8,128)(2,1)S(1)} %get-tuple-element.36), channel_id=1, source_target_pairs={{0,16},{16,32},{32,48},{48,0},{1,17},{17,33},{33,49},{49,1},{2,18}... | collective-permute-start | bytes 196616 | tf_op jit(solution)/shard_map/ppermute | solution.py:227
  62.6 9.3 %collective-permute-start.5 = (bf16[64,8,128]{2,1,0:T(8,128)(2,1)S(1)}, bf16[64,8,128]{2,1,0:T(8,128)(2,1)S(1)}, u32[]{:S(2)}, u32[]{:S(2)}) collective-permute-start(bf16[64,8,128]{2,1,0:T(8,128)(2,1)S(1)} %all-to-all-done.1.in_ref), channel_id=1, source_target_pairs={{0,128},{64,192},{128,0},{192,64},{1,129},{65,193},{129,1},{193,65... | collective-permute-start | bytes 393224 | tf_op jit(solution)/shard_map/ppermute | solution.py:227
  65.1 7.5 %collective-permute-start.4 = (bf16[64,8,128]{2,1,0:T(8,128)(2,1)S(1)}, bf16[64,8,128]{2,1,0:T(8,128)(2,1)S(1)}, u32[]{:S(2)}, u32[]{:S(2)}) collective-permute-start(bf16[64,8,128]{2,1,0:T(8,128)(2,1)S(1)} %all-to-all-done.1.in_ref), channel_id=1, source_target_pairs={{0,192},{64,0},{128,64},{192,128},{1,193},{65,1},{129,65},{193,129... | collective-permute-start | bytes 393224 | tf_op jit(solution)/shard_map/ppermute | solution.py:227
  66.1 6.6 %collective-permute-start.3 = (bf16[64,8,128]{2,1,0:T(8,128)(2,1)S(1)}, bf16[64,8,128]{2,1,0:T(8,128)(2,1)S(1)}, u32[]{:S(2)}, u32[]{:S(2)}) collective-permute-start(bf16[64,8,128]{2,1,0:T(8,128)(2,1)S(1)} %all-to-all-done.1.in_ref), channel_id=1, source_target_pairs={{0,64},{64,128},{128,192},{192,0},{1,65},{65,129},{129,193},{193,1... | collective-permute-start | bytes 393224 | tf_op jit(solution)/shard_map/ppermute | solution.py:227
  66.6 5.2 %collective-permute-start.10 = (bf16[64,512]{1,0:T(8,128)(2,1)S(1)}, bf16[64,512]{1,0:T(8,128)(2,1)S(1)}, u32[]{:S(2)}, u32[]{:S(2)}) collective-permute-start(bf16[64,512]{1,0:T(8,128)(2,1)S(1)} %get-tuple-element.37), channel_id=1, source_target_pairs={{0,32},{16,48},{32,0},{48,16},{1,33},{17,49},{33,1},{49,17},{2,34}... | collective-permute-start | bytes 196616 | tf_op jit(solution)/shard_map/ppermute | solution.py:227
  67.3 4.5 %collective-permute-start.11 = (bf16[64,512]{1,0:T(8,128)(2,1)S(1)}, bf16[64,512]{1,0:T(8,128)(2,1)S(1)}, u32[]{:S(2)}, u32[]{:S(2)}) collective-permute-start(bf16[64,512]{1,0:T(8,128)(2,1)S(1)} %get-tuple-element.38), channel_id=1, source_target_pairs={{0,48},{16,0},{32,16},{48,32},{1,49},{17,1},{33,17},{49,33},{2,50}... | collective-permute-start | bytes 196616 | tf_op jit(solution)/shard_map/ppermute | solution.py:227
